TPU v7x, 32 devices: a whole 2x2x4 slice. The times are simulated.
32 devices in a mesh: grp: 2 (over x), chan: 16 (over z, y, core).
Axes of the slice: x: 2, y: 2, z: 4, core: 2. Of those that a mesh axis runs over, the one named last changes fastest.
Arguments:
- traces: bfloat16 [32, 16, 256, 512], P(('grp', 'chan')), parts along dimension 0, may hold values from -6 to 6
- mask: int32 [32, 16], P('grp'), parts along dimension 0, may hold values 0 or 1
- counts: int32 [32], P('grp'), parts along dimension 0, may hold values from 0 to 5, as said below
Outputs:
- forward: float32 [32, 5, 128, 512], P(('grp', 'chan')), parts along dimension 0
- backward: float32 [32, 5, 128, 512], P(('grp', 'chan')), parts along dimension 0
There are 2 independent parts, one for each index of `grp`. A program takes and returns all parts, laid end to end along the dimension named above; each array names one. Nothing has to cross between parts.
Inputs may be any that keep to these rules, and one draw needn't show every extreme that they name: counts[b] <= min(5, 15 - b); block 0 always has 5 partners.
All inputs are finite; a program needn't handle non-finite values.
Results may differ from a plain program's by a relative error of at most 0.0063.
Values may be sent and summed in bfloat16 or wider, within the bound.
No kernel may reach another device: no remote copies, remote signals or barrier semaphores. Data moves between devices by JAX's collectives and lax.ppermute only.
A program may use at most 128 MiB of HBM per device.

v0:
```python
import math

import jax
import jax.numpy as jnp
from jax import lax
from jax.sharding import PartitionSpec as P

MAXP = 5


def from_behind(shard, axis, by):
    peers = lax.axis_size(axis)
    pairs = [(i, i + by) for i in range(peers) if 0 <= i + by < peers]
    return lax.ppermute(shard, axis, pairs)


def lag_table(lags, bins):
    times = jnp.arange(lags, dtype=jnp.int32)[:, None]
    freqs = jnp.arange(1, bins + 1, dtype=jnp.int32)[None, :]
    phase = (times * freqs % lags).astype(jnp.float32) * (2.0 * math.pi / lags)
    return jnp.concatenate([jnp.cos(phase), -jnp.sin(phase)], axis=1).astype(jnp.bfloat16)


def whiten(record, table):
    bins = table.shape[1] // 2
    raw = jnp.einsum("tk,wtc->wkc", table, record, preferred_element_type=jnp.float32)
    power = jnp.sum(raw * raw, axis=1) / bins
    return (raw / jnp.sqrt(power + 1e-06)[:, None, :]).astype(jnp.bfloat16)


def stack_pair(first, second, weight):
    half = first.shape[1] // 2
    wlen = first.shape[0]
    first_re = first[:, :half].astype(jnp.float32)
    first_im = first[:, half:].astype(jnp.float32)
    second_re = second[:, :half].astype(jnp.float32)
    second_im = second[:, half:].astype(jnp.float32)
    scaled = weight[:, None, None]
    real_part = jnp.sum(scaled * (first_re * second_re + first_im * second_im), axis=0)
    imag_part = jnp.sum(scaled * (first_im * second_re - first_re * second_im), axis=0)
    return (jnp.concatenate([real_part, imag_part], axis=0) / math.sqrt(wlen)).astype(jnp.bfloat16)


def pair_lags(first, second, weight, table, bins):
    stacked = stack_pair(first, second, weight)
    return jnp.dot(table, stacked, preferred_element_type=jnp.float32) / math.sqrt(bins)


def pick_row(values, index):
    return lax.dynamic_index_in_dim(values, index, 0, keepdims=False)


def local(traces, mask, counts):
    myself = lax.axis_index("chan")
    blocks = mask.shape[0]
    record = traces[0]
    lags = record.shape[1]
    width = record.shape[2]
    bins = lags // 2
    table = lag_table(lags, bins)
    white = whiten(record, table)
    valid = mask.astype(jnp.float32)
    own_valid = pick_row(valid, myself)
    own_count = pick_row(counts, myself)
    zero_lags = jnp.zeros((lags, width), jnp.float32)
    forward_list = []
    backward_list = []
    for step in range(1, MAXP + 1):
        partner = from_behind(white, "chan", -step)
        other = jnp.minimum(myself + step, blocks - 1)
        weight = own_valid * pick_row(valid, other)
        corr = lax.cond(
            own_count >= step,
            lambda: pair_lags(white, partner, weight, table, bins),
            lambda: zero_lags,
        )
        forward_list.append(corr[:bins])
        returned = from_behind(corr[bins:][::-1], "chan", step)
        backward_list.append(returned)
    forward = jnp.stack(forward_list)[None]
    backward = jnp.stack(backward_list)[None]
    return (forward, backward)


def solution(mesh):
    return jax.shard_map(
        local,
        mesh=mesh,
        in_specs=(P(("grp", "chan"), None, None, None), P("grp", None), P("grp")),
        out_specs=(P(("grp", "chan"), None, None, None), P(("grp", "chan"), None, None, None)),
        check_vma=False,
    )
```

profile of v0, /device:TPU:16, one launch (start us, length us, event | category | flops | bytes accessed | tf_op | source)
XLA Modules:
  0.0 477.8 jit_solution(1164922830686994316)
XLA Ops:
  0.6 0.6 cosine_convert_fusion
  1.3 3.5 multiply_reduce_fusion
  4.7 0.0 copy-start.1
  4.8 0.0 copy-start.2
  4.8 3.3 fusion.62
  8.0 3.3 collective-permute-start.1
  11.4 1.9 collective-permute-start
  13.3 2.5 collective-permute-start.2
  15.8 1.9 collective-permute-start.3
  17.7 1.9 collective-permute-start.4
  19.7 0.6 dynamic_slice.48
  23.5 80.2 %collective-permute-done.1 = bf16[16,256,512]{2,1,0:T(8,128)(2,1)} collective-permute-done((bf16[16,256,512]{2,1,0:T(8,128)(2,1)}, bf16[16,256,512]{2,1,0:T(8,128)(2,1)}, u32[]{:S(2)}, u32[]{:S(2)}) %collective-permute-start.1) | collective-permute-done | bytes 4194336 | tf_op jit(solution)/shard_map/ppermute | solution.py:14
  103.7 4.7 conditional.6
  103.7 4.5 fusion.14
  108.2 0.3 fusion.18
  108.5 0.1 copy.31
  108.6 0.1 rev.16
  108.8 1.9 collective-permute-start.6
  110.7 81.8 %collective-permute-done = bf16[16,256,512]{2,1,0:T(8,128)(2,1)} collective-permute-done((bf16[16,256,512]{2,1,0:T(8,128)(2,1)}, bf16[16,256,512]{2,1,0:T(8,128)(2,1)}, u32[]{:S(2)}, u32[]{:S(2)}) %collective-permute-start) | collective-permute-done | bytes 4194336 | tf_op jit(solution)/shard_map/ppermute | solution.py:14
  192.6 4.8 conditional.5
  192.6 4.5 fusion.2
  197.0 0.3 fusion.6
  197.4 0.1 copy.30
  197.5 0.1 rev.15
  197.6 10.5 %collective-permute-start.5 = (f32[128,512]{1,0:T(8,128)S(1)}, f32[128,512]{1,0:T(8,128)S(1)}, u32[]{:S(2)}, u32[]{:S(2)}) collective-permute-start(f32[128,512]{1,0:T(8,128)S(1)} %rev.15), channel_id=1, source_target_pairs={{0,1},{1,2},{2,3},{3,4},{4,5},{5,6},{6,7},{7,8},{8,9},{9,10},{10,1... | collective-permute-start | bytes 786440 | tf_op jit(solution)/shard_map/ppermute | solution.py:14
  208.2 74.3 %collective-permute-done.2 = bf16[16,256,512]{2,1,0:T(8,128)(2,1)} collective-permute-done((bf16[16,256,512]{2,1,0:T(8,128)(2,1)}, bf16[16,256,512]{2,1,0:T(8,128)(2,1)}, u32[]{:S(2)}, u32[]{:S(2)}) %collective-permute-start.2) | collective-permute-done | bytes 4194336 | tf_op jit(solution)/shard_map/ppermute | solution.py:14
  282.4 4.7 conditional.7
  282.4 4.4 fusion.26
  286.9 0.3 fusion.30
  287.2 0.1 copy.32
  287.4 0.1 rev.17
  287.5 1.9 collective-permute-start.7
  289.4 83.8 %collective-permute-done.3 = bf16[16,256,512]{2,1,0:T(8,128)(2,1)} collective-permute-done((bf16[16,256,512]{2,1,0:T(8,128)(2,1)}, bf16[16,256,512]{2,1,0:T(8,128)(2,1)}, u32[]{:S(2)}, u32[]{:S(2)}) %collective-permute-start.3) | collective-permute-done | bytes 4194336 | tf_op jit(solution)/shard_map/ppermute | solution.py:14
  373.2 4.7 conditional.8
  373.2 4.5 fusion.38
  377.7 0.3 fusion.42
  378.0 0.1 copy.33
  378.1 1.3 rev.18
  379.5 1.9 collective-permute-start.8
  381.4 79.7 %collective-permute-done.4 = bf16[16,256,512]{2,1,0:T(8,128)(2,1)} collective-permute-done((bf16[16,256,512]{2,1,0:T(8,128)(2,1)}, bf16[16,256,512]{2,1,0:T(8,128)(2,1)}, u32[]{:S(2)}, u32[]{:S(2)}) %collective-permute-start.4) | collective-permute-done | bytes 4194336 | tf_op jit(solution)/shard_map/ppermute | solution.py:14
  461.1 4.8 conditional.9
  461.1 4.5 fusion.50
  465.5 0.3 fusion.54
  465.9 0.1 copy.34
  466.0 0.1 rev.19
  466.1 1.9 collective-permute-start.9
  468.1 0.1 copy.26
  468.2 0.1 copy.25
  468.3 0.7 bitcast_dynamic-update-slice_fusion.9
  469.1 0.1 copy.27
  469.2 0.1 copy.28
  469.3 0.7 bitcast_dynamic-update-slice_fusion.8
  470.1 0.7 bitcast_dynamic-update-slice_fusion.7
  470.8 0.7 bitcast_dynamic-update-slice_fusion.6
  471.5 0.1 copy.29
  471.6 0.7 bitcast_dynamic-update-slice_fusion.5
  472.4 0.0 collective-permute-done.5
  472.4 0.0 collective-permute-done.6
  472.4 1.0 bitcast_dynamic-update-slice_fusion.2
  473.4 1.0 bitcast_dynamic-update-slice_fusion.1
  474.4 1.3 collective-permute-done.9
  475.7 1.0 bitcast_dynamic-update-slice_fusion
  476.7 0.0 copy-start
  476.7 1.0 copy-done
  (21 shorter events, 0.3 us)
Async XLA Ops:
  4.7 14.9 %copy-start.1 = (s32[16,16]{1,0:T(8,128)S(1)}, s32[16,16]{1,0:T(8,128)}, u32[]{:S(2)}) copy-start(s32[16,16]{1,0:T(8,128)} %param.14) | copy-start | bytes 3076
  4.8 14.9 %copy-start.2 = (s32[16]{0:T(128)S(1)}, s32[16]{0:T(128)}, u32[]{:S(2)}) copy-start(s32[16]{0:T(128)} %param.15) | copy-start | bytes 196
  8.0 95.7 %collective-permute-start.1 = (bf16[16,256,512]{2,1,0:T(8,128)(2,1)}, bf16[16,256,512]{2,1,0:T(8,128)(2,1)}, u32[]{:S(2)}, u32[]{:S(2)}) collective-permute-start(bf16[16,256,512]{2,1,0:T(8,128)(2,1)} %fusion.62), channel_id=1, source_target_pairs={{2,0},{3,1},{4,2},{5,3},{6,4},{7,5},{8,6},{9,7},{10,8},{11,9},{12,... | collective-permute-start | bytes 12582920 | tf_op jit(solution)/shard_map/ppermute | solution.py:14
  11.4 181.2 %collective-permute-start = (bf16[16,256,512]{2,1,0:T(8,128)(2,1)}, bf16[16,256,512]{2,1,0:T(8,128)(2,1)}, u32[]{:S(2)}, u32[]{:S(2)}) collective-permute-start(bf16[16,256,512]{2,1,0:T(8,128)(2,1)} %fusion.62), channel_id=1, source_target_pairs={{1,0},{2,1},{3,2},{4,3},{5,4},{6,5},{7,6},{8,7},{9,8},{10,9},{11,1... | collective-permute-start | bytes 12582920 | tf_op jit(solution)/shard_map/ppermute | solution.py:14
  13.3 269.2 %collective-permute-start.2 = (bf16[16,256,512]{2,1,0:T(8,128)(2,1)}, bf16[16,256,512]{2,1,0:T(8,128)(2,1)}, u32[]{:S(2)}, u32[]{:S(2)}) collective-permute-start(bf16[16,256,512]{2,1,0:T(8,128)(2,1)} %fusion.62), channel_id=1, source_target_pairs={{3,0},{4,1},{5,2},{6,3},{7,4},{8,5},{9,6},{10,7},{11,8},{12,9},{13... | collective-permute-start | bytes 12582920 | tf_op jit(solution)/shard_map/ppermute | solution.py:14
  15.8 357.4 %collective-permute-start.3 = (bf16[16,256,512]{2,1,0:T(8,128)(2,1)}, bf16[16,256,512]{2,1,0:T(8,128)(2,1)}, u32[]{:S(2)}, u32[]{:S(2)}) collective-permute-start(bf16[16,256,512]{2,1,0:T(8,128)(2,1)} %fusion.62), channel_id=1, source_target_pairs={{4,0},{5,1},{6,2},{7,3},{8,4},{9,5},{10,6},{11,7},{12,8},{13,9},{1... | collective-permute-start | bytes 12582920 | tf_op jit(solution)/shard_map/ppermute | solution.py:14
  17.7 443.4 %collective-permute-start.4 = (bf16[16,256,512]{2,1,0:T(8,128)(2,1)}, bf16[16,256,512]{2,1,0:T(8,128)(2,1)}, u32[]{:S(2)}, u32[]{:S(2)}) collective-permute-start(bf16[16,256,512]{2,1,0:T(8,128)(2,1)} %fusion.62), channel_id=1, source_target_pairs={{5,0},{6,1},{7,2},{8,3},{9,4},{10,5},{11,6},{12,7},{13,8},{14,9},{... | collective-permute-start | bytes 12582920 | tf_op jit(solution)/shard_map/ppermute | solution.py:14
  108.8 363.6 %collective-permute-start.6 = (f32[128,512]{1,0:T(8,128)S(1)}, f32[128,512]{1,0:T(8,128)S(1)}, u32[]{:S(2)}, u32[]{:S(2)}) collective-permute-start(f32[128,512]{1,0:T(8,128)S(1)} %rev.16), channel_id=1, source_target_pairs={{0,2},{1,3},{2,4},{3,5},{4,6},{5,7},{6,8},{7,9},{8,10},{9,11},{10,... | collective-permute-start | bytes 786440 | tf_op jit(solution)/shard_map/ppermute | solution.py:14
  197.6 274.7 %collective-permute-start.5 = (f32[128,512]{1,0:T(8,128)S(1)}, f32[128,512]{1,0:T(8,128)S(1)}, u32[]{:S(2)}, u32[]{:S(2)}) collective-permute-start(f32[128,512]{1,0:T(8,128)S(1)} %rev.15), channel_id=1, source_target_pairs={{0,1},{1,2},{2,3},{3,4},{4,5},{5,6},{6,7},{7,8},{8,9},{9,10},{10,1... | collective-permute-start | bytes 786440 | tf_op jit(solution)/shard_map/ppermute | solution.py:14
  287.5 184.9 %collective-permute-start.7 = (f32[128,512]{1,0:T(8,128)S(1)}, f32[128,512]{1,0:T(8,128)}, u32[]{:S(2)}, u32[]{:S(2)}) collective-permute-start(f32[128,512]{1,0:T(8,128)S(1)} %rev.17), channel_id=1, source_target_pairs={{0,3},{1,4},{2,5},{3,6},{4,7},{5,8},{6,9},{7,10},{8,11},{9,12},{10... | collective-permute-start | bytes 786440 | tf_op jit(solution)/shard_map/ppermute | solution.py:14
  379.5 93.9 %collective-permute-start.8 = (f32[128,512]{1,0:T(8,128)}, f32[128,512]{1,0:T(8,128)}, u32[]{:S(2)}, u32[]{:S(2)}) collective-permute-start(f32[128,512]{1,0:T(8,128)} %rev.18), channel_id=1, source_target_pairs={{0,4},{1,5},{2,6},{3,7},{4,8},{5,9},{6,10},{7,11},{8,12},{9,13},{1... | collective-permute-start | bytes 786440 | tf_op jit(solution)/shard_map/ppermute | solution.py:14
  466.1 9.6 %collective-permute-start.9 = (f32[128,512]{1,0:T(8,128)S(1)}, f32[128,512]{1,0:T(8,128)}, u32[]{:S(2)}, u32[]{:S(2)}) collective-permute-start(f32[128,512]{1,0:T(8,128)S(1)} %rev.19), channel_id=1, source_target_pairs={{0,5},{1,6},{2,7},{3,8},{4,9},{5,10},{6,11},{7,12},{8,13},{9,14},{... | collective-permute-start | bytes 786440 | tf_op jit(solution)/shard_map/ppermute | solution.py:14
  476.7 1.1 copy-start
where the time goes:
time: 478 us
  waiting for transfers between devices  401 us (84%)
  starting transfers between devices  29.7 us (6%)
  other arithmetic  26.2 us (5%)
  local copies, waits for them, and re-layouts  11.6 us (2%)
  matrix products  4.85 us (1%)
    ppermute x10, waiting for transfers between devices, from_behind(): return lax.ppermute(shard, axis, pairs)  401 us
    ppermute x10, starting transfers between devices, from_behind(): return lax.ppermute(shard, axis, pairs)  29.7 us
    reduce_sum x5, other arithmetic, stack_pair(): jnp.sum(scaled * (first_re * second_re + first_im * second_im), axis=0)  22.3 us
  transfers between devices with their start and end apart: 10, of which 6 were waited for; matrix products, arithmetic and copies ran while one was open for 7% of the time, Pallas kernels for 0%

commit v1 on v0

v1 whole, which is shorter than its diff:
```python
import functools
import math

import jax
import jax.numpy as jnp
import numpy as np
from jax import lax
from jax.experimental import pallas as pl
from jax.experimental.pallas import tpu as pltpu
from jax.sharding import PartitionSpec as P

MAXP = 5
PLANE = 4
HALVES = 7
VMEM = 56 * 1024 * 1024

FIRST = -3
SPOTS = 9
GROUPS = (
    ((0, 4), (0, 5), (1, 4), (1, 5), (2, 5)),
    ((0, 1), (0, 2), (0, 3), (1, 2), (1, 3), (2, 3)),
    ((-1, 0), (-1, 1), (-1, 2), (-1, 3), (-1, 4)),
    ((-2, 0), (-2, 2), (-2, 3), (-3, 2)),
)
PAIRS = tuple(pair for group in GROUPS for pair in group)


def kept(spot):
    ahead = sorted(("ahead", b - a - 1) for a, b in PAIRS if a == spot)
    back = sorted(("back", b - a - 1) for a, b in PAIRS if b == spot)
    return ahead + back


def lag_tables(lags):
    bins = lags // 2
    phase = (np.arange(lags)[:, None] * np.arange(1, bins + 1)[None, :] % lags) * (2.0 * math.pi / lags)
    real, imag = np.cos(phase), -np.sin(phase)
    causal = np.concatenate([real, imag], axis=1)
    other = np.concatenate([real, -imag], axis=1)
    near = np.concatenate([causal[:bins], causal[bins:][::-1]], axis=0)
    far = np.concatenate([other[bins:][::-1], other[:bins]], axis=0)
    return causal.astype(jnp.bfloat16), np.stack([near, far]).astype(jnp.bfloat16)


def whiten_body(where_ref, mask_ref, table_ref, traces_ref, out_ref, *, first):
    bins = table_ref.shape[0] // 2
    step = traces_ref.shape[0]
    for w in range(step):
        raw = jnp.dot(table_ref[...], traces_ref[w], preferred_element_type=jnp.float32)
        power = jnp.sum(raw * raw, axis=0, keepdims=True) / bins
        valid = mask_ref[first + pl.program_id(0) * step + w].astype(jnp.float32)
        out_ref[w] = (raw * (valid * lax.rsqrt(power + 1e-06))).astype(jnp.bfloat16)


def whiten(record, table, mask, quarter, first, count):
    windows, lags, width = record.shape
    part = width // PLANE
    step = 4
    return pl.pallas_call(
        functools.partial(whiten_body, first=first),
        grid_spec=pltpu.PrefetchScalarGridSpec(
            num_scalar_prefetch=2,
            grid=(count // step,),
            in_specs=[
                pl.BlockSpec((lags, lags), lambda i, where, mask: (0, 0)),
                pl.BlockSpec((step, lags, part), lambda i, where, mask: (first // step + i, 0, where[0])),
            ],
            out_specs=pl.BlockSpec((step, lags, part), lambda i, where, mask: (i, 0, 0)),
        ),
        out_shape=jax.ShapeDtypeStruct((count, lags, part), jnp.bfloat16),
        cost_estimate=pl.CostEstimate(flops=2 * count * lags * lags * part, bytes_accessed=4 * count * lags * part, transcendentals=0),
    )(quarter[None], mask, table, record)


def correlate_body(place_ref, counts_ref, table_ref, own, sib, o0a, o0b, o1a, o1b, x0, x1, v0a, v0b, v1a, v1b, ea, eb,
                   g0, g1, g2, g3, s0, s1, d0, d1, extra, spots, stack, gs, xs, vs, es, sems):
    windows = own.shape[0]
    half = windows // 2
    bins = own.shape[1] // 2
    part = own.shape[2]
    far, m, base = place_ref[0], place_ref[1], place_ref[2]
    blocks = counts_ref.shape[0]
    lo, hi = pl.ds(0, half), pl.ds(half, half)
    every = pl.ds(0, windows)
    moves = (
        (own, 3 + m, every), (sib, 4 - m, every), (x0, 7 + m, every), (x1, 8 - m, every),
        (o0a, 5 + m, lo), (o0b, 5 + m, hi), (o1a, 6 - m, lo), (o1b, 6 - m, hi),
        (v0a, 1 + m, lo), (v0b, 1 + m, hi), (v1a, 2 - m, lo), (v1b, 2 - m, hi),
    )
    copies = [pltpu.make_async_copy(ref, spots.at[slot, span], sems.at[i]) for i, (ref, slot, span) in enumerate(moves)]
    for copy in copies:
        copy.start()
    far_copies = [pltpu.make_async_copy(ref, spots.at[0], sems.at[len(moves)]) for ref in (ea, eb)]

    @pl.when(m == 1)
    def _():
        far_copies[0].start()

    @pl.when(m == 0)
    def _():
        far_copies[1].start()

    for copy in copies:
        copy.wait()
    far_copies[0].wait()

    rows = 16
    at = 0
    for group in GROUPS:
        need = sorted({spot for pair in group for spot in pair})

        def tile(kt, carry, group=group, need=need, at=at):
            re_rows = pl.ds(pl.multiple_of(kt * rows, rows), rows)
            im_rows = pl.ds(pl.multiple_of(bins + kt * rows, rows), rows)

            def window(w, sums):
                real = {s: spots[s - FIRST, w, re_rows, :].astype(jnp.float32) for s in need}
                imag = {s: spots[s - FIRST, w, im_rows, :].astype(jnp.float32) for s in need}
                out = []
                for n, (a, b) in enumerate(group):
                    out.append(sums[2 * n] + (real[a] * real[b] + imag[a] * imag[b]))
                    out.append(sums[2 * n + 1] + (imag[a] * real[b] - real[a] * imag[b]))
                return tuple(out)

            zero = jnp.zeros((rows, part), jnp.float32)
            sums = lax.fori_loop(0, windows, window, (zero,) * (2 * len(group)), unroll=2)
            scale = 1.0 / math.sqrt(windows)
            for n in range(len(group)):
                lanes = pl.ds((at + n) * part, part)
                stack[re_rows, lanes] = (sums[2 * n] * scale).astype(jnp.bfloat16)
                stack[im_rows, lanes] = (sums[2 * n + 1] * scale).astype(jnp.bfloat16)
            return carry

        lax.fori_loop(0, bins // rows, tile, 0)
        at += len(group)

    norm = 1.0 / math.sqrt(bins)
    for n, (a, b) in enumerate(PAIRS):
        corr = jnp.dot(table_ref[far], stack[:, n * part:(n + 1) * part], preferred_element_type=jnp.float32)
        first = jnp.where(far == 0, base + a, base + 3 - b)
        count = counts_ref[jnp.clip(first, 0, blocks - 1)]
        corr = corr * jnp.where(count >= b - a, norm, 0.0)
        ahead, back = corr[:bins].astype(jnp.bfloat16), corr[bins:].astype(jnp.bfloat16)
        if a >= 0:
            gs[a, kept(a).index(("ahead", b - a - 1))] = ahead
        elif a == -3:
            es[0] = ahead
        else:
            vs[a + 2, [d for c, d in PAIRS if c == a].index(b)] = ahead
        if b < PLANE:
            gs[b, kept(b).index(("back", b - a - 1))] = back
        else:
            xs[b - PLANE, b - a - 3] = back

    outs = ((gs.at[m], g0), (gs.at[1 - m], g1), (gs.at[2 + m], g2), (gs.at[3 - m], g3),
            (xs.at[m], s0), (xs.at[1 - m], s1), (vs.at[m], d0), (vs.at[1 - m], d1), (es, extra))
    copies = [pltpu.make_async_copy(src, dst, sems.at[i]) for i, (src, dst) in enumerate(outs)]
    for copy in copies:
        copy.start()
    for copy in copies:
        copy.wait()


def correlate(place, counts, tables, whites):
    windows, lags, part = whites[0].shape
    bins = lags // 2
    anywhere = pl.BlockSpec(memory_space=pl.ANY)
    scalars = pl.BlockSpec(memory_space=pltpu.SMEM)
    sizes = [HALVES] * 4 + [3, 3, 5, 5, 1]
    return pl.pallas_call(
        correlate_body,
        in_specs=[scalars, scalars, pl.BlockSpec(memory_space=pltpu.VMEM)] + [anywhere] * len(whites),
        out_specs=[anywhere] * len(sizes),
        out_shape=[jax.ShapeDtypeStruct((n, bins, part), jnp.bfloat16) for n in sizes],
        scratch_shapes=[
            pltpu.VMEM((SPOTS, windows, lags, part), jnp.bfloat16),
            pltpu.VMEM((lags, len(PAIRS) * part), jnp.bfloat16),
            pltpu.VMEM((PLANE, HALVES, bins, part), jnp.bfloat16),
            pltpu.VMEM((2, 3, bins, part), jnp.bfloat16),
            pltpu.VMEM((2, 5, bins, part), jnp.bfloat16),
            pltpu.VMEM((1, bins, part), jnp.bfloat16),
            pltpu.SemaphoreType.DMA((13,)),
        ],
        compiler_params=pltpu.CompilerParams(vmem_limit_bytes=VMEM),
        cost_estimate=pl.CostEstimate(flops=16 * 20 * windows * bins * part, bytes_accessed=2 * 9 * windows * lags * part, transcendentals=0),
    )(place, counts, tables, *whites)


def assemble_body(place_ref, g0, g1, g2, g3, s0, s1, d0, d1, w0, w1, forward, backward, out, sems):
    far, m, q = place_ref[0], place_ref[1], place_ref[3]
    part = g0.shape[2]

    def put(side, j, quarter, value):
        lanes = pl.ds(pl.multiple_of(quarter * part, part), part)
        out[side, j, :, lanes] = value.astype(jnp.float32)

    def fill(spot, k, near, distant, last):
        quarter = q ^ k
        ahead = far if k < 2 else 1 - far
        have = kept(spot)
        for n, (kind, j) in enumerate(have):
            put(ahead if kind == "ahead" else 1 - ahead, j, quarter, near[n])
        if spot < 2:
            for n in range(3):
                put(1 - ahead, 2 + n, quarter, distant[n])
            if spot == 1:
                put(ahead, 4, quarter, last[0])
        else:
            missing = [j for j in range(MAXP) if ("ahead", j) not in have]
            for n, j in enumerate(missing):
                put(ahead, j, quarter, distant[n])

    for mine in range(2):
        @pl.when(m == mine)
        def _(mine=mine):
            fill(mine, 0, g0, s0, w0)
            fill(mine, 1, g1, s1, w1)
            fill(3 - mine, 2, g2, d0, None)
            fill(3 - mine, 3, g3, d1, None)

    copies = [pltpu.make_async_copy(out.at[side], ref.at[0], sems.at[side]) for side, ref in enumerate((forward, backward))]
    for copy in copies:
        copy.start()
    for copy in copies:
        copy.wait()


def assemble(place, parts, shape):
    scalars = pl.BlockSpec(memory_space=pltpu.SMEM)
    return pl.pallas_call(
        assemble_body,
        in_specs=[scalars] + [pl.BlockSpec(memory_space=pltpu.VMEM)] * len(parts),
        out_specs=[pl.BlockSpec(memory_space=pl.ANY)] * 2,
        out_shape=[jax.ShapeDtypeStruct((1,) + shape, jnp.float32)] * 2,
        scratch_shapes=[pltpu.VMEM((2,) + shape, jnp.float32), pltpu.SemaphoreType.DMA((2,))],
        compiler_params=pltpu.CompilerParams(vmem_limit_bytes=VMEM),
    )(place, *parts)


def local(traces, mask, counts):
    peers = lax.axis_size("chan")
    record = traces[0]
    windows, lags, width = record.shape
    me = lax.axis_index("chan").astype(jnp.int32)
    q = me % PLANE
    far = q // 2
    m = (q % 2) ^ far
    place = jnp.stack([far, m, me - q, q])
    own_mask = lax.dynamic_index_in_dim(mask, me, 0, keepdims=False)
    causal, tables = lag_tables(lags)
    rows = jnp.asarray(np.ascontiguousarray(causal.T))

    def send(value, flip, step):
        pairs = []
        for i in range(peers):
            mine = i % PLANE
            if step is None:
                pairs.append((i, i ^ flip))
            elif mine in step and 0 <= i + PLANE * step[mine] < peers:
                pairs.append((i, (i ^ flip) + PLANE * step[mine]))
        return lax.ppermute(value, "chan", pairs)

    out = {0: -1, 1: -1, 2: 1, 3: 1}
    relay = {0: 1, 1: 1, 2: -1, 3: -1}
    inner = {1: 1, 2: -1}

    half = windows // 2
    part = functools.partial(whiten, record, rows, own_mask)
    t2a, t3a = part(q ^ 2, 0, half), part(q ^ 3, 0, half)
    t0, t1 = part(q, 0, windows), part(q ^ 1, 0, windows)
    t2b, t3b = part(q ^ 2, half, half), part(q ^ 3, half, half)
    y2a, y3a = send(t2a, 2, None), send(t3a, 3, None)
    z0, z1 = send(t0, 0, out), send(t1, 1, out)
    ea, eb = send(t0, 0, inner), send(t1, 1, inner)
    d2b, d3b = send(t2b, 2, out), send(t3b, 3, out)
    u1 = send(t1, 1, None)
    y2a, y3a, t2b, t3b = lax.optimization_barrier((y2a, y3a, t2b, t3b))
    s2a, s3a = send(y2a, 0, relay), send(y3a, 0, relay)
    y2b, y3b = send(t2b, 2, None), send(t3b, 3, None)

    g0, g1, g2, g3, s0, s1, d0, d1, extra = correlate(
        place, counts, jnp.asarray(tables), (t0, u1, y2a, y2b, y3a, y3b, z0, z1, s2a, d2b, s3a, d3b, ea, eb))

    to_x = {0: 1, 1: 1, 2: -1, 3: -1}
    to_v = {0: -1, 1: -1, 2: 1, 3: 1}
    parts = (
        g0, send(g1, 1, None), send(g2, 2, None), send(g3, 3, None),
        send(s0, 0, to_x), send(s1, 1, to_x), send(d0, 2, to_v), send(d1, 3, to_v),
        send(extra, 0, {1: -1, 2: 1}), send(extra, 1, {0: -1, 3: 1}),
    )
    return tuple(assemble(place, parts, (MAXP, lags // 2, width)))


def solution(mesh):
    return jax.shard_map(
        local,
        mesh=mesh,
        in_specs=(P(("grp", "chan"), None, None, None), P("grp", None), P("grp")),
        out_specs=(P(("grp", "chan"), None, None, None), P(("grp", "chan"), None, None, None)),
        check_vma=False,
    )
```

time: 478 us -> 173 us (0.36)
  waiting for transfers between devices: 401 us -> 78.8 us
  Pallas kernels: 0 us -> 41.3 us
  other arithmetic: 26.2 us -> 0.65 us
  starting transfers between devices: 29.7 us -> 46.4 us
  local copies, waits for them, and re-layouts: 11.6 us -> 1.89 us
  matrix products: 4.85 us -> 0 us
    ppermute x10 -> x22, waiting for transfers between devices: 401 us -> 78.8 us  [send(): return lax.ppermute(value, 'chan', pairs)]
    pallas_call x0 -> x8, Pallas kernels: none -> 41.3 us  [the longest x6 21.7 us: whiten(): pl.pallas_call(functools.partial(whiten_body, first=first), grid_spec=plt...]
    reduce_sum x5 -> x0, other arithmetic: 22.3 us -> none  [stack_pair(): jnp.sum(scaled * (first_re * second_re + first_im * second_im), axis=0)]
    ppermute x10 -> x22, starting transfers between devices: 29.7 us -> 46.4 us  [send(): return lax.ppermute(value, 'chan', pairs)]
    unnamed x24 -> x30, local copies, waits for them, and re-layouts: 7.21 us -> 1.37 us
    dot_general x6 -> x0, matrix products: 4.85 us -> none  [the longest x1 3.46 us: whiten(): jnp.einsum('tk,wtc->wkc', table, record, preferred_element_type=jnp.float32)]
  transfers between devices with their start and end apart: 10 -> 22, of which waited for: 6 -> 10; matrix products, arithmetic and copies ran while one was open for 7% -> 0% of each run, Pallas kernels for 0% -> 11%
where the time goes in v1:
time: 173 us; the launch traced here: 170 us
  waiting for transfers between devices  78.8 us (46%)
  starting transfers between devices  46.4 us (27%)
  Pallas kernels  41.3 us (24%)
  local copies, waits for them, and re-layouts  1.89 us (1%)
    ppermute x22, waiting for transfers between devices, send(): return lax.ppermute(value, 'chan', pairs)  78.8 us
    ppermute x22, starting transfers between devices, send(): return lax.ppermute(value, 'chan', pairs)  46.4 us
    pallas_call x6, Pallas kernels, whiten(): pl.pallas_call(functools.partial(whiten_body, first=first), grid_spec=plt...  21.7 us
    pallas_call x1, Pallas kernels, correlate(): pl.pallas_call(correlate_body, in_specs=[scalars, scalars, pl.BlockSpec(m...  16.3 us
  transfers between devices with their start and end apart: 22, of which 10 were waited for; matrix products, arithmetic and copies ran while one was open for 0% of the time, Pallas kernels for 11%

profile of v1, /device:TPU:16, one launch (start us, length us, event | category | flops | bytes accessed | tf_op | source)
XLA Modules:
  0.0 169.9 jit_solution(13919467500882622300)
XLA Ops:
  0.6 0.0 copy-start
  0.7 0.7 copy-done
  1.3 0.5 dynamic-slice_bitcast_fusion.mask_ref
  1.9 3.0 %shard_map.70 = bf16[8,256,128]{2,1,0:T(8,128)(2,1)} custom-call(s32[1]{0:T(128)} %bitcast.7.where_ref, s32[16]{0:T(128)} %dynamic-slice_bitcast_fusion.mask_ref, bf16[256,256]{1,0:T(8,128)(2,1)} %constant.49.clone.table_ref, bf16[16,256,512]{2,1,0:T(8,128)(2,1)} %bitcast.10), custom_call_target="tpu_custom_call" | custom-call | flops 134217728 | bytes 1048576 | tf_op jit(solution)/shard_map/pallas_call | solution.py:59
  4.9 1.5 collective-permute-start.1
  6.4 3.0 %shard_map.71 = bf16[8,256,128]{2,1,0:T(8,128)(2,1)} custom-call(s32[1]{0:T(128)} %bitcast.8.where_ref, s32[16]{0:T(128)} %dynamic-slice_bitcast_fusion.mask_ref, bf16[256,256]{1,0:T(8,128)(2,1)} %constant.49.clone.table_ref, bf16[16,256,512]{2,1,0:T(8,128)(2,1)} %bitcast.11), custom_call_target="tpu_custom_call" | custom-call | flops 134217728 | bytes 1048576 | tf_op jit(solution)/shard_map/pallas_call | solution.py:59
  9.5 0.0 collective-permute-start.2
  9.5 3.0 %shard_map.72 = bf16[8,256,128]{2,1,0:T(8,128)(2,1)} custom-call(s32[1]{0:T(128)} %bitcast.7.where_ref, s32[16]{0:T(128)} %dynamic-slice_bitcast_fusion.mask_ref, bf16[256,256]{1,0:T(8,128)(2,1)} %constant.49.clone.table_ref, bf16[16,256,512]{2,1,0:T(8,128)(2,1)} %bitcast.12), custom_call_target="tpu_custom_call" | custom-call | flops 134217728 | bytes 1048576 | tf_op jit(solution)/shard_map/pallas_call | solution.py:59
  12.5 3.1 %collective-permute-start.8 = (bf16[8,256,128]{2,1,0:T(8,128)(2,1)}, bf16[8,256,128]{2,1,0:T(8,128)(2,1)S(1)}, u32[]{:S(2)}, u32[]{:S(2)}) collective-permute-start(bf16[8,256,128]{2,1,0:T(8,128)(2,1)} %shard_map.72), channel_id=1, source_target_pairs={{2,4},{3,5},{4,2},{5,3},{6,8},{7,9},{8,6},{9,7},{10,12},{11,13},{1... | collective-permute-start | bytes 1572872 | tf_op jit(solution)/shard_map/ppermute | solution.py:261
  15.6 3.0 %shard_map.73 = bf16[8,256,128]{2,1,0:T(8,128)(2,1)} custom-call(s32[1]{0:T(128)} %bitcast.8.where_ref, s32[16]{0:T(128)} %dynamic-slice_bitcast_fusion.mask_ref, bf16[256,256]{1,0:T(8,128)(2,1)} %constant.49.clone.table_ref, bf16[16,256,512]{2,1,0:T(8,128)(2,1)} %bitcast.13), custom_call_target="tpu_custom_call" | custom-call | flops 134217728 | bytes 1048576 | tf_op jit(solution)/shard_map/pallas_call | solution.py:59
  18.7 3.7 %collective-permute-start.10 = (bf16[8,256,128]{2,1,0:T(8,128)(2,1)}, bf16[8,256,128]{2,1,0:T(8,128)(2,1)}, u32[]{:S(2)}, u32[]{:S(2)}) collective-permute-start(bf16[8,256,128]{2,1,0:T(8,128)(2,1)} %shard_map.73), channel_id=1, source_target_pairs={{2,5},{3,4},{4,3},{5,2},{6,9},{7,8},{8,7},{9,6},{10,13},{11,12},{1... | collective-permute-start | bytes 1572872 | tf_op jit(solution)/shard_map/ppermute | solution.py:261
  22.4 20.1 %collective-permute-done.1.o0a = bf16[8,256,128]{2,1,0:T(8,128)(2,1)} collective-permute-done((bf16[8,256,128]{2,1,0:T(8,128)(2,1)}, bf16[8,256,128]{2,1,0:T(8,128)(2,1)}, u32[]{:S(2)}, u32[]{:S(2)}) %collective-permute-start.1) | collective-permute-done | bytes 524320 | tf_op jit(solution)/shard_map/ppermute | solution.py:261
  42.5 9.1 %collective-permute-done.2.o1a = bf16[8,256,128]{2,1,0:T(8,128)(2,1)} collective-permute-done((bf16[8,256,128]{2,1,0:T(8,128)(2,1)}, bf16[8,256,128]{2,1,0:T(8,128)(2,1)}, u32[]{:S(2)}, u32[]{:S(2)}) %collective-permute-start.2) | collective-permute-done | bytes 524320 | tf_op jit(solution)/shard_map/ppermute | solution.py:261
  51.6 0.0 copy-done.5
  51.6 1.3 collective-permute-start.3
  53.0 0.8 collective-permute-start.4
  53.8 3.5 %collective-permute-start.7 = (bf16[8,256,128]{2,1,0:T(8,128)(2,1)}, bf16[8,256,128]{2,1,0:T(8,128)(2,1)}, u32[]{:S(2)}, u32[]{:S(2)}) collective-permute-start(bf16[8,256,128]{2,1,0:T(8,128)(2,1)} %collective-permute-done.1.o0a), channel_id=1, source_target_pairs={{0,4},{1,5},{4,8},{5,9},{6,2},{7,3},{8,12},{9,13},{10,6},{11,7},{1... | collective-permute-start | bytes 1572872 | tf_op jit(solution)/shard_map/ppermute | solution.py:261
  57.2 0.0 collective-permute-done.8.v0b
  57.2 0.0 copy-start.4
  57.3 1.9 %collective-permute-start.9 = (bf16[8,256,128]{2,1,0:T(8,128)(2,1)}, bf16[8,256,128]{2,1,0:T(8,128)(2,1)}, u32[]{:S(2)}, u32[]{:S(2)}) collective-permute-start(bf16[8,256,128]{2,1,0:T(8,128)(2,1)} %collective-permute-done.2.o1a), channel_id=1, source_target_pairs={{0,4},{1,5},{4,8},{5,9},{6,2},{7,3},{8,12},{9,13},{10,6},{11,7},{1... | collective-permute-start | bytes 1572872 | tf_op jit(solution)/shard_map/ppermute | solution.py:261
  59.2 4.7 %shard_map.69 = bf16[16,256,128]{2,1,0:T(8,128)(2,1)} custom-call(s32[1]{0:T(128)} %bitcast.6.where_ref, s32[16]{0:T(128)} %dynamic-slice_bitcast_fusion.mask_ref, bf16[256,256]{1,0:T(8,128)(2,1)} %constant.49.clone.table_ref, bf16[16,256,512]{2,1,0:T(8,128)(2,1)} %bitcast.14), custom_call_target="tpu_custom_call" | custom-call | flops 268435456 | bytes 2097152 | tf_op jit(solution)/shard_map/pallas_call | solution.py:59
  63.9 0.0 copy-done.4
  63.9 4.8 %shard_map.68.own = bf16[16,256,128]{2,1,0:T(8,128)(2,1)} custom-call(s32[1]{0:T(128)} %bitcast.3.where_ref, s32[16]{0:T(128)} %dynamic-slice_bitcast_fusion.mask_ref, bf16[256,256]{1,0:T(8,128)(2,1)} %constant.49.clone.table_ref, bf16[16,256,512]{2,1,0:T(8,128)(2,1)} %bitcast.15), custom_call_target="tpu_custom_call" | custom-call | flops 268435456 | bytes 2097152 | tf_op jit(solution)/shard_map/pallas_call | solution.py:59
  68.7 0.0 collective-permute-done.10.v1b
  68.7 0.7 collective-permute-start.11
  69.4 0.0 collective-permute-done.3.o0b
  69.4 3.9 %collective-permute-start.5 = (bf16[16,256,128]{2,1,0:T(8,128)(2,1)}, bf16[16,256,128]{2,1,0:T(8,128)(2,1)S(1)}, u32[]{:S(2)}, u32[]{:S(2)}) collective-permute-start(bf16[16,256,128]{2,1,0:T(8,128)(2,1)} %shard_map.68.own), channel_id=1, source_target_pairs={{2,6},{3,7},{4,0},{5,1},{6,10},{7,11},{8,4},{9,5},{10,14},{11,15},... | collective-permute-start | bytes 3145736 | tf_op jit(solution)/shard_map/ppermute | solution.py:261
  73.4 4.0 %collective-permute-done.4.o1b = bf16[8,256,128]{2,1,0:T(8,128)(2,1)} collective-permute-done((bf16[8,256,128]{2,1,0:T(8,128)(2,1)}, bf16[8,256,128]{2,1,0:T(8,128)(2,1)}, u32[]{:S(2)}, u32[]{:S(2)}) %collective-permute-start.4) | collective-permute-done | bytes 524320 | tf_op jit(solution)/shard_map/ppermute | solution.py:261
  77.4 0.0 copy-done.1
  77.4 1.3 collective-permute-start.12
  78.7 0.0 collective-permute-done.7.v0a
  78.7 5.2 %collective-permute-start.6 = (bf16[16,256,128]{2,1,0:T(8,128)(2,1)S(1)}, bf16[16,256,128]{2,1,0:T(8,128)(2,1)}, u32[]{:S(2)}, u32[]{:S(2)}) collective-permute-start(bf16[16,256,128]{2,1,0:T(8,128)(2,1)S(1)} %copy-done.1), channel_id=1, source_target_pairs={{2,7},{3,6},{4,1},{5,0},{6,11},{7,10},{8,5},{9,4},{10,15},{11,14},... | collective-permute-start | bytes 3145736 | tf_op jit(solution)/shard_map/ppermute | solution.py:261
  83.9 0.0 collective-permute-done.9.v1a
  83.9 0.2 collective-permute-start
  84.2 0.6 pad_add_fusion.place_ref
  84.8 0.0 collective-permute-done.11.ea
  84.8 12.7 %collective-permute-done.5.x0 = bf16[16,256,128]{2,1,0:T(8,128)(2,1)S(1)} collective-permute-done((bf16[16,256,128]{2,1,0:T(8,128)(2,1)}, bf16[16,256,128]{2,1,0:T(8,128)(2,1)S(1)}, u32[]{:S(2)}, u32[]{:S(2)}) %collective-permute-start.5) | collective-permute-done | bytes 1048608 | tf_op jit(solution)/shard_map/ppermute | solution.py:261
  97.6 5.9 %collective-permute-done.12.eb = bf16[16,256,128]{2,1,0:T(8,128)(2,1)} collective-permute-done((bf16[16,256,128]{2,1,0:T(8,128)(2,1)S(1)}, bf16[16,256,128]{2,1,0:T(8,128)(2,1)}, u32[]{:S(2)}, u32[]{:S(2)}) %collective-permute-start.12) | collective-permute-done | bytes 1048608 | tf_op jit(solution)/shard_map/ppermute | solution.py:261
  103.5 16.2 %collective-permute-done.6.x1 = bf16[16,256,128]{2,1,0:T(8,128)(2,1)} collective-permute-done((bf16[16,256,128]{2,1,0:T(8,128)(2,1)S(1)}, bf16[16,256,128]{2,1,0:T(8,128)(2,1)}, u32[]{:S(2)}, u32[]{:S(2)}) %collective-permute-start.6) | collective-permute-done | bytes 1048608 | tf_op jit(solution)/shard_map/ppermute | solution.py:261
  119.7 0.0 collective-permute-done.sib
  119.7 0.0 copy-done.2
  119.7 0.0 copy-done.3
  119.7 16.3 %shard_map.74 = (bf16[7,128,128]{2,1,0:T(8,128)(2,1)}, bf16[7,128,128]{2,1,0:T(8,128)(2,1)}, bf16[7,128,128]{2,1,0:T(8,128)(2,1)}, bf16[7,128,128]{2,1,0:T(8,128...) custom-call(s32[4]{0:T(128)} %pad_add_fusion.place_ref, ...), custom_call_target="tpu_custom_call" | custom-call | flops 83886080 | bytes 9437184 | tf_op jit(solution)/shard_map/pallas_call | solution.py:170
  136.0 1.9 %collective-permute-start.16 = (bf16[3,128,128]{2,1,0:T(8,128)(2,1)}, bf16[3,128,128]{2,1,0:T(8,128)(2,1)S(1)}, u32[]{:S(2)}, u32[]{:S(2)}) collective-permute-start(bf16[3,128,128]{2,1,0:T(8,128)(2,1)} %get-tuple-element.23), channel_id=1, source_target_pairs={{0,4},{1,5},{4,8},{5,9},{6,2},{7,3},{8,12},{9,13},{10,6},{11,7},{1... | collective-permute-start | bytes 294920 | tf_op jit(solution)/shard_map/ppermute | solution.py:261
  137.9 3.4 %collective-permute-start.21 = (bf16[1,128,128]{2,1,0:T(8,128)(2,1)}, bf16[1,128,128]{2,1,0:T(8,128)(2,1)S(1)}, u32[]{:S(2)}, u32[]{:S(2)}) collective-permute-start(bf16[1,128,128]{2,1,0:T(8,128)(2,1)} %get-tuple-element.27), channel_id=1, source_target_pairs={{3,6},{4,1},{7,10},{8,5},{11,14},{12,9},{19,22},{20,17},{23,26},{2... | collective-permute-start | bytes 98312 | tf_op jit(solution)/shard_map/ppermute | solution.py:261
  141.3 1.9 %collective-permute-start.17 = (bf16[3,128,128]{2,1,0:T(8,128)(2,1)}, bf16[3,128,128]{2,1,0:T(8,128)(2,1)S(1)}, u32[]{:S(2)}, u32[]{:S(2)}) collective-permute-start(bf16[3,128,128]{2,1,0:T(8,128)(2,1)} %get-tuple-element.24), channel_id=1, source_target_pairs={{0,5},{1,4},{4,9},{5,8},{6,3},{7,2},{8,13},{9,12},{10,7},{11,6},{1... | collective-permute-start | bytes 294920 | tf_op jit(solution)/shard_map/ppermute | solution.py:261
  143.2 0.7 collective-permute-start.20
  143.9 3.2 %collective-permute-start.13 = (bf16[7,128,128]{2,1,0:T(8,128)(2,1)}, bf16[7,128,128]{2,1,0:T(8,128)(2,1)S(1)}, u32[]{:S(2)}, u32[]{:S(2)}) collective-permute-start(bf16[7,128,128]{2,1,0:T(8,128)(2,1)} %get-tuple-element.20), channel_id=1, source_target_pairs={{0,1},{1,0},{2,3},{3,2},{4,5},{5,4},{6,7},{7,6},{8,9},{9,8},{10,11... | collective-permute-start | bytes 688136 | tf_op jit(solution)/shard_map/ppermute | solution.py:261
  147.0 0.0 collective-permute-done.21.w1
  147.1 0.0 collective-permute-start.14
  147.1 0.0 collective-permute-done.20.w0
  147.1 1.4 collective-permute-start.15
  148.5 0.0 collective-permute-done.16.s0
  148.5 4.7 %collective-permute-start.18 = (bf16[5,128,128]{2,1,0:T(8,128)(2,1)}, bf16[5,128,128]{2,1,0:T(8,128)(2,1)S(1)}, u32[]{:S(2)}, u32[]{:S(2)}) collective-permute-start(bf16[5,128,128]{2,1,0:T(8,128)(2,1)} %get-tuple-element.25), channel_id=1, source_target_pairs={{2,4},{3,5},{4,2},{5,3},{6,8},{7,9},{8,6},{9,7},{10,12},{11,13},{1... | collective-permute-start | bytes 491528 | tf_op jit(solution)/shard_map/ppermute | solution.py:261
  153.2 0.0 collective-permute-done.17.s1
  153.2 2.1 %collective-permute-start.19 = (bf16[5,128,128]{2,1,0:T(8,128)(2,1)}, bf16[5,128,128]{2,1,0:T(8,128)(2,1)S(1)}, u32[]{:S(2)}, u32[]{:S(2)}) collective-permute-start(bf16[5,128,128]{2,1,0:T(8,128)(2,1)} %get-tuple-element.26), channel_id=1, source_target_pairs={{2,5},{3,4},{4,3},{5,2},{6,9},{7,8},{8,7},{9,6},{10,13},{11,12},{1... | collective-permute-start | bytes 491528 | tf_op jit(solution)/shard_map/ppermute | solution.py:261
  155.3 3.1 %collective-permute-done.18.d0 = bf16[5,128,128]{2,1,0:T(8,128)(2,1)S(1)} collective-permute-done((bf16[5,128,128]{2,1,0:T(8,128)(2,1)}, bf16[5,128,128]{2,1,0:T(8,128)(2,1)S(1)}, u32[]{:S(2)}, u32[]{:S(2)}) %collective-permute-start.18) | collective-permute-done | bytes 163872 | tf_op jit(solution)/shard_map/ppermute | solution.py:261
  158.4 3.5 %collective-permute-done.19.d1 = bf16[5,128,128]{2,1,0:T(8,128)(2,1)S(1)} collective-permute-done((bf16[5,128,128]{2,1,0:T(8,128)(2,1)}, bf16[5,128,128]{2,1,0:T(8,128)(2,1)S(1)}, u32[]{:S(2)}, u32[]{:S(2)}) %collective-permute-start.19) | collective-permute-done | bytes 163872 | tf_op jit(solution)/shard_map/ppermute | solution.py:261
  161.9 0.0 collective-permute-done.13.g1
  161.9 0.8 collective-permute-done.14.g2
  162.7 3.2 %collective-permute-done.15.g3 = bf16[7,128,128]{2,1,0:T(8,128)(2,1)S(1)} collective-permute-done((bf16[7,128,128]{2,1,0:T(8,128)(2,1)}, bf16[7,128,128]{2,1,0:T(8,128)(2,1)S(1)}, u32[]{:S(2)}, u32[]{:S(2)}) %collective-permute-start.15) | collective-permute-done | bytes 229408 | tf_op jit(solution)/shard_map/ppermute | solution.py:261
  166.0 0.0 copy-done.11
  166.0 0.6 copy-done.8
  166.7 3.3 %shard_map.75 = (f32[1,5,128,512]{3,2,1,0:T(8,128)}, f32[1,5,128,512]{3,2,1,0:T(8,128)}) custom-call(s32[4]{0:T(128)} %pad_add_fusion.place_ref, bf16[7,128,128]{2,1,0:T(8,128)(2,1)} %get-tuple-element.19.g0, bf16[7,128,128]{2,1,0:T(8,128)(2,1)} %copy-done.6, bf16[7,128,128]{2,1,0:T(8,128)(2,1)} %copy-done.7, bf16[7,128,128]{2,1,0:T(8,128)(2,1)} %copy-done.8, ...), custom_call_target="tpu_custom_call" | custom-call | tf_op jit(solution)/shard_map/pallas_call | solution.py:230
  (20 shorter events, 0.0 us)
Async XLA Ops:
  0.6 0.7 copy-start
  4.9 37.6 %collective-permute-start.1 = (bf16[8,256,128]{2,1,0:T(8,128)(2,1)}, bf16[8,256,128]{2,1,0:T(8,128)(2,1)}, u32[]{:S(2)}, u32[]{:S(2)}) collective-permute-start(bf16[8,256,128]{2,1,0:T(8,128)(2,1)} %shard_map.70), channel_id=1, source_target_pairs={{0,2},{1,3},{2,0},{3,1},{4,6},{5,7},{6,4},{7,5},{8,10},{9,11},{10,... | collective-permute-start | bytes 1572872 | tf_op jit(solution)/shard_map/ppermute | solution.py:261
  9.5 42.2 %collective-permute-start.2 = (bf16[8,256,128]{2,1,0:T(8,128)(2,1)}, bf16[8,256,128]{2,1,0:T(8,128)(2,1)}, u32[]{:S(2)}, u32[]{:S(2)}) collective-permute-start(bf16[8,256,128]{2,1,0:T(8,128)(2,1)} %shard_map.71), channel_id=1, source_target_pairs={{0,3},{1,2},{2,1},{3,0},{4,7},{5,6},{6,5},{7,4},{8,11},{9,10},{10,... | collective-permute-start | bytes 1572872 | tf_op jit(solution)/shard_map/ppermute | solution.py:261
  12.5 39.1 %copy-start.5 = (bf16[8,256,128]{2,1,0:T(8,128)(2,1)S(1)}, bf16[8,256,128]{2,1,0:T(8,128)(2,1)}, u32[]{:S(2)}) copy-start(bf16[8,256,128]{2,1,0:T(8,128)(2,1)} %shard_map.72) | copy-start | bytes 1572868
  12.5 44.7 %collective-permute-start.8 = (bf16[8,256,128]{2,1,0:T(8,128)(2,1)}, bf16[8,256,128]{2,1,0:T(8,128)(2,1)S(1)}, u32[]{:S(2)}, u32[]{:S(2)}) collective-permute-start(bf16[8,256,128]{2,1,0:T(8,128)(2,1)} %shard_map.72), channel_id=1, source_target_pairs={{2,4},{3,5},{4,2},{5,3},{6,8},{7,9},{8,6},{9,7},{10,12},{11,13},{1... | collective-permute-start | bytes 1572872 | tf_op jit(solution)/shard_map/ppermute | solution.py:261
  18.7 50.0 %collective-permute-start.10 = (bf16[8,256,128]{2,1,0:T(8,128)(2,1)}, bf16[8,256,128]{2,1,0:T(8,128)(2,1)}, u32[]{:S(2)}, u32[]{:S(2)}) collective-permute-start(bf16[8,256,128]{2,1,0:T(8,128)(2,1)} %shard_map.73), channel_id=1, source_target_pairs={{2,5},{3,4},{4,3},{5,2},{6,9},{7,8},{8,7},{9,6},{10,13},{11,12},{1... | collective-permute-start | bytes 1572872 | tf_op jit(solution)/shard_map/ppermute | solution.py:261
  51.6 17.8 %collective-permute-start.3 = (bf16[8,256,128]{2,1,0:T(8,128)(2,1)S(1)}, bf16[8,256,128]{2,1,0:T(8,128)(2,1)}, u32[]{:S(2)}, u32[]{:S(2)}) collective-permute-start(bf16[8,256,128]{2,1,0:T(8,128)(2,1)S(1)} %copy-done.5), channel_id=1, source_target_pairs={{0,2},{1,3},{2,0},{3,1},{4,6},{5,7},{6,4},{7,5},{8,10},{9,11},{10,... | collective-permute-start | bytes 1572872 | tf_op jit(solution)/shard_map/ppermute | solution.py:261
  53.0 24.4 %collective-permute-start.4 = (bf16[8,256,128]{2,1,0:T(8,128)(2,1)}, bf16[8,256,128]{2,1,0:T(8,128)(2,1)}, u32[]{:S(2)}, u32[]{:S(2)}) collective-permute-start(bf16[8,256,128]{2,1,0:T(8,128)(2,1)} %shard_map.73), channel_id=1, source_target_pairs={{0,3},{1,2},{2,1},{3,0},{4,7},{5,6},{6,5},{7,4},{8,11},{9,10},{10,... | collective-permute-start | bytes 1572872 | tf_op jit(solution)/shard_map/ppermute | solution.py:261
  53.8 24.9 %collective-permute-start.7 = (bf16[8,256,128]{2,1,0:T(8,128)(2,1)}, bf16[8,256,128]{2,1,0:T(8,128)(2,1)}, u32[]{:S(2)}, u32[]{:S(2)}) collective-permute-start(bf16[8,256,128]{2,1,0:T(8,128)(2,1)} %collective-permute-done.1.o0a), channel_id=1, source_target_pairs={{0,4},{1,5},{4,8},{5,9},{6,2},{7,3},{8,12},{9,13},{10,6},{11,7},{1... | collective-permute-start | bytes 1572872 | tf_op jit(solution)/shard_map/ppermute | solution.py:261
  57.2 6.6 %copy-start.4 = (bf16[8,256,128]{2,1,0:T(8,128)(2,1)}, bf16[8,256,128]{2,1,0:T(8,128)(2,1)S(1)}, u32[]{:S(2)}) copy-start(bf16[8,256,128]{2,1,0:T(8,128)(2,1)S(1)} %collective-permute-done.8.v0b) | copy-start | bytes 1572868
  57.3 26.7 %collective-permute-start.9 = (bf16[8,256,128]{2,1,0:T(8,128)(2,1)}, bf16[8,256,128]{2,1,0:T(8,128)(2,1)}, u32[]{:S(2)}, u32[]{:S(2)}) collective-permute-start(bf16[8,256,128]{2,1,0:T(8,128)(2,1)} %collective-permute-done.2.o1a), channel_id=1, source_target_pairs={{0,4},{1,5},{4,8},{5,9},{6,2},{7,3},{8,12},{9,13},{10,6},{11,7},{1... | collective-permute-start | bytes 1572872 | tf_op jit(solution)/shard_map/ppermute | solution.py:261
  63.9 13.5 %copy-start.1 = (bf16[16,256,128]{2,1,0:T(8,128)(2,1)S(1)}, bf16[16,256,128]{2,1,0:T(8,128)(2,1)}, u32[]{:S(2)}) copy-start(bf16[16,256,128]{2,1,0:T(8,128)(2,1)} %shard_map.69) | copy-start | bytes 3145732
  68.7 16.1 %collective-permute-start.11 = (bf16[16,256,128]{2,1,0:T(8,128)(2,1)}, bf16[16,256,128]{2,1,0:T(8,128)(2,1)S(1)}, u32[]{:S(2)}, u32[]{:S(2)}) collective-permute-start(bf16[16,256,128]{2,1,0:T(8,128)(2,1)} %shard_map.68.own), channel_id=1, source_target_pairs={{1,5},{5,9},{6,2},{9,13},{10,6},{14,10},{17,21},{21,25},{22,18},{2... | collective-permute-start | bytes 3145736 | tf_op jit(solution)/shard_map/ppermute | solution.py:261
  69.4 28.1 %collective-permute-start.5 = (bf16[16,256,128]{2,1,0:T(8,128)(2,1)}, bf16[16,256,128]{2,1,0:T(8,128)(2,1)S(1)}, u32[]{:S(2)}, u32[]{:S(2)}) collective-permute-start(bf16[16,256,128]{2,1,0:T(8,128)(2,1)} %shard_map.68.own), channel_id=1, source_target_pairs={{2,6},{3,7},{4,0},{5,1},{6,10},{7,11},{8,4},{9,5},{10,14},{11,15},... | collective-permute-start | bytes 3145736 | tf_op jit(solution)/shard_map/ppermute | solution.py:261
  77.4 26.1 %collective-permute-start.12 = (bf16[16,256,128]{2,1,0:T(8,128)(2,1)S(1)}, bf16[16,256,128]{2,1,0:T(8,128)(2,1)}, u32[]{:S(2)}, u32[]{:S(2)}) collective-permute-start(bf16[16,256,128]{2,1,0:T(8,128)(2,1)S(1)} %copy-done.1), channel_id=1, source_target_pairs={{1,4},{5,8},{6,3},{9,12},{10,7},{14,11},{17,20},{21,24},{22,19},{2... | collective-permute-start | bytes 3145736 | tf_op jit(solution)/shard_map/ppermute | solution.py:261
  78.7 41.0 %collective-permute-start.6 = (bf16[16,256,128]{2,1,0:T(8,128)(2,1)S(1)}, bf16[16,256,128]{2,1,0:T(8,128)(2,1)}, u32[]{:S(2)}, u32[]{:S(2)}) collective-permute-start(bf16[16,256,128]{2,1,0:T(8,128)(2,1)S(1)} %copy-done.1), channel_id=1, source_target_pairs={{2,7},{3,6},{4,1},{5,0},{6,11},{7,10},{8,5},{9,4},{10,15},{11,14},... | collective-permute-start | bytes 3145736 | tf_op jit(solution)/shard_map/ppermute | solution.py:261
  83.9 35.7 %collective-permute-start = (bf16[16,256,128]{2,1,0:T(8,128)(2,1)S(1)}, bf16[16,256,128]{2,1,0:T(8,128)(2,1)}, u32[]{:S(2)}, u32[]{:S(2)}) collective-permute-start(bf16[16,256,128]{2,1,0:T(8,128)(2,1)S(1)} %copy-done.1), channel_id=1, source_target_pairs={{0,1},{1,0},{2,3},{3,2},{4,5},{5,4},{6,7},{7,6},{8,9},{9,8},{10,11... | collective-permute-start | bytes 3145736 | tf_op jit(solution)/shard_map/ppermute | solution.py:261
  84.8 34.9 %copy-start.2 = (bf16[16,256,128]{2,1,0:T(8,128)(2,1)}, bf16[16,256,128]{2,1,0:T(8,128)(2,1)S(1)}, u32[]{:S(2)}) copy-start(bf16[16,256,128]{2,1,0:T(8,128)(2,1)S(1)} %collective-permute-done.11.ea) | copy-start | bytes 3145732
  97.6 22.1 %copy-start.3 = (bf16[16,256,128]{2,1,0:T(8,128)(2,1)}, bf16[16,256,128]{2,1,0:T(8,128)(2,1)S(1)}, u32[]{:S(2)}) copy-start(bf16[16,256,128]{2,1,0:T(8,128)(2,1)S(1)} %collective-permute-done.5.x0) | copy-start | bytes 3145732
  136.0 12.5 %collective-permute-start.16 = (bf16[3,128,128]{2,1,0:T(8,128)(2,1)}, bf16[3,128,128]{2,1,0:T(8,128)(2,1)S(1)}, u32[]{:S(2)}, u32[]{:S(2)}) collective-permute-start(bf16[3,128,128]{2,1,0:T(8,128)(2,1)} %get-tuple-element.23), channel_id=1, source_target_pairs={{0,4},{1,5},{4,8},{5,9},{6,2},{7,3},{8,12},{9,13},{10,6},{11,7},{1... | collective-permute-start | bytes 294920 | tf_op jit(solution)/shard_map/ppermute | solution.py:261
  137.9 9.1 %collective-permute-start.21 = (bf16[1,128,128]{2,1,0:T(8,128)(2,1)}, bf16[1,128,128]{2,1,0:T(8,128)(2,1)S(1)}, u32[]{:S(2)}, u32[]{:S(2)}) collective-permute-start(bf16[1,128,128]{2,1,0:T(8,128)(2,1)} %get-tuple-element.27), channel_id=1, source_target_pairs={{3,6},{4,1},{7,10},{8,5},{11,14},{12,9},{19,22},{20,17},{23,26},{2... | collective-permute-start | bytes 98312 | tf_op jit(solution)/shard_map/ppermute | solution.py:261
  141.3 11.9 %collective-permute-start.17 = (bf16[3,128,128]{2,1,0:T(8,128)(2,1)}, bf16[3,128,128]{2,1,0:T(8,128)(2,1)S(1)}, u32[]{:S(2)}, u32[]{:S(2)}) collective-permute-start(bf16[3,128,128]{2,1,0:T(8,128)(2,1)} %get-tuple-element.24), channel_id=1, source_target_pairs={{0,5},{1,4},{4,9},{5,8},{6,3},{7,2},{8,13},{9,12},{10,7},{11,6},{1... | collective-permute-start | bytes 294920 | tf_op jit(solution)/shard_map/ppermute | solution.py:261
  143.2 3.8 %collective-permute-start.20 = (bf16[1,128,128]{2,1,0:T(8,128)(2,1)}, bf16[1,128,128]{2,1,0:T(8,128)(2,1)S(1)}, u32[]{:S(2)}, u32[]{:S(2)}) collective-permute-start(bf16[1,128,128]{2,1,0:T(8,128)(2,1)} %get-tuple-element.27), channel_id=1, source_target_pairs={{2,6},{5,1},{6,10},{9,5},{10,14},{13,9},{18,22},{21,17},{22,26},{2... | collective-permute-start | bytes 98312 | tf_op jit(solution)/shard_map/ppermute | solution.py:261
  143.9 18.0 %collective-permute-start.13 = (bf16[7,128,128]{2,1,0:T(8,128)(2,1)}, bf16[7,128,128]{2,1,0:T(8,128)(2,1)S(1)}, u32[]{:S(2)}, u32[]{:S(2)}) collective-permute-start(bf16[7,128,128]{2,1,0:T(8,128)(2,1)} %get-tuple-element.20), channel_id=1, source_target_pairs={{0,1},{1,0},{2,3},{3,2},{4,5},{5,4},{6,7},{7,6},{8,9},{9,8},{10,11... | collective-permute-start | bytes 688136 | tf_op jit(solution)/shard_map/ppermute | solution.py:261
  147.1 18.9 %copy-start.13 = (bf16[1,128,128]{2,1,0:T(8,128)(2,1)}, bf16[1,128,128]{2,1,0:T(8,128)(2,1)S(1)}, u32[]{:S(2)}) copy-start(bf16[1,128,128]{2,1,0:T(8,128)(2,1)S(1)} %collective-permute-done.21.w1) | copy-start | bytes 98308
  147.1 15.7 %collective-permute-start.14 = (bf16[7,128,128]{2,1,0:T(8,128)(2,1)}, bf16[7,128,128]{2,1,0:T(8,128)(2,1)S(1)}, u32[]{:S(2)}, u32[]{:S(2)}) collective-permute-start(bf16[7,128,128]{2,1,0:T(8,128)(2,1)} %get-tuple-element.21), channel_id=1, source_target_pairs={{0,2},{1,3},{2,0},{3,1},{4,6},{5,7},{6,4},{7,5},{8,10},{9,11},{10,... | collective-permute-start | bytes 688136 | tf_op jit(solution)/shard_map/ppermute | solution.py:261
  147.1 18.9 %copy-start.14 = (bf16[1,128,128]{2,1,0:T(8,128)(2,1)}, bf16[1,128,128]{2,1,0:T(8,128)(2,1)S(1)}, u32[]{:S(2)}) copy-start(bf16[1,128,128]{2,1,0:T(8,128)(2,1)S(1)} %collective-permute-done.20.w0) | copy-start | bytes 98308
  147.1 18.9 %collective-permute-start.15 = (bf16[7,128,128]{2,1,0:T(8,128)(2,1)}, bf16[7,128,128]{2,1,0:T(8,128)(2,1)S(1)}, u32[]{:S(2)}, u32[]{:S(2)}) collective-permute-start(bf16[7,128,128]{2,1,0:T(8,128)(2,1)} %get-tuple-element.22), channel_id=1, source_target_pairs={{0,3},{1,2},{2,1},{3,0},{4,7},{5,6},{6,5},{7,4},{8,11},{9,10},{10,... | collective-permute-start | bytes 688136 | tf_op jit(solution)/shard_map/ppermute | solution.py:261
  148.5 17.5 %copy-start.11 = (bf16[3,128,128]{2,1,0:T(8,128)(2,1)}, bf16[3,128,128]{2,1,0:T(8,128)(2,1)S(1)}, u32[]{:S(2)}) copy-start(bf16[3,128,128]{2,1,0:T(8,128)(2,1)S(1)} %collective-permute-done.16.s0) | copy-start | bytes 294916
  148.5 9.9 %collective-permute-start.18 = (bf16[5,128,128]{2,1,0:T(8,128)(2,1)}, bf16[5,128,128]{2,1,0:T(8,128)(2,1)S(1)}, u32[]{:S(2)}, u32[]{:S(2)}) collective-permute-start(bf16[5,128,128]{2,1,0:T(8,128)(2,1)} %get-tuple-element.25), channel_id=1, source_target_pairs={{2,4},{3,5},{4,2},{5,3},{6,8},{7,9},{8,6},{9,7},{10,12},{11,13},{1... | collective-permute-start | bytes 491528 | tf_op jit(solution)/shard_map/ppermute | solution.py:261
  153.2 12.8 %copy-start.12 = (bf16[3,128,128]{2,1,0:T(8,128)(2,1)}, bf16[3,128,128]{2,1,0:T(8,128)(2,1)S(1)}, u32[]{:S(2)}) copy-start(bf16[3,128,128]{2,1,0:T(8,128)(2,1)S(1)} %collective-permute-done.17.s1) | copy-start | bytes 294916
  153.2 8.7 %collective-permute-start.19 = (bf16[5,128,128]{2,1,0:T(8,128)(2,1)}, bf16[5,128,128]{2,1,0:T(8,128)(2,1)S(1)}, u32[]{:S(2)}, u32[]{:S(2)}) collective-permute-start(bf16[5,128,128]{2,1,0:T(8,128)(2,1)} %get-tuple-element.26), channel_id=1, source_target_pairs={{2,5},{3,4},{4,3},{5,2},{6,9},{7,8},{8,7},{9,6},{10,13},{11,12},{1... | collective-permute-start | bytes 491528 | tf_op jit(solution)/shard_map/ppermute | solution.py:261
  158.4 7.6 %copy-start.9 = (bf16[5,128,128]{2,1,0:T(8,128)(2,1)}, bf16[5,128,128]{2,1,0:T(8,128)(2,1)S(1)}, u32[]{:S(2)}) copy-start(bf16[5,128,128]{2,1,0:T(8,128)(2,1)S(1)} %collective-permute-done.18.d0) | copy-start | bytes 491524
  161.9 4.1 %copy-start.10 = (bf16[5,128,128]{2,1,0:T(8,128)(2,1)}, bf16[5,128,128]{2,1,0:T(8,128)(2,1)S(1)}, u32[]{:S(2)}) copy-start(bf16[5,128,128]{2,1,0:T(8,128)(2,1)S(1)} %collective-permute-done.19.d1) | copy-start | bytes 491524
  161.9 4.1 %copy-start.6 = (bf16[7,128,128]{2,1,0:T(8,128)(2,1)}, bf16[7,128,128]{2,1,0:T(8,128)(2,1)S(1)}, u32[]{:S(2)}) copy-start(bf16[7,128,128]{2,1,0:T(8,128)(2,1)S(1)} %collective-permute-done.13.g1) | copy-start | bytes 688132
  162.7 3.3 %copy-start.7 = (bf16[7,128,128]{2,1,0:T(8,128)(2,1)}, bf16[7,128,128]{2,1,0:T(8,128)(2,1)S(1)}, u32[]{:S(2)}) copy-start(bf16[7,128,128]{2,1,0:T(8,128)(2,1)S(1)} %collective-permute-done.14.g2) | copy-start | bytes 688132
  165.9 0.7 copy-start.8

commit v2 on v0

v2 whole, which is shorter than its diff:
```python
import functools
import math

import jax
import jax.numpy as jnp
import numpy as np
from jax import lax
from jax.experimental import pallas as pl
from jax.experimental.pallas import tpu as pltpu
from jax.sharding import PartitionSpec as P

MAXP = 5
PLANE = 4
VMEM = 56 * 1024 * 1024
ROWS = 16
CHUNKS = 2

BASE = (
    ((0, 4), (0, 5), (1, 4), (1, 5), (0, 1)),
    ((0, 2), (0, 3), (1, 2), (1, 3), (2, 3)),
    ((3, 5), (-3, 2)),
)
OUTER = (((-1, 0), (-1, 2), (-1, 3), (-1, 4)),)
INNER = (((-2, 0), (-2, 1), (-2, 2), (-2, 3)),)
ALL = BASE + OUTER + INNER
DESTS = ((0, 1), (2, 3), (4, 5), (-2, -1), (None, -3))


def flat(groups):
    return [pair for group in groups for pair in group]


PAIRS = flat(ALL)


def items(spot):
    ahead = sorted(("ahead", b - a - 1) for a, b in PAIRS if a == spot)
    back = sorted(("back", b - a - 1) for a, b in PAIRS if b == spot)
    return ahead + back


SIZES = [max(len(items(spot)) for spot in spots) for spots in DESTS]
STARTS = [sum(SIZES[:d]) for d in range(len(SIZES))]
PLACE = {spot: (d, i) for d, spots in enumerate(DESTS) for i, spot in enumerate(spots)}


def lag_tables(lags):
    bins = lags // 2
    phase = (np.arange(lags)[:, None] * np.arange(1, bins + 1)[None, :] % lags) * (2.0 * math.pi / lags)
    real, imag = np.cos(phase), -np.sin(phase)
    causal = np.concatenate([real, imag], axis=1)
    other = np.concatenate([real, -imag], axis=1)
    near = np.concatenate([causal[:bins], causal[bins:][::-1]], axis=0)
    far = np.concatenate([other[bins:][::-1], other[:bins]], axis=0)
    return causal.astype(jnp.bfloat16), np.stack([near, far]).astype(jnp.bfloat16)


def whereabouts():
    me = lax.axis_index("chan").astype(jnp.int32)
    q = lax.rem(me, PLANE)
    far = q // 2
    return far, lax.rem(q, 2) ^ far, me - q, q


def whiten_body(mask_ref, table_ref, traces_ref, t0, t1, t2, t3, white, sems):
    outs = (t0, t1, t2, t3)
    _, _, base, q = whereabouts()
    bins = table_ref.shape[0] // 2
    part = white.shape[-1]
    step = traces_ref.shape[0]
    at = pl.program_id(0)
    for n in range(step):
        w = at * step + n
        raw = jnp.dot(table_ref[...], traces_ref[n], preferred_element_type=jnp.float32)
        power = jnp.sum(raw * raw, axis=0, keepdims=True) / bins
        valid = mask_ref[base + q, w].astype(jnp.float32)
        scaled = (raw * (valid * lax.rsqrt(power + 1e-06))).astype(jnp.bfloat16)
        for quarter in range(PLANE):
            piece = scaled[:, quarter * part:(quarter + 1) * part]
            white[quarter ^ q, w, 0] = piece[:bins]
            white[quarter ^ q, w, 1] = piece[bins:]

    def copy(k, i):
        span = pl.ds(i * step, step)
        return pltpu.make_async_copy(white.at[k, span], outs[k].at[span], sems.at[k, i])

    for k in range(PLANE):
        copy(k, at).start()

    @pl.when(at == pl.num_programs(0) - 1)
    def _():
        for k in range(PLANE):
            for i in range(sems.shape[1]):
                copy(k, i).wait()


def whiten(mask, table, record):
    windows, lags, width = record.shape
    bins = lags // 2
    part = width // PLANE
    step = 4
    return pl.pallas_call(
        whiten_body,
        grid=(windows // step,),
        in_specs=[
            pl.BlockSpec(memory_space=pltpu.SMEM),
            pl.BlockSpec((lags, lags), lambda i: (0, 0)),
            pl.BlockSpec((step, lags, width), lambda i: (i, 0, 0)),
        ],
        out_specs=[pl.BlockSpec(memory_space=pl.ANY)] * PLANE,
        out_shape=[jax.ShapeDtypeStruct((windows, 2, bins, part), jnp.bfloat16)] * PLANE,
        scratch_shapes=[
            pltpu.VMEM((PLANE, windows, 2, bins, part), jnp.bfloat16),
            pltpu.SemaphoreType.DMA((PLANE, windows // step)),
        ],
        compiler_params=pltpu.CompilerParams(vmem_limit_bytes=VMEM),
        cost_estimate=pl.CostEstimate(flops=2 * windows * lags * lags * width, bytes_accessed=4 * windows * lags * width, transcendentals=0),
    )(mask, table, record)


def on(m, mine):
    return (lambda body: body()) if mine is None else pl.when(m == mine)


def correlate_body(counts_ref, table_ref, *refs, work, slots, loads, late):
    ins, refs = refs[:len(loads)], refs[len(loads) + late * (len(DESTS) + 1):]
    outs, refs = refs[:len(DESTS) + 1], refs[len(DESTS) + 1:]
    blocks_ref, stack, kept, sems, out_sems = refs[0], refs[1], refs[2:2 + len(DESTS)], refs[-2], refs[-1]
    windows, _, bins, part = ins[0].shape
    far, m, base, _ = whereabouts()
    blocks = counts_ref.shape[0]
    chunk = bins // CHUNKS

    waits = [[] for _ in range(CHUNKS)]
    for c in range(CHUNKS):
        span = pl.ds(c * chunk, chunk)
        for n, both in enumerate(loads):
            there = [s for s in both if s is not None]
            mine = None if len(there) == 2 else both.index(there[0])
            slot = there[0] + m * (there[-1] - there[0])
            one = pltpu.make_async_copy(ins[n].at[:, :, span], blocks_ref.at[slot, :, :, span], sems.at[n, c])
            on(m, mine)(one.start)
            waits[c].append((mine, one))

    scale = 1.0 / math.sqrt(windows)
    begin = [sum(len(flat(groups)) for _, groups in work[:n]) for n in range(len(work))]

    def sum_up(group, at, c):
        need = sorted({spot for pair in group for spot in pair})

        def tile(kt, carry):
            top = pl.multiple_of(kt * ROWS, ROWS)
            rows = pl.ds(top, ROWS)

            def window(w, sums):
                real = {s: blocks_ref[slots[s], w, 0, rows, :].astype(jnp.float32) for s in need}
                imag = {s: blocks_ref[slots[s], w, 1, rows, :].astype(jnp.float32) for s in need}
                out = []
                for n, (a, b) in enumerate(group):
                    out.append(sums[2 * n] + (real[a] * real[b] + imag[a] * imag[b]))
                    out.append(sums[2 * n + 1] + (imag[a] * real[b] - real[a] * imag[b]))
                return tuple(out)

            zero = jnp.zeros((ROWS, part), jnp.float32)
            sums = lax.fori_loop(0, windows, window, (zero,) * (2 * len(group)), unroll=8)
            for n in range(len(group)):
                lanes = pl.ds((at + n) * part, part)
                stack[rows, lanes] = (sums[2 * n] * scale).astype(jnp.bfloat16)
                stack[pl.ds(pl.multiple_of(bins + top, ROWS), ROWS), lanes] = (sums[2 * n + 1] * scale).astype(jnp.bfloat16)
            return carry

        lax.fori_loop(c * chunk // ROWS, (c + 1) * chunk // ROWS, tile, 0)

    norm = 1.0 / math.sqrt(bins)

    def to_lags(groups, at):
        for n, (a, b) in enumerate(flat(groups), at):
            corr = jnp.dot(table_ref[far], stack[:, n * part:(n + 1) * part], preferred_element_type=jnp.float32)
            first = jnp.where(far == 0, base + a, base + 3 - b)
            reach = counts_ref[jnp.clip(first, 0, blocks - 1)]
            corr = corr * jnp.where(reach >= b - a, norm, 0.0)
            for spot, kind, rows in ((a, "ahead", corr[:bins]), (b, "back", corr[bins:])):
                d, i = PLACE[spot]
                kept[d][i, items(spot).index((kind, b - a - 1))] = rows.astype(jnp.bfloat16)

    for c in range(CHUNKS):
        for mine, one in waits[c]:
            on(m, mine)(one.wait)
        for n, (mine, groups) in enumerate(work):
            @on(m, mine)
            def _(at=begin[n], groups=groups):
                for g, group in enumerate(groups):
                    sum_up(group, at + len(flat(groups[:g])), c)

    for n, (mine, groups) in enumerate(work):
        @on(m, mine)
        def _(at=begin[n], mine=mine, groups=groups):
            to_lags(groups, at)
            if not late:
                return
            copies = []
            for a, b in flat(groups):
                for spot, kind in ((a, "ahead"), (b, "back")):
                    d, i = PLACE[spot]
                    row = items(spot).index((kind, b - a - 1))
                    target = outs[d].at[row] if i == mine else outs[-1].at[STARTS[d] + row]
                    copies.append(pltpu.make_async_copy(kept[d].at[i, row], target, out_sems.at[len(copies)]))
            for one in copies:
                one.start()
            for one in copies:
                one.wait()

    if not late:
        copies = []
        for d, size in enumerate(SIZES):
            copies.append(pltpu.make_async_copy(kept[d].at[m], outs[d].at[pl.ds(0, size)], out_sems.at[2 * d]))
            copies.append(pltpu.make_async_copy(kept[d].at[1 - m], outs[-1].at[pl.ds(STARTS[d], size)], out_sems.at[2 * d + 1]))
        for one in copies:
            one.start()
        for one in copies:
            one.wait()


def correlate(counts, tables, whites, work, slots, loads, filled=()):
    windows, _, bins, part = whites[0].shape
    most = max(sum(len(flat(groups)) for mine, groups in work if mine in (None, m)) for m in range(2))
    widest = sum(len(flat(groups)) for _, groups in work)
    anywhere = pl.BlockSpec(memory_space=pl.ANY)
    scalars = pl.BlockSpec(memory_space=pltpu.SMEM)
    lengths = [SIZES[0]] + [2 * size for size in SIZES[1:]] + [sum(SIZES)]
    return pl.pallas_call(
        functools.partial(correlate_body, work=work, slots=slots, loads=loads, late=bool(filled)),
        in_specs=[scalars, pl.BlockSpec(memory_space=pltpu.VMEM)] + [anywhere] * (len(whites) + len(filled)),
        out_specs=[anywhere] * len(lengths),
        out_shape=[jax.ShapeDtypeStruct((n, bins, part), jnp.bfloat16) for n in lengths],
        scratch_shapes=[
            pltpu.VMEM((max(slots.values()) + 1, windows, 2, bins, part), jnp.bfloat16),
            pltpu.VMEM((2 * bins, widest * part), jnp.bfloat16),
            *[pltpu.VMEM((2, size, bins, part), jnp.bfloat16) for size in SIZES],
            pltpu.SemaphoreType.DMA((len(whites), CHUNKS)),
            pltpu.SemaphoreType.DMA((2 * max(len(DESTS), most),)),
        ],
        input_output_aliases={2 + len(whites) + i: i for i in range(len(filled))},
        compiler_params=pltpu.CompilerParams(vmem_limit_bytes=VMEM),
        cost_estimate=pl.CostEstimate(flops=100 * most * windows * bins * part, bytes_accessed=4 * len(whites) * windows * bins * part, transcendentals=0),
    )(counts, tables, *whites, *filled)


def merge_body(sib, *refs):
    outs, sems = refs[len(DESTS) - 1:-1], refs[-1]
    copies = []
    for d in range(1, len(DESTS)):
        copies.append(pltpu.make_async_copy(
            sib.at[pl.ds(STARTS[d], SIZES[d])], outs[d - 1].at[pl.ds(SIZES[d], SIZES[d])], sems.at[d - 1]))
    for one in copies:
        one.start()
    for one in copies:
        one.wait()


def merge(sib, own):
    anywhere = pl.BlockSpec(memory_space=pl.ANY)
    return pl.pallas_call(
        merge_body,
        in_specs=[pl.BlockSpec(memory_space=pltpu.VMEM)] + [anywhere] * len(own),
        out_specs=[anywhere] * len(own),
        out_shape=[jax.ShapeDtypeStruct(value.shape, value.dtype) for value in own],
        scratch_shapes=[pltpu.SemaphoreType.DMA((len(own),))],
        input_output_aliases={1 + i: i for i in range(len(own))},
    )(sib, *own)


def assemble_body(*refs, plan, count, filled):
    ins, refs = refs[:count], refs[count + 2 * filled:]
    forward, backward, wide, sems = refs
    far, m, _, q = whereabouts()
    part = ins[0].shape[2]
    for mine in range(2):
        @pl.when(m == mine)
        def _(mine=mine):
            waits = []
            for a, k, spot, first in plan[mine]:
                lanes = pl.ds(pl.multiple_of((q ^ k) * part, part), part)
                ahead = far if k < 2 else 1 - far
                for n, (kind, j) in enumerate(items(spot)):
                    at = len(waits)
                    wide[at] = ins[a][first + n].astype(jnp.float32)
                    side = ahead if kind == "ahead" else 1 - ahead
                    copies = [pltpu.make_async_copy(wide.at[at], ref.at[0, j, :, lanes], sems.at[at]) for ref in (forward, backward)]
                    for value, copy in enumerate(copies):
                        pl.when(side == value)(copy.start)
                    waits.append(copies[0])
            for copy in waits:
                copy.wait()


def assemble(parts, shape, plan, filled=()):
    steps = max(sum(len(items(spot)) for _, _, spot, _ in one) for one in plan)
    anywhere = pl.BlockSpec(memory_space=pl.ANY)
    bins, part = parts[0].shape[1:]
    return pl.pallas_call(
        functools.partial(assemble_body, plan=plan, count=len(parts), filled=len(filled) // 2),
        in_specs=[pl.BlockSpec(memory_space=pltpu.VMEM)] * len(parts) + [anywhere] * len(filled),
        out_specs=[anywhere] * 2,
        out_shape=[jax.ShapeDtypeStruct((1,) + shape, jnp.float32)] * 2,
        scratch_shapes=[pltpu.VMEM((steps, bins, part), jnp.float32), pltpu.SemaphoreType.DMA((steps,))],
        input_output_aliases={len(parts) + i: i for i in range(len(filled))},
        compiler_params=pltpu.CompilerParams(vmem_limit_bytes=VMEM),
        cost_estimate=pl.CostEstimate(flops=steps * bins * part, bytes_accessed=6 * steps * bins * part, transcendentals=0),
    )(*parts, *filled)


HERE = (0, 0, 0, 0)
OUTWARD = (-1, -1, 1, 1)
INWARD = (1, 1, -1, -1)
INNER_INWARD = (None, 1, -1, None)
INNER_OUTWARD = (None, -1, 1, None)


def send(value, flip, step):
    peers = lax.axis_size("chan")
    pairs = []
    for i in range(peers):
        planes = step[i % PLANE]
        if planes is not None and 0 <= i + PLANE * planes < peers:
            pairs.append((i, (i ^ flip) + PLANE * planes))
    return lax.ppermute(value, "chan", pairs)


def after(value, *done):
    return lax.optimization_barrier((value,) + done)[0]


def local(traces, mask, counts):
    record = traces[0]
    windows, lags, width = record.shape
    causal, tables = lag_tables(lags)
    tables = jnp.asarray(tables)
    t0, t1, t2, t3 = whiten(mask, jnp.asarray(np.ascontiguousarray(causal.T)), record)

    y2, y3 = send(t2, 2, HERE), send(t3, 3, HERE)
    z0 = send(t0, 0, OUTWARD)
    ea, eb = send(t0, 0, INNER_INWARD), send(t1, 1, INNER_INWARD)
    t1 = after(t1, z0)
    z1, u1 = send(t1, 1, OUTWARD), send(t1, 1, HERE)
    r2, r3 = send(after(y2, ea, eb), 0, INWARD), send(y3, 0, INWARD)

    parts = correlate(
        counts, tables, (t0, u1, y2, y3, z0, z1, eb, ea, r2), ((None, BASE), (0, INNER), (1, OUTER)),
        slots={0: 0, 1: 1, 2: 2, 3: 3, 4: 4, 5: 5, -3: 6, -2: 7, -1: 7},
        loads=((0, 1), (1, 0), (2, 3), (3, 2), (4, 5), (5, 4), (6, None), (None, 6), (7, 7)))
    keep, f, x, v, w, sib = correlate(
        counts, tables, (t0, u1, y2, y3, z0, r3), ((0, OUTER), (1, INNER)),
        slots={0: 0, 1: 1, 2: 2, 3: 3, 4: 4, -2: 5, -1: 5},
        loads=((0, 1), (1, 0), (2, 3), (3, 2), (4, None), (5, 5)), filled=parts)

    sib = send(sib, 1, HERE)
    f, x, v, w = merge(sib, (f, x, v, w))
    f, x, v = send(f, 2, HERE), send(x, 0, INWARD), send(v, 2, OUTWARD)
    w = send(w, 0, INNER_OUTWARD)

    shape = (MAXP, lags // 2, width)
    filled = assemble((keep, sib), shape, [[(0, 0, mine, 0), (1, 1, mine, 0)] for mine in range(2)])
    return tuple(assemble((f, x, v, w), shape, [
        [(0, 2, 3 - mine, 0), (0, 3, 3 - mine, SIZES[1]), (1, 0, 4 + mine, 0), (1, 1, 4 + mine, SIZES[2]),
         (2, 2, -1 - mine, 0), (2, 3, -1 - mine, SIZES[3])] + inner
        for mine, inner in enumerate(([], [(3, 0, -3, 0), (3, 1, -3, 1)]))], filled))


def solution(mesh):
    return jax.shard_map(
        local,
        mesh=mesh,
        in_specs=(P(("grp", "chan"), None, None, None), P("grp", None), P("grp")),
        out_specs=(P(("grp", "chan"), None, None, None), P(("grp", "chan"), None, None, None)),
        check_vma=False,
    )
```

time: 478 us -> 116 us (0.24)
  waiting for transfers between devices: 401 us -> 58.2 us
  Pallas kernels: 0 us -> 30.1 us
  other arithmetic: 26.2 us -> 0 us
  local copies, waits for them, and re-layouts: 11.6 us -> 1.63 us
  matrix products: 4.85 us -> 0 us
    ppermute x10 -> x14, waiting for transfers between devices: 401 us -> 58.2 us  [send(): return lax.ppermute(value, 'chan', pairs)]
    pallas_call x0 -> x6, Pallas kernels: none -> 30.1 us  [the longest x2 17.4 us: correlate(): pl.pallas_call(functools.partial(correlate_body, work=work, slots=slots,...]
    reduce_sum x5 -> x0, other arithmetic: 22.3 us -> none  [stack_pair(): jnp.sum(scaled * (first_re * second_re + first_im * second_im), axis=0)]
    unnamed x24, local copies, waits for them, and re-layouts: 7.21 us -> 1.63 us
    dot_general x6 -> x0, matrix products: 4.85 us -> none  [the longest x1 3.46 us: whiten(): jnp.einsum('tk,wtc->wkc', table, record, preferred_element_type=jnp.float32)]
    ppermute x10 -> x14, starting transfers between devices: 29.7 us -> 25.1 us  [send(): return lax.ppermute(value, 'chan', pairs)]
  transfers between devices with their start and end apart: 10 -> 14, of which waited for: 6 -> 9; matrix products, arithmetic and copies ran while one was open for 7% -> 0% of each run, Pallas kernels for 0% -> 12%
where the time goes in v2:
time: 116 us
  waiting for transfers between devices  58.2 us (50%)
  Pallas kernels  30.1 us (26%)
  starting transfers between devices  25.1 us (22%)
  local copies, waits for them, and re-layouts  1.63 us (1%)
    ppermute x14, waiting for transfers between devices, send(): return lax.ppermute(value, 'chan', pairs)  58.2 us
    ppermute x14, starting transfers between devices, send(): return lax.ppermute(value, 'chan', pairs)  25.1 us
    pallas_call x2, Pallas kernels, correlate(): pl.pallas_call(functools.partial(correlate_body, work=work, slots=slots,...  17.4 us
    pallas_call x1, Pallas kernels, whiten(): pl.pallas_call(whiten_body, grid=(windows // step,), in_specs=[pl.BlockSp...  5.92 us
    pallas_call x2, Pallas kernels, assemble(): pl.pallas_call(functools.partial(assemble_body, plan=plan, count=len(part...  4.84 us
  transfers between devices with their start and end apart: 14, of which 9 were waited for; matrix products, arithmetic and copies ran while one was open for 0% of the time, Pallas kernels for 12%

profile of v2, /device:TPU:16, one launch (start us, length us, event | category | flops | bytes accessed | tf_op | source)
XLA Modules:
  0.0 115.9 jit_solution(3184140012323447587)
XLA Ops:
  0.6 5.9 %shard_map.68 = (bf16[16,2,128,128]{3,2,1,0:T(8,128)(2,1)}, bf16[16,2,128,128]{3,2,1,0:T(8,128)(2,1)}, bf16[16,2,128,128]{3,2,1,0:T(8,128)(2,1)}, bf16[16,2,128,128]{3,2,1,0:T(8,128)(2,1)}) custom-call(s32[16,16]{1,0:T(8,128)} %mask_ref.1, bf16[256,256]{1,0:T(8,128)(2,1)} %constant.5.clone.table_ref, bf16[16,256,512]{2,1,0:T(8,128)(2,1)} %bitcast.1), custom_call_target="tpu_custom_call" | custom-call | flops 1073741824 | bytes 8388608 | tf_op jit(solution)/shard_map/pallas_call | solution.py:102
  6.6 0.7 collective-permute-start.7
  7.3 3.2 %collective-permute-start.2 = (bf16[16,2,128,128]{3,2,1,0:T(8,128)(2,1)}, bf16[16,2,128,128]{3,2,1,0:T(8,128)(2,1)S(1)}, u32[]{:S(2)}, u32[]{:S(2)}) collective-permute-start(bf16[16,2,128,128]{3,2,1,0:T(8,128)(2,1)} %get-tuple-element.29), channel_id=1, source_target_pairs={{0,2},{1,3},{2,0},{3,1},{4,6},{5,7},{6,4},{7,5},{8,10},{9,11},{10,... | collective-permute-start | bytes 3145736 | tf_op jit(solution)/shard_map/ppermute | solution.py:327
  10.5 1.3 %collective-permute-start.6 = (bf16[16,2,128,128]{3,2,1,0:T(8,128)(2,1)}, bf16[16,2,128,128]{3,2,1,0:T(8,128)(2,1)S(1)}, u32[]{:S(2)}, u32[]{:S(2)}) collective-permute-start(bf16[16,2,128,128]{3,2,1,0:T(8,128)(2,1)} %get-tuple-element.28), channel_id=1, source_target_pairs={{1,4},{5,8},{6,3},{9,12},{10,7},{14,11},{17,20},{21,24},{22,19},{2... | collective-permute-start | bytes 3145736 | tf_op jit(solution)/shard_map/ppermute | solution.py:327
  11.8 2.4 %collective-permute-start = (bf16[16,2,128,128]{3,2,1,0:T(8,128)(2,1)}, bf16[16,2,128,128]{3,2,1,0:T(8,128)(2,1)S(1)}, u32[]{:S(2)}, u32[]{:S(2)}) collective-permute-start(bf16[16,2,128,128]{3,2,1,0:T(8,128)(2,1)} %get-tuple-element.26.refs_0_), channel_id=1, source_target_pairs={{2,6},{3,7},{4,0},{5,1},{6,10},{7,11},{8,4},{9,5},{10,14},{11,15},... | collective-permute-start | bytes 3145736 | tf_op jit(solution)/shard_map/ppermute | solution.py:327
  14.2 0.1 collective-permute-start.3
  14.3 0.0 collective-permute-done.7.refs_7_
  14.3 0.0 copy-start.5
  14.3 20.2 %collective-permute-done.2.refs_2_ = bf16[16,2,128,128]{3,2,1,0:T(8,128)(2,1)S(1)} collective-permute-done((bf16[16,2,128,128]{3,2,1,0:T(8,128)(2,1)}, bf16[16,2,128,128]{3,2,1,0:T(8,128)(2,1)S(1)}, u32[]{:S(2)}, u32[]{:S(2)}) %collective-permute-start.2) | collective-permute-done | bytes 1048608 | tf_op jit(solution)/shard_map/ppermute | solution.py:327
  34.5 0.0 copy-start
  34.5 0.0 collective-permute-done.6.refs_6_
  34.5 0.0 copy-start.6
  34.5 3.8 %collective-permute-start.8 = (bf16[16,2,128,128]{3,2,1,0:T(8,128)(2,1)S(1)}, bf16[16,2,128,128]{3,2,1,0:T(8,128)(2,1)S(1)}, u32[]{:S(2)}, u32[]{:S(2)}) collective-permute-start(bf16[16,2,128,128]{3,2,1,0:T(8,128)(2,1)S(1)} %collective-permute-done.2.refs_2_), channel_id=1, source_target_pairs={{0,4},{1,5},{4,8},{5,9},{6,2},{7,3},{8,12},{9,13},{10,6},{11,7},{1... | collective-permute-start | bytes 3145736 | tf_op jit(solution)/shard_map/ppermute | solution.py:327
  38.3 0.1 collective-permute-done.refs_4_
  38.4 0.0 copy-start.1
  38.4 1.6 %collective-permute-start.1 = (bf16[16,2,128,128]{3,2,1,0:T(8,128)(2,1)}, bf16[16,2,128,128]{3,2,1,0:T(8,128)(2,1)S(1)}, u32[]{:S(2)}, u32[]{:S(2)}) collective-permute-start(bf16[16,2,128,128]{3,2,1,0:T(8,128)(2,1)} %get-tuple-element.28), channel_id=1, source_target_pairs={{0,1},{1,0},{2,3},{3,2},{4,5},{5,4},{6,7},{7,6},{8,9},{9,8},{10,11... | collective-permute-start | bytes 3145736 | tf_op jit(solution)/shard_map/ppermute | solution.py:327
  40.0 2.0 %collective-permute-start.5 = (bf16[16,2,128,128]{3,2,1,0:T(8,128)(2,1)}, bf16[16,2,128,128]{3,2,1,0:T(8,128)(2,1)}, u32[]{:S(2)}, u32[]{:S(2)}) collective-permute-start(bf16[16,2,128,128]{3,2,1,0:T(8,128)(2,1)} %get-tuple-element.28), channel_id=1, source_target_pairs={{2,7},{3,6},{4,1},{5,0},{6,11},{7,10},{8,5},{9,4},{10,15},{11,14},... | collective-permute-start | bytes 3145736 | tf_op jit(solution)/shard_map/ppermute | solution.py:327
  42.0 15.2 %collective-permute-done.3.refs_3_ = bf16[16,2,128,128]{3,2,1,0:T(8,128)(2,1)S(1)} collective-permute-done((bf16[16,2,128,128]{3,2,1,0:T(8,128)(2,1)}, bf16[16,2,128,128]{3,2,1,0:T(8,128)(2,1)S(1)}, u32[]{:S(2)}, u32[]{:S(2)}) %collective-permute-start.3) | collective-permute-done | bytes 1048608 | tf_op jit(solution)/shard_map/ppermute | solution.py:327
  57.2 0.0 copy-start.2
  57.2 1.9 %collective-permute-start.4 = (bf16[16,2,128,128]{3,2,1,0:T(8,128)(2,1)S(1)}, bf16[16,2,128,128]{3,2,1,0:T(8,128)(2,1)}, u32[]{:S(2)}, u32[]{:S(2)}) collective-permute-start(bf16[16,2,128,128]{3,2,1,0:T(8,128)(2,1)S(1)} %collective-permute-done.3.refs_3_), channel_id=1, source_target_pairs={{0,4},{1,5},{4,8},{5,9},{6,2},{7,3},{8,12},{9,13},{10,6},{11,7},{1... | collective-permute-start | bytes 3145736 | tf_op jit(solution)/shard_map/ppermute | solution.py:327
  59.1 3.2 %collective-permute-done.8.refs_8_ = bf16[16,2,128,128]{3,2,1,0:T(8,128)(2,1)S(1)} collective-permute-done((bf16[16,2,128,128]{3,2,1,0:T(8,128)(2,1)S(1)}, bf16[16,2,128,128]{3,2,1,0:T(8,128)(2,1)S(1)}, u32[]{:S(2)}, u32[]{:S(2)}) %collective-permute-start.8) | collective-permute-done | bytes 1048608 | tf_op jit(solution)/shard_map/ppermute | solution.py:327
  62.3 0.0 copy-start.7
  62.3 0.0 collective-permute-done.1.refs_1_
  62.3 0.0 copy-start.3
  62.3 5.2 %collective-permute-done.5.refs_5_ = bf16[16,2,128,128]{3,2,1,0:T(8,128)(2,1)} collective-permute-done((bf16[16,2,128,128]{3,2,1,0:T(8,128)(2,1)}, bf16[16,2,128,128]{3,2,1,0:T(8,128)(2,1)}, u32[]{:S(2)}, u32[]{:S(2)}) %collective-permute-start.5) | collective-permute-done | bytes 1048608 | tf_op jit(solution)/shard_map/ppermute | solution.py:327
  67.5 0.0 copy-done.5
  67.5 0.0 copy-done
  67.5 0.0 copy-done.6
  67.5 0.0 copy-done.1
  67.5 0.0 copy-done.2
  67.6 0.0 copy-done.7
  67.6 0.0 copy-done.3
  67.6 11.7 %shard_map.69 = (bf16[7,128,128]{2,1,0:T(8,128)(2,1)}, bf16[12,128,128]{2,1,0:T(8,128)(2,1)}, bf16[6,128,128]{2,1,0:T(8,128)(2,1)}, bf16[8,128,128]{2,1,0:T(8,12...) custom-call(s32[16]{0:T(128)} %counts_ref.3, bf16[2,256,256]{2,1,0:T(8,128)(2,1)} %constant.4.clone.table_ref, ...), custom_call_target="tpu_custom_call" | custom-call | flops 419430400 | bytes 9437184 | tf_op jit(solution)/shard_map/pallas_call | solution.py:231
  79.3 5.3 %collective-permute-done.4.refs_5_ = bf16[16,2,128,128]{3,2,1,0:T(8,128)(2,1)} collective-permute-done((bf16[16,2,128,128]{3,2,1,0:T(8,128)(2,1)S(1)}, bf16[16,2,128,128]{3,2,1,0:T(8,128)(2,1)}, u32[]{:S(2)}, u32[]{:S(2)}) %collective-permute-start.4) | collective-permute-done | bytes 1048608 | tf_op jit(solution)/shard_map/ppermute | solution.py:327
  84.6 5.7 %shard_map.70 = (bf16[7,128,128]{2,1,0:T(8,128)(2,1)}, bf16[12,128,128]{2,1,0:T(8,128)(2,1)}, bf16[6,128,128]{2,1,0:T(8,128)(2,1)}, bf16[8,128,128]{2,1,0:T(8,12...) custom-call(s32[16]{0:T(128)} %counts_ref.3, ...), custom_call_target="tpu_custom_call", output_to_operand_aliasing={{0}: (8, {}), {1}: (9, {}), {2}: (10, {}), {3}: (11, {}), {... | custom-call | flops 104857600 | bytes 6291456 | tf_op jit(solution)/shard_map/pallas_call | solution.py:231
  90.3 0.1 collective-permute-start.9
  90.4 2.3 %collective-permute-done.9.sib.refs_1_ = bf16[21,128,128]{2,1,0:T(8,128)(2,1)S(1)} collective-permute-done((bf16[21,128,128]{2,1,0:T(8,128)(2,1)}, bf16[21,128,128]{2,1,0:T(8,128)(2,1)S(1)}, u32[]{:S(2)}, u32[]{:S(2)}) %collective-permute-start.9) | collective-permute-done | bytes 688160 | tf_op jit(solution)/shard_map/ppermute | solution.py:327
  92.7 0.0 copy-start.4
  92.7 0.8 copy-done.4
  93.6 1.9 %shard_map.71 = (bf16[12,128,128]{2,1,0:T(8,128)(2,1)}, bf16[6,128,128]{2,1,0:T(8,128)(2,1)}, bf16[8,128,128]{2,1,0:T(8,128)(2,1)}, bf16[2,128,128]{2,1,0:T(8,128)(2,1)}) custom-call(bf16[21,128,128]{2,1,0:T(8,128)(2,1)} %copy-done.4, ...), custom_call_target="tpu_custom_call", output_to_operand_aliasing={{0}: (1, {}), {1}: (2, {}), {2}: (3, {}), {3}: (4, {})} | custom-call | tf_op jit(solution)/shard_map/pallas_call | solution.py:263
  95.5 1.0 collective-permute-start.10
  96.5 2.8 %collective-permute-start.12 = (bf16[8,128,128]{2,1,0:T(8,128)(2,1)}, bf16[8,128,128]{2,1,0:T(8,128)(2,1)S(1)}, u32[]{:S(2)}, u32[]{:S(2)}) collective-permute-start(bf16[8,128,128]{2,1,0:T(8,128)(2,1)} %get-tuple-element.45), channel_id=1, source_target_pairs={{2,4},{3,5},{4,2},{5,3},{6,8},{7,9},{8,6},{9,7},{10,12},{11,13},{1... | collective-permute-start | bytes 786440 | tf_op jit(solution)/shard_map/ppermute | solution.py:327
  99.4 3.5 %collective-permute-start.11 = (bf16[6,128,128]{2,1,0:T(8,128)(2,1)}, bf16[6,128,128]{2,1,0:T(8,128)(2,1)S(1)}, u32[]{:S(2)}, u32[]{:S(2)}) collective-permute-start(bf16[6,128,128]{2,1,0:T(8,128)(2,1)} %get-tuple-element.44), channel_id=1, source_target_pairs={{0,4},{1,5},{4,8},{5,9},{6,2},{7,3},{8,12},{9,13},{10,6},{11,7},{1... | collective-permute-start | bytes 589832 | tf_op jit(solution)/shard_map/ppermute | solution.py:327
  102.8 0.7 collective-permute-start.13
  103.5 2.3 %shard_map.72 = (f32[1,5,128,512]{3,2,1,0:T(8,128)}, f32[1,5,128,512]{3,2,1,0:T(8,128)}) custom-call(bf16[7,128,128]{2,1,0:T(8,128)(2,1)} %get-tuple-element.47.refs_0_, bf16[21,128,128]{2,1,0:T(8,128)(2,1)} %copy-done.4), custom_call_target="tpu_custom_call" | custom-call | flops 229376 | bytes 1376256 | tf_op jit(solution)/shard_map/pallas_call | solution.py:301
  105.8 0.0 collective-permute-done.13.refs_3_
  105.8 0.0 copy-start.11
  105.8 2.0 %collective-permute-done.11.refs_1_ = bf16[6,128,128]{2,1,0:T(8,128)(2,1)S(1)} collective-permute-done((bf16[6,128,128]{2,1,0:T(8,128)(2,1)}, bf16[6,128,128]{2,1,0:T(8,128)(2,1)S(1)}, u32[]{:S(2)}, u32[]{:S(2)}) %collective-permute-start.11) | collective-permute-done | bytes 196640 | tf_op jit(solution)/shard_map/ppermute | solution.py:327
  107.8 0.0 copy-start.10
  107.8 0.0 collective-permute-done.12.refs_2_
  107.8 0.0 copy-start.9
  107.8 4.7 %collective-permute-done.10.refs_0_ = bf16[12,128,128]{2,1,0:T(8,128)(2,1)S(1)} collective-permute-done((bf16[12,128,128]{2,1,0:T(8,128)(2,1)}, bf16[12,128,128]{2,1,0:T(8,128)(2,1)S(1)}, u32[]{:S(2)}, u32[]{:S(2)}) %collective-permute-start.10) | collective-permute-done | bytes 393248 | tf_op jit(solution)/shard_map/ppermute | solution.py:327
  112.5 0.0 copy-start.8
  112.5 0.0 copy-done.11
  112.5 0.0 copy-done.10
  112.5 0.0 copy-done.9
  112.5 0.7 copy-done.8
  113.3 2.6 %shard_map.73 = (f32[1,5,128,512]{3,2,1,0:T(8,128)}, f32[1,5,128,512]{3,2,1,0:T(8,128)}) custom-call(bf16[12,128,128]{2,1,0:T(8,128)(2,1)} %copy-done.8, bf16[6,128,128]{2,1,0:T(8,128)(2,1)} %copy-done.10, bf16[8,128,128]{2,1,0:T(8,128)(2,1)} %copy-done.9, bf16[2,128,128]{2,1,0:T(8,128)(2,1)} %copy-done.11, ...), custom_call_target="tpu_custom_call", output_to_operand_aliasing={{0}: (4, {}), {1}: (5, {})} | custom-call | flops 458752 | bytes 2752512 | tf_op jit(solution)/shard_map/pallas_call | solution.py:301
Async XLA Ops:
  6.6 7.7 %collective-permute-start.7 = (bf16[16,2,128,128]{3,2,1,0:T(8,128)(2,1)}, bf16[16,2,128,128]{3,2,1,0:T(8,128)(2,1)S(1)}, u32[]{:S(2)}, u32[]{:S(2)}) collective-permute-start(bf16[16,2,128,128]{3,2,1,0:T(8,128)(2,1)} %get-tuple-element.26.refs_0_), channel_id=1, source_target_pairs={{1,5},{5,9},{6,2},{9,13},{10,6},{14,10},{17,21},{21,25},{22,18},{2... | collective-permute-start | bytes 3145736 | tf_op jit(solution)/shard_map/ppermute | solution.py:327
  7.3 27.2 %collective-permute-start.2 = (bf16[16,2,128,128]{3,2,1,0:T(8,128)(2,1)}, bf16[16,2,128,128]{3,2,1,0:T(8,128)(2,1)S(1)}, u32[]{:S(2)}, u32[]{:S(2)}) collective-permute-start(bf16[16,2,128,128]{3,2,1,0:T(8,128)(2,1)} %get-tuple-element.29), channel_id=1, source_target_pairs={{0,2},{1,3},{2,0},{3,1},{4,6},{5,7},{6,4},{7,5},{8,10},{9,11},{10,... | collective-permute-start | bytes 3145736 | tf_op jit(solution)/shard_map/ppermute | solution.py:327
  10.5 24.0 %collective-permute-start.6 = (bf16[16,2,128,128]{3,2,1,0:T(8,128)(2,1)}, bf16[16,2,128,128]{3,2,1,0:T(8,128)(2,1)S(1)}, u32[]{:S(2)}, u32[]{:S(2)}) collective-permute-start(bf16[16,2,128,128]{3,2,1,0:T(8,128)(2,1)} %get-tuple-element.28), channel_id=1, source_target_pairs={{1,4},{5,8},{6,3},{9,12},{10,7},{14,11},{17,20},{21,24},{22,19},{2... | collective-permute-start | bytes 3145736 | tf_op jit(solution)/shard_map/ppermute | solution.py:327
  11.8 26.6 %collective-permute-start = (bf16[16,2,128,128]{3,2,1,0:T(8,128)(2,1)}, bf16[16,2,128,128]{3,2,1,0:T(8,128)(2,1)S(1)}, u32[]{:S(2)}, u32[]{:S(2)}) collective-permute-start(bf16[16,2,128,128]{3,2,1,0:T(8,128)(2,1)} %get-tuple-element.26.refs_0_), channel_id=1, source_target_pairs={{2,6},{3,7},{4,0},{5,1},{6,10},{7,11},{8,4},{9,5},{10,14},{11,15},... | collective-permute-start | bytes 3145736 | tf_op jit(solution)/shard_map/ppermute | solution.py:327
  14.2 43.0 %collective-permute-start.3 = (bf16[16,2,128,128]{3,2,1,0:T(8,128)(2,1)}, bf16[16,2,128,128]{3,2,1,0:T(8,128)(2,1)S(1)}, u32[]{:S(2)}, u32[]{:S(2)}) collective-permute-start(bf16[16,2,128,128]{3,2,1,0:T(8,128)(2,1)} %get-tuple-element.30), channel_id=1, source_target_pairs={{0,3},{1,2},{2,1},{3,0},{4,7},{5,6},{6,5},{7,4},{8,11},{9,10},{10,... | collective-permute-start | bytes 3145736 | tf_op jit(solution)/shard_map/ppermute | solution.py:327
  14.3 53.2 %copy-start.5 = (bf16[16,2,128,128]{3,2,1,0:T(8,128)(2,1)}, bf16[16,2,128,128]{3,2,1,0:T(8,128)(2,1)S(1)}, u32[]{:S(2)}) copy-start(bf16[16,2,128,128]{3,2,1,0:T(8,128)(2,1)S(1)} %collective-permute-done.7.refs_7_) | copy-start | bytes 3145732
  34.5 33.0 %copy-start = (bf16[16,2,128,128]{3,2,1,0:T(8,128)(2,1)}, bf16[16,2,128,128]{3,2,1,0:T(8,128)(2,1)S(1)}, u32[]{:S(2)}) copy-start(bf16[16,2,128,128]{3,2,1,0:T(8,128)(2,1)S(1)} %collective-permute-done.2.refs_2_) | copy-start | bytes 3145732
  34.5 33.0 %copy-start.6 = (bf16[16,2,128,128]{3,2,1,0:T(8,128)(2,1)}, bf16[16,2,128,128]{3,2,1,0:T(8,128)(2,1)S(1)}, u32[]{:S(2)}) copy-start(bf16[16,2,128,128]{3,2,1,0:T(8,128)(2,1)S(1)} %collective-permute-done.6.refs_6_) | copy-start | bytes 3145732
  34.5 27.8 %collective-permute-start.8 = (bf16[16,2,128,128]{3,2,1,0:T(8,128)(2,1)S(1)}, bf16[16,2,128,128]{3,2,1,0:T(8,128)(2,1)S(1)}, u32[]{:S(2)}, u32[]{:S(2)}) collective-permute-start(bf16[16,2,128,128]{3,2,1,0:T(8,128)(2,1)S(1)} %collective-permute-done.2.refs_2_), channel_id=1, source_target_pairs={{0,4},{1,5},{4,8},{5,9},{6,2},{7,3},{8,12},{9,13},{10,6},{11,7},{1... | collective-permute-start | bytes 3145736 | tf_op jit(solution)/shard_map/ppermute | solution.py:327
  38.4 29.1 %copy-start.1 = (bf16[16,2,128,128]{3,2,1,0:T(8,128)(2,1)}, bf16[16,2,128,128]{3,2,1,0:T(8,128)(2,1)S(1)}, u32[]{:S(2)}) copy-start(bf16[16,2,128,128]{3,2,1,0:T(8,128)(2,1)S(1)} %collective-permute-done.refs_4_) | copy-start | bytes 3145732
  38.4 23.9 %collective-permute-start.1 = (bf16[16,2,128,128]{3,2,1,0:T(8,128)(2,1)}, bf16[16,2,128,128]{3,2,1,0:T(8,128)(2,1)S(1)}, u32[]{:S(2)}, u32[]{:S(2)}) collective-permute-start(bf16[16,2,128,128]{3,2,1,0:T(8,128)(2,1)} %get-tuple-element.28), channel_id=1, source_target_pairs={{0,1},{1,0},{2,3},{3,2},{4,5},{5,4},{6,7},{7,6},{8,9},{9,8},{10,11... | collective-permute-start | bytes 3145736 | tf_op jit(solution)/shard_map/ppermute | solution.py:327
  40.0 27.5 %collective-permute-start.5 = (bf16[16,2,128,128]{3,2,1,0:T(8,128)(2,1)}, bf16[16,2,128,128]{3,2,1,0:T(8,128)(2,1)}, u32[]{:S(2)}, u32[]{:S(2)}) collective-permute-start(bf16[16,2,128,128]{3,2,1,0:T(8,128)(2,1)} %get-tuple-element.28), channel_id=1, source_target_pairs={{2,7},{3,6},{4,1},{5,0},{6,11},{7,10},{8,5},{9,4},{10,15},{11,14},... | collective-permute-start | bytes 3145736 | tf_op jit(solution)/shard_map/ppermute | solution.py:327
  57.2 10.3 %copy-start.2 = (bf16[16,2,128,128]{3,2,1,0:T(8,128)(2,1)}, bf16[16,2,128,128]{3,2,1,0:T(8,128)(2,1)S(1)}, u32[]{:S(2)}) copy-start(bf16[16,2,128,128]{3,2,1,0:T(8,128)(2,1)S(1)} %collective-permute-done.3.refs_3_) | copy-start | bytes 3145732
  57.2 27.4 %collective-permute-start.4 = (bf16[16,2,128,128]{3,2,1,0:T(8,128)(2,1)S(1)}, bf16[16,2,128,128]{3,2,1,0:T(8,128)(2,1)}, u32[]{:S(2)}, u32[]{:S(2)}) collective-permute-start(bf16[16,2,128,128]{3,2,1,0:T(8,128)(2,1)S(1)} %collective-permute-done.3.refs_3_), channel_id=1, source_target_pairs={{0,4},{1,5},{4,8},{5,9},{6,2},{7,3},{8,12},{9,13},{10,6},{11,7},{1... | collective-permute-start | bytes 3145736 | tf_op jit(solution)/shard_map/ppermute | solution.py:327
  62.3 5.3 %copy-start.7 = (bf16[16,2,128,128]{3,2,1,0:T(8,128)(2,1)}, bf16[16,2,128,128]{3,2,1,0:T(8,128)(2,1)S(1)}, u32[]{:S(2)}) copy-start(bf16[16,2,128,128]{3,2,1,0:T(8,128)(2,1)S(1)} %collective-permute-done.8.refs_8_) | copy-start | bytes 3145732
  62.3 5.3 %copy-start.3 = (bf16[16,2,128,128]{3,2,1,0:T(8,128)(2,1)}, bf16[16,2,128,128]{3,2,1,0:T(8,128)(2,1)S(1)}, u32[]{:S(2)}) copy-start(bf16[16,2,128,128]{3,2,1,0:T(8,128)(2,1)S(1)} %collective-permute-done.1.refs_1_) | copy-start | bytes 3145732
  90.3 2.4 %collective-permute-start.9 = (bf16[21,128,128]{2,1,0:T(8,128)(2,1)}, bf16[21,128,128]{2,1,0:T(8,128)(2,1)S(1)}, u32[]{:S(2)}, u32[]{:S(2)}) collective-permute-start(bf16[21,128,128]{2,1,0:T(8,128)(2,1)} %get-tuple-element.38), channel_id=1, source_target_pairs={{0,1},{1,0},{2,3},{3,2},{4,5},{5,4},{6,7},{7,6},{8,9},{9,8},{10,11... | collective-permute-start | bytes 2064392 | tf_op jit(solution)/shard_map/ppermute | solution.py:327
  92.7 0.8 copy-start.4
  95.5 17.1 %collective-permute-start.10 = (bf16[12,128,128]{2,1,0:T(8,128)(2,1)}, bf16[12,128,128]{2,1,0:T(8,128)(2,1)S(1)}, u32[]{:S(2)}, u32[]{:S(2)}) collective-permute-start(bf16[12,128,128]{2,1,0:T(8,128)(2,1)} %get-tuple-element.43), channel_id=1, source_target_pairs={{0,2},{1,3},{2,0},{3,1},{4,6},{5,7},{6,4},{7,5},{8,10},{9,11},{10,... | collective-permute-start | bytes 1179656 | tf_op jit(solution)/shard_map/ppermute | solution.py:327
  96.5 11.3 %collective-permute-start.12 = (bf16[8,128,128]{2,1,0:T(8,128)(2,1)}, bf16[8,128,128]{2,1,0:T(8,128)(2,1)S(1)}, u32[]{:S(2)}, u32[]{:S(2)}) collective-permute-start(bf16[8,128,128]{2,1,0:T(8,128)(2,1)} %get-tuple-element.45), channel_id=1, source_target_pairs={{2,4},{3,5},{4,2},{5,3},{6,8},{7,9},{8,6},{9,7},{10,12},{11,13},{1... | collective-permute-start | bytes 786440 | tf_op jit(solution)/shard_map/ppermute | solution.py:327
  99.4 8.5 %collective-permute-start.11 = (bf16[6,128,128]{2,1,0:T(8,128)(2,1)}, bf16[6,128,128]{2,1,0:T(8,128)(2,1)S(1)}, u32[]{:S(2)}, u32[]{:S(2)}) collective-permute-start(bf16[6,128,128]{2,1,0:T(8,128)(2,1)} %get-tuple-element.44), channel_id=1, source_target_pairs={{0,4},{1,5},{4,8},{5,9},{6,2},{7,3},{8,12},{9,13},{10,6},{11,7},{1... | collective-permute-start | bytes 589832 | tf_op jit(solution)/shard_map/ppermute | solution.py:327
  102.8 2.9 %collective-permute-start.13 = (bf16[2,128,128]{2,1,0:T(8,128)(2,1)}, bf16[2,128,128]{2,1,0:T(8,128)(2,1)S(1)}, u32[]{:S(2)}, u32[]{:S(2)}) collective-permute-start(bf16[2,128,128]{2,1,0:T(8,128)(2,1)} %get-tuple-element.46), channel_id=1, source_target_pairs={{2,6},{5,1},{6,10},{9,5},{10,14},{13,9},{18,22},{21,17},{22,26},{2... | collective-permute-start | bytes 196616 | tf_op jit(solution)/shard_map/ppermute | solution.py:327
  105.8 6.7 %copy-start.11 = (bf16[2,128,128]{2,1,0:T(8,128)(2,1)}, bf16[2,128,128]{2,1,0:T(8,128)(2,1)S(1)}, u32[]{:S(2)}) copy-start(bf16[2,128,128]{2,1,0:T(8,128)(2,1)S(1)} %collective-permute-done.13.refs_3_) | copy-start | bytes 196612
  107.8 4.7 %copy-start.10 = (bf16[6,128,128]{2,1,0:T(8,128)(2,1)}, bf16[6,128,128]{2,1,0:T(8,128)(2,1)S(1)}, u32[]{:S(2)}) copy-start(bf16[6,128,128]{2,1,0:T(8,128)(2,1)S(1)} %collective-permute-done.11.refs_1_) | copy-start | bytes 589828
  107.8 4.7 %copy-start.9 = (bf16[8,128,128]{2,1,0:T(8,128)(2,1)}, bf16[8,128,128]{2,1,0:T(8,128)(2,1)S(1)}, u32[]{:S(2)}) copy-start(bf16[8,128,128]{2,1,0:T(8,128)(2,1)S(1)} %collective-permute-done.12.refs_2_) | copy-start | bytes 786436
  112.5 0.8 copy-start.8

commit v3 on v2

v3 whole, which is shorter than its diff:
```python
import functools
import math

import jax
import jax.numpy as jnp
import numpy as np
from jax import lax
from jax.experimental import pallas as pl
from jax.experimental.pallas import tpu as pltpu
from jax.sharding import PartitionSpec as P

MAXP = 5
PLANE = 4
MIB = 1024 * 1024
ROWS = 16
STEP = 8

NEAR = (((0, 1), (0, 2), (1, 2)), ((0, 1), (0, 3), (1, 3)))
REST = (((0, 3), (1, 3), (2, 3)), ((0, 2), (1, 2), (2, 3)))
FIRST = ((-3, 2),)
BEYOND = ((0, 4), (0, 5), (1, 4), (1, 5), (3, 5))
OUTER = ((-1, 0), (-1, 2), (-1, 3), (-1, 4))
INNER = ((-2, 0), (-2, 1), (-2, 2), (-2, 3))
PAIRS = NEAR[0] + REST[0] + FIRST + BEYOND + OUTER + INNER
DESTS = ((0, 1), (2, 3), (4, 5), (-2, -1), (None, -3))


def flat(groups):
    return [pair for group in groups for pair in group]


def items(spot):
    ahead = sorted(("ahead", b - a - 1) for a, b in PAIRS if a == spot)
    back = sorted(("back", b - a - 1) for a, b in PAIRS if b == spot)
    return ahead + back


SIZES = [max(len(items(spot)) for spot in spots) for spots in DESTS]
STARTS = [sum(SIZES[:d]) for d in range(len(SIZES))]
PLACE = {spot: (d, i) for d, spots in enumerate(DESTS) for i, spot in enumerate(spots)}


def lag_tables(lags):
    bins = lags // 2
    phase = (np.arange(lags)[:, None] * np.arange(1, bins + 1)[None, :] % lags) * (2.0 * math.pi / lags)
    real, imag = np.cos(phase), -np.sin(phase)
    causal = np.concatenate([real, imag], axis=1)
    other = np.concatenate([real, -imag], axis=1)
    near = np.concatenate([causal[:bins], causal[bins:][::-1]], axis=0)
    far = np.concatenate([other[bins:][::-1], other[:bins]], axis=0)
    return causal.astype(jnp.bfloat16), np.stack([near, far]).astype(jnp.bfloat16)


def whereabouts():
    me = lax.axis_index("chan").astype(jnp.int32)
    q = lax.rem(me, PLANE)
    far = q // 2
    return far, lax.rem(q, 2) ^ far, me - q, q


def whiten_body(mask_ref, table_ref, traces_ref, *refs):
    outs, (white, sems) = refs[:-2], refs[-2:]
    _, _, base, q = whereabouts()
    windows = white.shape[1]
    bins = table_ref.shape[0] // 2
    part = white.shape[-1]
    step = traces_ref.shape[1]
    at = pl.program_id(0)
    for n in range(step):
        w = at * step + n
        raw = jnp.dot(table_ref[...], traces_ref[0, n], preferred_element_type=jnp.float32)
        power = jnp.sum(raw * raw, axis=0, keepdims=True) / bins
        valid = mask_ref[base + q, w].astype(jnp.float32)
        scaled = (raw * (valid * lax.rsqrt(power + 1e-06))).astype(jnp.bfloat16)
        for quarter in range(2):
            piece = scaled[:, quarter * part:(quarter + 1) * part]
            white[quarter ^ lax.rem(q, 2), w, 0] = piece[:bins]
            white[quarter ^ lax.rem(q, 2), w, 1] = piece[bins:]

    def copies(i):
        span = pl.ds(i * step, step)
        targets = (outs[0].at[span], outs[0].at[pl.ds(windows + i * step, step)]) if len(outs) == 1 else [out.at[span] for out in outs]
        return [pltpu.make_async_copy(white.at[k, span], target, sems.at[k, i]) for k, target in enumerate(targets)]

    for one in copies(at):
        one.start()

    @pl.when(at == pl.num_programs(0) - 1)
    def _():
        for i in range(sems.shape[1]):
            for one in copies(i):
                one.wait()


def whiten(mask, table, traces, lengths):
    _, windows, lags, width = traces.shape
    bins = lags // 2
    part = width // PLANE
    other = len(lengths) - 1

    def half(i):
        far = whereabouts()[0]
        return 0, i, 0, 1 - far if other else far

    return pl.pallas_call(
        whiten_body,
        grid=(windows // STEP,),
        in_specs=[
            pl.BlockSpec(memory_space=pltpu.SMEM),
            pl.BlockSpec((lags, lags), lambda i: (0, 0)),
            pl.BlockSpec((1, STEP, lags, 2 * part), half),
        ],
        out_specs=[pl.BlockSpec(memory_space=pl.ANY)] * len(lengths),
        out_shape=[jax.ShapeDtypeStruct((n, 2, bins, part), jnp.bfloat16) for n in lengths],
        scratch_shapes=[
            pltpu.VMEM((2, windows, 2, bins, part), jnp.bfloat16),
            pltpu.SemaphoreType.DMA((2, windows // STEP)),
        ],
        compiler_params=pltpu.CompilerParams(vmem_limit_bytes=57 * MIB),
        cost_estimate=pl.CostEstimate(flops=windows * lags * lags * width, bytes_accessed=2 * windows * lags * width, transcendentals=0),
    )(mask, table, traces)


def relayed(windows):
    return windows * 5 // 8


def correlate_body(counts_ref, table_ref, *refs, work, sources, filled):
    ins, refs = refs[:len(refs) - 2 * len(DESTS) - 3 - filled], refs[len(refs) - 2 * len(DESTS) - 3:]
    outs, stack, kept, out_sems = refs[:len(DESTS) + 1], refs[len(DESTS) + 1], refs[len(DESTS) + 2:-1], refs[-1]
    windows, _, bins, part = ins[1].shape
    far, m, base, _ = whereabouts()
    blocks = counts_ref.shape[0]
    scale = 1.0 / math.sqrt(windows)
    norm = 1.0 / math.sqrt(bins)

    def sum_up(group, at, where):
        need = sorted({spot for pair in group for spot in pair})
        edges = sorted({edge for s in need for _, start, stop in where[s] for edge in (start, stop)})

        def tile(kt, carry):
            top = pl.multiple_of(kt * ROWS, ROWS)
            rows = pl.ds(top, ROWS)
            sums = (jnp.zeros((ROWS, part), jnp.float32),) * (2 * len(group))
            for start, stop in zip(edges, edges[1:]):
                def window(w, sums, start=start):
                    real, imag = {}, {}
                    for s in need:
                        array, begin = [(a, start - first) for a, first, last in where[s] if first <= start < last][0]
                        real[s] = ins[array][begin + w, 0, rows, :].astype(jnp.float32)
                        imag[s] = ins[array][begin + w, 1, rows, :].astype(jnp.float32)
                    out = []
                    for n, (a, b) in enumerate(group):
                        out.append(sums[2 * n] + (real[a] * real[b] + imag[a] * imag[b]))
                        out.append(sums[2 * n + 1] + (imag[a] * real[b] - real[a] * imag[b]))
                    return tuple(out)

                sums = lax.fori_loop(0, stop - start, window, sums, unroll=math.gcd(stop - start, 8))
            for n in range(len(group)):
                lanes = pl.ds((at + n) * part, part)
                stack[rows, lanes] = (sums[2 * n] * scale).astype(jnp.bfloat16)
                stack[pl.ds(pl.multiple_of(bins + top, ROWS), ROWS), lanes] = (sums[2 * n + 1] * scale).astype(jnp.bfloat16)
            return carry

        lax.fori_loop(0, bins // ROWS, tile, 0)

    for mine in range(2):
        @pl.when(m == mine)
        def _(mine=mine):
            copies = []
            for g, group in enumerate(work[mine]):
                at = len(flat(work[mine][:g]))
                sum_up(group, at, sources[mine])
                lags = jnp.dot(table_ref[far], stack[:, at * part:(at + len(group)) * part], preferred_element_type=jnp.float32)
                for n, (a, b) in enumerate(group):
                    first = jnp.where(far == 0, base + a, base + 3 - b)
                    reach = counts_ref[jnp.clip(first, 0, blocks - 1)]
                    corr = lags[:, n * part:(n + 1) * part] * jnp.where(reach >= b - a, norm, 0.0)
                    for spot, kind, rows in ((a, "ahead", corr[:bins]), (b, "back", corr[bins:])):
                        d, i = PLACE[spot]
                        row = items(spot).index((kind, b - a - 1))
                        kept[d][i, row] = rows.astype(jnp.bfloat16)
                        target = outs[d].at[row] if i == mine else outs[-1].at[STARTS[d] + row]
                        one = pltpu.make_async_copy(kept[d].at[i, row], target, out_sems.at[len(copies)])
                        one.start()
                        copies.append(one)
            for one in copies:
                one.wait()


def correlate(counts, tables, whites, work, sources, filled=(), weight=1):
    windows, _, bins, part = whites[1].shape
    most = max(len(flat(groups)) for groups in work)
    anywhere = pl.BlockSpec(memory_space=pl.ANY)
    scalars = pl.BlockSpec(memory_space=pltpu.SMEM)
    lengths = [SIZES[0]] + [2 * size for size in SIZES[1:]] + [sum(SIZES)]
    return pl.pallas_call(
        functools.partial(correlate_body, work=work, sources=sources, filled=len(filled)),
        in_specs=[scalars] + [pl.BlockSpec(memory_space=pltpu.VMEM)] * (1 + len(whites)) + [anywhere] * len(filled),
        out_specs=[anywhere] * len(lengths),
        out_shape=[jax.ShapeDtypeStruct((n, bins, part), jnp.bfloat16) for n in lengths],
        scratch_shapes=[
            pltpu.VMEM((2 * bins, most * part), jnp.bfloat16),
            *[pltpu.VMEM((2, size, bins, part), jnp.bfloat16) for size in SIZES],
            pltpu.SemaphoreType.DMA((2 * most,)),
        ],
        input_output_aliases={2 + len(whites) + i: i for i in range(len(filled))},
        compiler_params=pltpu.CompilerParams(vmem_limit_bytes=12 * MIB),
        cost_estimate=pl.CostEstimate(flops=weight * 100 * most * windows * bins * part, bytes_accessed=min(weight, 1) * 4 * len(whites) * windows * bins * part, transcendentals=0),
    )(counts, tables, *whites, *filled)


def merge_body(sib, *refs):
    outs, sems = refs[len(DESTS) - 1:-1], refs[-1]
    copies = []
    for d in range(1, len(DESTS)):
        copies.append(pltpu.make_async_copy(
            sib.at[pl.ds(STARTS[d], SIZES[d])], outs[d - 1].at[pl.ds(SIZES[d], SIZES[d])], sems.at[d - 1]))
    for one in copies:
        one.start()
    for one in copies:
        one.wait()


def merge(sib, own):
    anywhere = pl.BlockSpec(memory_space=pl.ANY)
    return pl.pallas_call(
        merge_body,
        in_specs=[pl.BlockSpec(memory_space=pltpu.VMEM)] + [anywhere] * len(own),
        out_specs=[anywhere] * len(own),
        out_shape=[jax.ShapeDtypeStruct(value.shape, value.dtype) for value in own],
        scratch_shapes=[pltpu.SemaphoreType.DMA((len(own),))],
        input_output_aliases={1 + i: i for i in range(len(own))},
        compiler_params=pltpu.CompilerParams(vmem_limit_bytes=4 * MIB),
    )(sib, *own)


def assemble_body(*refs, plan, count, filled):
    ins, refs = refs[:count], refs[count + 2 * filled:]
    forward, backward, wide, sems = refs
    far, m, _, q = whereabouts()
    part = ins[0].shape[2]
    for mine in range(2):
        @pl.when(m == mine)
        def _(mine=mine):
            waits = []
            for a, k, spot, first in plan[mine]:
                lanes = pl.ds(pl.multiple_of((q ^ k) * part, part), part)
                ahead = far if k < 2 else 1 - far
                for n, (kind, j) in enumerate(items(spot)):
                    at = len(waits)
                    wide[at] = ins[a][first + n].astype(jnp.float32)
                    side = ahead if kind == "ahead" else 1 - ahead
                    copies = [pltpu.make_async_copy(wide.at[at], ref.at[0, j, :, lanes], sems.at[at]) for ref in (forward, backward)]
                    for value, copy in enumerate(copies):
                        pl.when(side == value)(copy.start)
                    waits.append(copies[0])
            for copy in waits:
                copy.wait()


def assemble(parts, shape, plan, filled=()):
    steps = max(sum(len(items(spot)) for _, _, spot, _ in one) for one in plan)
    anywhere = pl.BlockSpec(memory_space=pl.ANY)
    bins, part = parts[0].shape[1:]
    return pl.pallas_call(
        functools.partial(assemble_body, plan=plan, count=len(parts), filled=len(filled) // 2),
        in_specs=[pl.BlockSpec(memory_space=pltpu.VMEM)] * len(parts) + [anywhere] * len(filled),
        out_specs=[anywhere] * 2,
        out_shape=[jax.ShapeDtypeStruct((1,) + shape, jnp.float32)] * 2,
        scratch_shapes=[pltpu.VMEM((steps, bins, part), jnp.float32), pltpu.SemaphoreType.DMA((steps,))],
        input_output_aliases={len(parts) + i: i for i in range(len(filled))},
        compiler_params=pltpu.CompilerParams(vmem_limit_bytes=12 * MIB),
        cost_estimate=pl.CostEstimate(flops=steps * bins * part, bytes_accessed=6 * steps * bins * part, transcendentals=0),
    )(*parts, *filled)


HERE = (0, 0, 0, 0)
OUTWARD = (-1, -1, 1, 1)
INWARD = (1, 1, -1, -1)
INNER_HERE = (None, 0, 0, None)
INNER_INWARD = (None, 1, -1, None)
INNER_OUTWARD = (None, -1, 1, None)


def send(value, flip, step):
    peers = lax.axis_size("chan")
    pairs = []
    for i in range(peers):
        planes = step[i % PLANE]
        if planes is not None and 0 <= i + PLANE * planes < peers:
            pairs.append((i, (i ^ flip) + PLANE * planes))
    return lax.ppermute(value, "chan", pairs)


def after(value, *done):
    return lax.optimization_barrier((value,) + done)[0]


def local(traces, mask, counts):
    _, windows, lags, width = traces.shape
    causal, tables = lag_tables(lags)
    tables = jnp.asarray(tables)
    rows = jnp.asarray(np.ascontiguousarray(causal.T))
    t2, t3 = whiten(mask, rows, traces, (windows, windows))
    t01, = whiten(after(mask, t2), rows, traces, (2 * windows,))

    y2, y3 = send(t2, 2, HERE), send(t3, 3, HERE)
    z, e = send(t01, 0, OUTWARD), send(t01, 0, INNER_INWARD)
    u1 = send(t01[windows:], 1, HERE)
    r2 = send(after(y2, u1), 0, INWARD)
    r3b = send(after(t3, y2)[relayed(windows):], 3, OUTWARD)

    whole = lambda *arrays: {spot: ((array, 0, windows),) for spot, array in arrays}
    parts = correlate(
        counts, tables, (t01, u1, y2), ((NEAR[0],), (NEAR[1],)), sources=(
            whole((0, 0), (1, 1), (2, 2)),
            whole((0, 1), (1, 0), (3, 2))), weight=200)
    r3a = send(after(y3, parts[4])[:relayed(windows)], 0, INWARD)
    e1 = send(after(e, parts[4])[windows:], 1, INNER_HERE)
    parts = correlate(
        counts, tables, (t01, u1, y2, y3), ((REST[0],), (REST[1],)), sources=(
            whole((0, 0), (1, 1), (2, 2), (3, 3)),
            whole((0, 1), (1, 0), (2, 3), (3, 2))), filled=parts, weight=200)
    half = windows // 2
    z = after(z, parts[4])
    z1a, z1b = send(z[windows:windows + half], 1, HERE), send(z[windows + half:], 1, HERE)
    other = ((5, 0, half), (6, half, windows))
    parts = correlate(
        counts, tables, (t01, u1, y2, y3, z, z1a, z1b, r2, e1, e), ((BEYOND, INNER, FIRST), (BEYOND, OUTER, FIRST)), sources=(
            whole((0, 0), (1, 1), (2, 2), (3, 3), (4, 4), (-2, 7), (-3, 8)) | {5: other},
            whole((0, 1), (1, 0), (2, 3), (3, 2), (5, 4), (-1, 7), (-3, 9)) | {4: other}), filled=parts, weight=0)
    last = ((5, 0, relayed(windows)), (6, relayed(windows), windows))
    keep, f, x, v, w, sib = correlate(
        counts, tables, (t01, u1, y2, y3, z, r3a, r3b), ((OUTER,), (INNER,)), sources=(
            whole((0, 0), (1, 1), (2, 2), (3, 3), (4, 4)) | {-1: last},
            whole((0, 1), (1, 0), (2, 3), (3, 2)) | {-2: last}), filled=parts)

    sib = send(sib, 1, HERE)
    f, x, v, w = merge(sib, (f, x, v, w))
    f, x, v = send(f, 2, HERE), send(x, 0, INWARD), send(v, 2, OUTWARD)
    w = send(w, 0, INNER_OUTWARD)

    shape = (MAXP, lags // 2, width)
    filled = assemble((keep, sib), shape, [[(0, 0, mine, 0), (1, 1, mine, 0)] for mine in range(2)])
    return tuple(assemble((f, x, v, w), shape, [
        [(0, 2, 3 - mine, 0), (0, 3, 3 - mine, SIZES[1]), (1, 0, 4 + mine, 0), (1, 1, 4 + mine, SIZES[2]),
         (2, 2, -1 - mine, 0), (2, 3, -1 - mine, SIZES[3])] + inner
        for mine, inner in enumerate(([], [(3, 0, -3, 0), (3, 1, -3, 1)]))], filled))


def solution(mesh):
    return jax.shard_map(
        local,
        mesh=mesh,
        in_specs=(P(("grp", "chan"), None, None, None), P("grp", None), P("grp")),
        out_specs=(P(("grp", "chan"), None, None, None), P(("grp", "chan"), None, None, None)),
        check_vma=False,
    )
```

time: 116 us -> 101 us (0.87)
  waiting for transfers between devices: 58.2 us -> 45.8 us
  Pallas kernels: 30.1 us -> 24.5 us
  starting transfers between devices: 25.1 us -> 27.7 us
    ppermute x14 -> x16, waiting for transfers between devices: 58.2 us -> 45.8 us  [send(): return lax.ppermute(value, 'chan', pairs)]
    ppermute x14 -> x16, starting transfers between devices: 25.1 us -> 27.7 us  [send(): return lax.ppermute(value, 'chan', pairs)]
    pallas_call x2, Pallas kernels: 4.84 us -> 2.46 us  [assemble(): pl.pallas_call(functools.partial(assemble_body, plan=plan, count=len(part...]
    pallas_call x3 -> x6, Pallas kernels: 23.3 us -> 21.5 us  [the longest x4 14.6 us: correlate(): pl.pallas_call(functools.partial(correlate_body, work=work, sources=sourc...]
    slice x0 -> x5, local copies, waits for them, and re-layouts: none -> 1.71 us  [the longest x1 1.44 us: local(): u1 = send(t01[windows:], 1, HERE)]
    unnamed x24 -> x8, local copies, waits for them, and re-layouts: 1.63 us -> 0.02 us
    pallas_call x1, Pallas kernels: 1.9 us -> 0.6 us  [merge(): pl.pallas_call(merge_body, in_specs=[pl.BlockSpec(memory_space=pltpu.VMEM...]
  transfers between devices with their start and end apart: 14 -> 16, of which waited for: 9 -> 8; matrix products, arithmetic and copies ran while one was open for 0% -> 2% of each run, Pallas kernels for 12% -> 16%
where the time goes in v3:
time: 101 us
  waiting for transfers between devices  45.8 us (45%)
  starting transfers between devices  27.7 us (27%)
  Pallas kernels  24.5 us (24%)
  local copies, waits for them, and re-layouts  1.73 us (2%)
    ppermute x16, waiting for transfers between devices, send(): return lax.ppermute(value, 'chan', pairs)  45.8 us
    ppermute x16, starting transfers between devices, send(): return lax.ppermute(value, 'chan', pairs)  27.7 us
    pallas_call x4, Pallas kernels, correlate(): pl.pallas_call(functools.partial(correlate_body, work=work, sources=sourc...  14.6 us
    pallas_call x2, Pallas kernels, whiten(): pl.pallas_call(whiten_body, grid=(windows // STEP,), in_specs=[pl.BlockSp...  6.82 us
    pallas_call x2, Pallas kernels, assemble(): pl.pallas_call(functools.partial(assemble_body, plan=plan, count=len(part...  2.46 us
  transfers between devices with their start and end apart: 16, of which 8 were waited for; matrix products, arithmetic and copies ran while one was open for 2% of the time, Pallas kernels for 16%

profile of v3, /device:TPU:16, one launch (start us, length us, event | category | flops | bytes accessed | tf_op | source)
XLA Modules:
  0.0 100.6 jit_solution(1568261328225922156)
XLA Ops:
  0.6 3.4 %shard_map.68 = (bf16[16,2,128,128]{3,2,1,0:T(8,128)(2,1)}, bf16[16,2,128,128]{3,2,1,0:T(8,128)(2,1)}) custom-call(s32[16,16]{1,0:T(8,128)} %mask_ref.2, bf16[256,256]{1,0:T(8,128)(2,1)} %constant.5.clone.table_ref, bf16[1,16,256,512]{3,2,1,0:T(8,128)(2,1)} %traces_ref.3), custom_call_target="tpu_custom_call" | custom-call | flops 536870912 | bytes 4194304 | tf_op jit(solution)/shard_map/pallas_call | solution.py:105
  4.0 1.6 %collective-permute-start.1 = (bf16[16,2,128,128]{3,2,1,0:T(8,128)(2,1)}, bf16[16,2,128,128]{3,2,1,0:T(8,128)(2,1)S(1)}, u32[]{:S(2)}, u32[]{:S(2)}) collective-permute-start(bf16[16,2,128,128]{3,2,1,0:T(8,128)(2,1)} %get-tuple-element.40), channel_id=1, source_target_pairs={{0,2},{1,3},{2,0},{3,1},{4,6},{5,7},{6,4},{7,5},{8,10},{9,11},{10,... | collective-permute-start | bytes 3145736 | tf_op jit(solution)/shard_map/ppermute | solution.py:293
  5.6 0.0 copy-start.3
  5.6 0.0 copy-start.1
  5.6 3.5 %shard_map.69.refs_0_ = bf16[32,2,128,128]{3,2,1,0:T(8,128)(2,1)} custom-call(s32[16,16]{1,0:T(8,128)} %mask_ref.2, bf16[256,256]{1,0:T(8,128)(2,1)} %constant.5.clone.table_ref, bf16[1,16,256,512]{3,2,1,0:T(8,128)(2,1)} %traces_ref.3), custom_call_target="tpu_custom_call" | custom-call | flops 536870912 | bytes 4194304 | tf_op jit(solution)/shard_map/pallas_call | solution.py:105
  9.1 0.0 copy-start
  9.1 0.0 copy-start.2
  9.1 1.4 %slice.24 = bf16[16,2,128,128]{3,2,1,0:T(8,128)(2,1)S(1)} slice(bf16[32,2,128,128]{3,2,1,0:T(8,128)(2,1)} %shard_map.69.refs_0_), slice={[16:32], [0:2], [0:128], [0:128]} | slice | bytes 2097152 | tf_op jit(solution)/shard_map/slice | solution.py:310
  10.5 0.1 collective-permute-start
  10.6 0.8 collective-permute-start.9
  11.4 2.4 %collective-permute-start.3 = (bf16[32,2,128,128]{3,2,1,0:T(8,128)(2,1)}, bf16[32,2,128,128]{3,2,1,0:T(8,128)(2,1)S(1)}, u32[]{:S(2)}, u32[]{:S(2)}) collective-permute-start(bf16[32,2,128,128]{3,2,1,0:T(8,128)(2,1)} %shard_map.69.refs_0_), channel_id=1, source_target_pairs={{2,6},{3,7},{4,0},{5,1},{6,10},{7,11},{8,4},{9,5},{10,14},{11,15},... | collective-permute-start | bytes 6291464 | tf_op jit(solution)/shard_map/ppermute | solution.py:293
  13.8 0.0 copy-done.3
  13.8 1.5 %collective-permute-start.2 = (bf16[16,2,128,128]{3,2,1,0:T(8,128)(2,1)S(1)}, bf16[16,2,128,128]{3,2,1,0:T(8,128)(2,1)S(1)}, u32[]{:S(2)}, u32[]{:S(2)}) collective-permute-start(bf16[16,2,128,128]{3,2,1,0:T(8,128)(2,1)S(1)} %copy-done.3), channel_id=1, source_target_pairs={{0,3},{1,2},{2,1},{3,0},{4,7},{5,6},{6,5},{7,4},{8,11},{9,10},{10,... | collective-permute-start | bytes 3145736 | tf_op jit(solution)/shard_map/ppermute | solution.py:293
  15.3 15.0 %collective-permute-done.1.refs_2_ = bf16[16,2,128,128]{3,2,1,0:T(8,128)(2,1)S(1)} collective-permute-done((bf16[16,2,128,128]{3,2,1,0:T(8,128)(2,1)}, bf16[16,2,128,128]{3,2,1,0:T(8,128)(2,1)S(1)}, u32[]{:S(2)}, u32[]{:S(2)}) %collective-permute-start.1) | collective-permute-done | bytes 1048608 | tf_op jit(solution)/shard_map/ppermute | solution.py:293
  30.3 0.0 collective-permute-done.refs_1_
  30.3 3.5 %collective-permute-start.8 = (bf16[16,2,128,128]{3,2,1,0:T(8,128)(2,1)S(1)}, bf16[16,2,128,128]{3,2,1,0:T(8,128)(2,1)S(1)}, u32[]{:S(2)}, u32[]{:S(2)}) collective-permute-start(bf16[16,2,128,128]{3,2,1,0:T(8,128)(2,1)S(1)} %collective-permute-done.1.refs_2_), channel_id=1, source_target_pairs={{0,4},{1,5},{4,8},{5,9},{6,2},{7,3},{8,12},{9,13},{10,6},{11,7},{1... | collective-permute-start | bytes 3145736 | tf_op jit(solution)/shard_map/ppermute | solution.py:293
  33.8 0.0 copy-done.1
  33.8 0.0 copy-done
  33.8 0.0 copy-done.2
  33.8 2.3 %shard_map.70 = (bf16[7,128,128]{2,1,0:T(8,128)(2,1)S(1)}, bf16[12,128,128]{2,1,0:T(8,128)(2,1)S(1)}, bf16[6,128,128]{2,1,0:T(8,128)(2,1)S(1)}, bf16[8,128,128]{...) custom-call(s32[16]{0:T(128)S(1)} %copy-done.2, ...), custom_call_target="tpu_custom_call" | custom-call | flops 15728640000 | bytes 3145728 | tf_op jit(solution)/shard_map/pallas_call | solution.py:197
  36.1 14.6 %collective-permute-done.2.refs_3_ = bf16[16,2,128,128]{3,2,1,0:T(8,128)(2,1)S(1)} collective-permute-done((bf16[16,2,128,128]{3,2,1,0:T(8,128)(2,1)S(1)}, bf16[16,2,128,128]{3,2,1,0:T(8,128)(2,1)S(1)}, u32[]{:S(2)}, u32[]{:S(2)}) %collective-permute-start.2) | collective-permute-done | bytes 1048608 | tf_op jit(solution)/shard_map/ppermute | solution.py:293
  50.7 0.1 slice.19
  50.7 3.5 %collective-permute-start.4 = (bf16[10,2,128,128]{3,2,1,0:T(8,128)(2,1)S(1)}, bf16[10,2,128,128]{3,2,1,0:T(8,128)(2,1)S(1)}, u32[]{:S(2)}, u32[]{:S(2)}) collective-permute-start(bf16[10,2,128,128]{3,2,1,0:T(8,128)(2,1)S(1)} %slice.19), channel_id=1, source_target_pairs={{0,4},{1,5},{4,8},{5,9},{6,2},{7,3},{8,12},{9,13},{10,6},{11,7},{1... | collective-permute-start | bytes 1966088 | tf_op jit(solution)/shard_map/ppermute | solution.py:293
  54.2 0.0 collective-permute-done.9.refs_9_
  54.2 0.1 slice.23
  54.3 1.3 %collective-permute-start.10 = (bf16[16,2,128,128]{3,2,1,0:T(8,128)(2,1)S(1)}, bf16[16,2,128,128]{3,2,1,0:T(8,128)(2,1)S(1)}, u32[]{:S(2)}, u32[]{:S(2)}) collective-permute-start(bf16[16,2,128,128]{3,2,1,0:T(8,128)(2,1)S(1)} %slice.23), channel_id=1, source_target_pairs={{1,0},{2,3},{5,4},{6,7},{9,8},{10,11},{13,12},{14,15},{17,16},{18,... | collective-permute-start | bytes 3145736 | tf_op jit(solution)/shard_map/ppermute | solution.py:293
  55.6 2.4 %shard_map.71 = (bf16[7,128,128]{2,1,0:T(8,128)(2,1)S(1)}, bf16[12,128,128]{2,1,0:T(8,128)(2,1)S(1)}, bf16[6,128,128]{2,1,0:T(8,128)(2,1)S(1)}, bf16[8,128,128]{...) custom-call(s32[16]{0:T(128)S(1)} %copy-done.2, ...), custom_call_target="tpu_custom_call", output_to_operand_aliasing={{0}: (6, {}), {1}: (7, {}), {2}: (8, {}), {3}: (9, {}), {4}... | custom-call | flops 15728640000 | bytes 4194304 | tf_op jit(solution)/shard_map/pallas_call | solution.py:197
  58.0 2.0 %collective-permute-done.3.refs_4_ = bf16[32,2,128,128]{3,2,1,0:T(8,128)(2,1)S(1)} collective-permute-done((bf16[32,2,128,128]{3,2,1,0:T(8,128)(2,1)}, bf16[32,2,128,128]{3,2,1,0:T(8,128)(2,1)S(1)}, u32[]{:S(2)}, u32[]{:S(2)}) %collective-permute-start.3) | collective-permute-done | bytes 2097184 | tf_op jit(solution)/shard_map/ppermute | solution.py:293
  60.0 0.1 fusion
  60.1 2.2 %collective-permute-start.7 = (bf16[8,2,128,128]{3,2,1,0:T(8,128)(2,1)S(1)}, bf16[8,2,128,128]{3,2,1,0:T(8,128)(2,1)S(1)}, u32[]{:S(2)}, u32[]{:S(2)}) collective-permute-start(bf16[8,2,128,128]{3,2,1,0:T(8,128)(2,1)S(1)} %get-tuple-element.78), channel_id=1, source_target_pairs={{0,1},{1,0},{2,3},{3,2},{4,5},{5,4},{6,7},{7,6},{8,9},{9,8},{10,11... | collective-permute-start | bytes 1572872 | tf_op jit(solution)/shard_map/ppermute | solution.py:293
  62.3 0.1 collective-permute-start.6
  62.4 0.0 collective-permute-done.8.refs_7_
  62.4 1.9 %collective-permute-start.5 = (bf16[6,2,128,128]{3,2,1,0:T(8,128)(2,1)S(1)}, bf16[6,2,128,128]{3,2,1,0:T(8,128)(2,1)S(1)}, u32[]{:S(2)}, u32[]{:S(2)}) collective-permute-start(bf16[6,2,128,128]{3,2,1,0:T(8,128)(2,1)S(1)} %slice.20), channel_id=1, source_target_pairs={{2,5},{3,4},{4,3},{5,2},{6,9},{7,8},{8,7},{9,6},{10,13},{11,12},{1... | collective-permute-start | bytes 1179656 | tf_op jit(solution)/shard_map/ppermute | solution.py:293
  64.3 0.0 collective-permute-done.7.refs_6_
  64.4 0.2 collective-permute-done.6.refs_5_
  64.6 0.0 collective-permute-done.10.refs_8_
  64.6 6.7 %shard_map.72 = (bf16[7,128,128]{2,1,0:T(8,128)(2,1)S(1)}, bf16[12,128,128]{2,1,0:T(8,128)(2,1)S(1)}, bf16[6,128,128]{2,1,0:T(8,128)(2,1)S(1)}, bf16[8,128,128]{...) custom-call(s32[16]{0:T(128)S(1)} %copy-done.2, ...), custom_call_target="tpu_custom_call", output_to_operand_aliasing={{0}: (12, {}), {1}: (13, {}), {2}: (14, {}), {3}: (15, {}),... | custom-call | tf_op jit(solution)/shard_map/pallas_call | solution.py:197
  71.3 4.3 %collective-permute-done.5.refs_6_ = bf16[6,2,128,128]{3,2,1,0:T(8,128)(2,1)S(1)} collective-permute-done((bf16[6,2,128,128]{3,2,1,0:T(8,128)(2,1)S(1)}, bf16[6,2,128,128]{3,2,1,0:T(8,128)(2,1)S(1)}, u32[]{:S(2)}, u32[]{:S(2)}) %collective-permute-start.5) | collective-permute-done | bytes 393248 | tf_op jit(solution)/shard_map/ppermute | solution.py:293
  75.6 0.0 collective-permute-done.4.refs_5_
  75.6 3.2 %shard_map.73 = (bf16[7,128,128]{2,1,0:T(8,128)(2,1)S(1)}, bf16[12,128,128]{2,1,0:T(8,128)(2,1)S(1)}, bf16[6,128,128]{2,1,0:T(8,128)(2,1)S(1)}, bf16[8,128,128]{...) custom-call(s32[16]{0:T(128)S(1)} %copy-done.2, ...), custom_call_target="tpu_custom_call", output_to_operand_aliasing={{0}: (9, {}), {1}: (10, {}), {2}: (11, {}), {3}: (12, {}), ... | custom-call | flops 104857600 | bytes 7340032 | tf_op jit(solution)/shard_map/pallas_call | solution.py:197
  78.9 0.9 collective-permute-start.11
  79.8 1.8 %collective-permute-done.11.sib.refs_1_ = bf16[21,128,128]{2,1,0:T(8,128)(2,1)S(1)} collective-permute-done((bf16[21,128,128]{2,1,0:T(8,128)(2,1)S(1)}, bf16[21,128,128]{2,1,0:T(8,128)(2,1)S(1)}, u32[]{:S(2)}, u32[]{:S(2)}) %collective-permute-start.11) | collective-permute-done | bytes 688160 | tf_op jit(solution)/shard_map/ppermute | solution.py:293
  81.5 0.6 shard_map.74
  82.1 1.2 %collective-permute-start.12 = (bf16[12,128,128]{2,1,0:T(8,128)(2,1)S(1)}, bf16[12,128,128]{2,1,0:T(8,128)(2,1)S(1)}, u32[]{:S(2)}, u32[]{:S(2)}) collective-permute-start(bf16[12,128,128]{2,1,0:T(8,128)(2,1)S(1)} %get-tuple-element.71), channel_id=1, source_target_pairs={{0,2},{1,3},{2,0},{3,1},{4,6},{5,7},{6,4},{7,5},{8,10},{9,11},{10,... | collective-permute-start | bytes 1179656 | tf_op jit(solution)/shard_map/ppermute | solution.py:293
  83.4 2.7 %collective-permute-start.14 = (bf16[8,128,128]{2,1,0:T(8,128)(2,1)S(1)}, bf16[8,128,128]{2,1,0:T(8,128)(2,1)S(1)}, u32[]{:S(2)}, u32[]{:S(2)}) collective-permute-start(bf16[8,128,128]{2,1,0:T(8,128)(2,1)S(1)} %get-tuple-element.73), channel_id=1, source_target_pairs={{2,4},{3,5},{4,2},{5,3},{6,8},{7,9},{8,6},{9,7},{10,12},{11,13},{1... | collective-permute-start | bytes 786440 | tf_op jit(solution)/shard_map/ppermute | solution.py:293
  86.0 3.5 %collective-permute-start.13 = (bf16[6,128,128]{2,1,0:T(8,128)(2,1)S(1)}, bf16[6,128,128]{2,1,0:T(8,128)(2,1)S(1)}, u32[]{:S(2)}, u32[]{:S(2)}) collective-permute-start(bf16[6,128,128]{2,1,0:T(8,128)(2,1)S(1)} %get-tuple-element.72), channel_id=1, source_target_pairs={{0,4},{1,5},{4,8},{5,9},{6,2},{7,3},{8,12},{9,13},{10,6},{11,7},{1... | collective-permute-start | bytes 589832 | tf_op jit(solution)/shard_map/ppermute | solution.py:293
  89.5 0.7 collective-permute-start.15
  90.2 1.1 %shard_map.75 = (f32[1,5,128,512]{3,2,1,0:T(8,128)}, f32[1,5,128,512]{3,2,1,0:T(8,128)}) custom-call(bf16[7,128,128]{2,1,0:T(8,128)(2,1)S(1)} %get-tuple-element.75.refs_0_, bf16[21,128,128]{2,1,0:T(8,128)(2,1)S(1)} %collective-permute-done.11.sib.refs_1_), custom_call_target="tpu_custom_call" | custom-call | flops 229376 | bytes 1376256 | tf_op jit(solution)/shard_map/pallas_call | solution.py:266
  91.3 0.0 collective-permute-done.15.refs_3_
  91.3 3.3 %collective-permute-done.13.refs_1_ = bf16[6,128,128]{2,1,0:T(8,128)(2,1)S(1)} collective-permute-done((bf16[6,128,128]{2,1,0:T(8,128)(2,1)S(1)}, bf16[6,128,128]{2,1,0:T(8,128)(2,1)S(1)}, u32[]{:S(2)}, u32[]{:S(2)}) %collective-permute-start.13) | collective-permute-done | bytes 196640 | tf_op jit(solution)/shard_map/ppermute | solution.py:293
  94.5 0.0 collective-permute-done.14.refs_2_
  94.5 4.7 %collective-permute-done.12.refs_0_ = bf16[12,128,128]{2,1,0:T(8,128)(2,1)S(1)} collective-permute-done((bf16[12,128,128]{2,1,0:T(8,128)(2,1)S(1)}, bf16[12,128,128]{2,1,0:T(8,128)(2,1)S(1)}, u32[]{:S(2)}, u32[]{:S(2)}) %collective-permute-start.12) | collective-permute-done | bytes 393248 | tf_op jit(solution)/shard_map/ppermute | solution.py:293
  99.2 1.4 %shard_map.76 = (f32[1,5,128,512]{3,2,1,0:T(8,128)}, f32[1,5,128,512]{3,2,1,0:T(8,128)}) custom-call(bf16[12,128,128]{2,1,0:T(8,128)(2,1)S(1)} %collective-permute-done.12.refs_0_, bf16[6,128,128]{2,1,0:T(8,128)(2,1)S(1)} %collective-permute-done.13.refs_1_, ...), custom_call_target="tpu_custom_call", output_to_operand_aliasing={{0}: (4, {}), {1}: (5, {})} | custom-call | flops 458752 | bytes 2752512 | tf_op jit(solution)/shard_map/pallas_call | solution.py:266
  (1 shorter events, 0.0 us)
Async XLA Ops:
  4.0 26.3 %collective-permute-start.1 = (bf16[16,2,128,128]{3,2,1,0:T(8,128)(2,1)}, bf16[16,2,128,128]{3,2,1,0:T(8,128)(2,1)S(1)}, u32[]{:S(2)}, u32[]{:S(2)}) collective-permute-start(bf16[16,2,128,128]{3,2,1,0:T(8,128)(2,1)} %get-tuple-element.40), channel_id=1, source_target_pairs={{0,2},{1,3},{2,0},{3,1},{4,6},{5,7},{6,4},{7,5},{8,10},{9,11},{10,... | collective-permute-start | bytes 3145736 | tf_op jit(solution)/shard_map/ppermute | solution.py:293
  5.6 8.2 %copy-start.3 = (bf16[16,2,128,128]{3,2,1,0:T(8,128)(2,1)S(1)}, bf16[16,2,128,128]{3,2,1,0:T(8,128)(2,1)}, u32[]{:S(2)}) copy-start(bf16[16,2,128,128]{3,2,1,0:T(8,128)(2,1)} %get-tuple-element.52) | copy-start | bytes 3145732
  5.6 28.2 %copy-start.1 = (bf16[2,256,256]{2,1,0:T(8,128)(2,1)S(1)}, bf16[2,256,256]{2,1,0:T(8,128)(2,1)}, u32[]{:S(2)}) copy-start(bf16[2,256,256]{2,1,0:T(8,128)(2,1)} %constant.4.clone.table_ref) | copy-start | bytes 786436
  9.1 24.8 %copy-start = (bf16[32,2,128,128]{3,2,1,0:T(8,128)(2,1)S(1)}, bf16[32,2,128,128]{3,2,1,0:T(8,128)(2,1)}, u32[]{:S(2)}) copy-start(bf16[32,2,128,128]{3,2,1,0:T(8,128)(2,1)} %shard_map.69.refs_0_) | copy-start | bytes 6291460
  9.1 24.8 %copy-start.2 = (s32[16]{0:T(128)S(1)}, s32[16]{0:T(128)}, u32[]{:S(2)}) copy-start(s32[16]{0:T(128)} %counts_ref.7) | copy-start | bytes 196
  10.5 19.8 %collective-permute-start = (bf16[16,2,128,128]{3,2,1,0:T(8,128)(2,1)S(1)}, bf16[16,2,128,128]{3,2,1,0:T(8,128)(2,1)S(1)}, u32[]{:S(2)}, u32[]{:S(2)}) collective-permute-start(bf16[16,2,128,128]{3,2,1,0:T(8,128)(2,1)S(1)} %slice.24), channel_id=1, source_target_pairs={{0,1},{1,0},{2,3},{3,2},{4,5},{5,4},{6,7},{7,6},{8,9},{9,8},{10,11... | collective-permute-start | bytes 3145736 | tf_op jit(solution)/shard_map/ppermute | solution.py:293
  10.6 43.6 %collective-permute-start.9 = (bf16[32,2,128,128]{3,2,1,0:T(8,128)(2,1)}, bf16[32,2,128,128]{3,2,1,0:T(8,128)(2,1)S(1)}, u32[]{:S(2)}, u32[]{:S(2)}) collective-permute-start(bf16[32,2,128,128]{3,2,1,0:T(8,128)(2,1)} %shard_map.69.refs_0_), channel_id=1, source_target_pairs={{1,5},{5,9},{6,2},{9,13},{10,6},{14,10},{17,21},{21,25},{22,18},{2... | collective-permute-start | bytes 6291464 | tf_op jit(solution)/shard_map/ppermute | solution.py:293
  11.4 48.6 %collective-permute-start.3 = (bf16[32,2,128,128]{3,2,1,0:T(8,128)(2,1)}, bf16[32,2,128,128]{3,2,1,0:T(8,128)(2,1)S(1)}, u32[]{:S(2)}, u32[]{:S(2)}) collective-permute-start(bf16[32,2,128,128]{3,2,1,0:T(8,128)(2,1)} %shard_map.69.refs_0_), channel_id=1, source_target_pairs={{2,6},{3,7},{4,0},{5,1},{6,10},{7,11},{8,4},{9,5},{10,14},{11,15},... | collective-permute-start | bytes 6291464 | tf_op jit(solution)/shard_map/ppermute | solution.py:293
  13.8 36.9 %collective-permute-start.2 = (bf16[16,2,128,128]{3,2,1,0:T(8,128)(2,1)S(1)}, bf16[16,2,128,128]{3,2,1,0:T(8,128)(2,1)S(1)}, u32[]{:S(2)}, u32[]{:S(2)}) collective-permute-start(bf16[16,2,128,128]{3,2,1,0:T(8,128)(2,1)S(1)} %copy-done.3), channel_id=1, source_target_pairs={{0,3},{1,2},{2,1},{3,0},{4,7},{5,6},{6,5},{7,4},{8,11},{9,10},{10,... | collective-permute-start | bytes 3145736 | tf_op jit(solution)/shard_map/ppermute | solution.py:293
  30.3 32.1 %collective-permute-start.8 = (bf16[16,2,128,128]{3,2,1,0:T(8,128)(2,1)S(1)}, bf16[16,2,128,128]{3,2,1,0:T(8,128)(2,1)S(1)}, u32[]{:S(2)}, u32[]{:S(2)}) collective-permute-start(bf16[16,2,128,128]{3,2,1,0:T(8,128)(2,1)S(1)} %collective-permute-done.1.refs_2_), channel_id=1, source_target_pairs={{0,4},{1,5},{4,8},{5,9},{6,2},{7,3},{8,12},{9,13},{10,6},{11,7},{1... | collective-permute-start | bytes 3145736 | tf_op jit(solution)/shard_map/ppermute | solution.py:293
  50.7 24.9 %collective-permute-start.4 = (bf16[10,2,128,128]{3,2,1,0:T(8,128)(2,1)S(1)}, bf16[10,2,128,128]{3,2,1,0:T(8,128)(2,1)S(1)}, u32[]{:S(2)}, u32[]{:S(2)}) collective-permute-start(bf16[10,2,128,128]{3,2,1,0:T(8,128)(2,1)S(1)} %slice.19), channel_id=1, source_target_pairs={{0,4},{1,5},{4,8},{5,9},{6,2},{7,3},{8,12},{9,13},{10,6},{11,7},{1... | collective-permute-start | bytes 1966088 | tf_op jit(solution)/shard_map/ppermute | solution.py:293
  54.3 10.2 %collective-permute-start.10 = (bf16[16,2,128,128]{3,2,1,0:T(8,128)(2,1)S(1)}, bf16[16,2,128,128]{3,2,1,0:T(8,128)(2,1)S(1)}, u32[]{:S(2)}, u32[]{:S(2)}) collective-permute-start(bf16[16,2,128,128]{3,2,1,0:T(8,128)(2,1)S(1)} %slice.23), channel_id=1, source_target_pairs={{1,0},{2,3},{5,4},{6,7},{9,8},{10,11},{13,12},{14,15},{17,16},{18,... | collective-permute-start | bytes 3145736 | tf_op jit(solution)/shard_map/ppermute | solution.py:293
  60.1 4.2 %collective-permute-start.7 = (bf16[8,2,128,128]{3,2,1,0:T(8,128)(2,1)S(1)}, bf16[8,2,128,128]{3,2,1,0:T(8,128)(2,1)S(1)}, u32[]{:S(2)}, u32[]{:S(2)}) collective-permute-start(bf16[8,2,128,128]{3,2,1,0:T(8,128)(2,1)S(1)} %get-tuple-element.78), channel_id=1, source_target_pairs={{0,1},{1,0},{2,3},{3,2},{4,5},{5,4},{6,7},{7,6},{8,9},{9,8},{10,11... | collective-permute-start | bytes 1572872 | tf_op jit(solution)/shard_map/ppermute | solution.py:293
  62.3 2.3 %collective-permute-start.6 = (bf16[8,2,128,128]{3,2,1,0:T(8,128)(2,1)S(1)}, bf16[8,2,128,128]{3,2,1,0:T(8,128)(2,1)S(1)}, u32[]{:S(2)}, u32[]{:S(2)}) collective-permute-start(bf16[8,2,128,128]{3,2,1,0:T(8,128)(2,1)S(1)} %get-tuple-element.79), channel_id=1, source_target_pairs={{0,1},{1,0},{2,3},{3,2},{4,5},{5,4},{6,7},{7,6},{8,9},{9,8},{10,11... | collective-permute-start | bytes 1572872 | tf_op jit(solution)/shard_map/ppermute | solution.py:293
  62.4 13.2 %collective-permute-start.5 = (bf16[6,2,128,128]{3,2,1,0:T(8,128)(2,1)S(1)}, bf16[6,2,128,128]{3,2,1,0:T(8,128)(2,1)S(1)}, u32[]{:S(2)}, u32[]{:S(2)}) collective-permute-start(bf16[6,2,128,128]{3,2,1,0:T(8,128)(2,1)S(1)} %slice.20), channel_id=1, source_target_pairs={{2,5},{3,4},{4,3},{5,2},{6,9},{7,8},{8,7},{9,6},{10,13},{11,12},{1... | collective-permute-start | bytes 1179656 | tf_op jit(solution)/shard_map/ppermute | solution.py:293
  78.9 2.7 %collective-permute-start.11 = (bf16[21,128,128]{2,1,0:T(8,128)(2,1)S(1)}, bf16[21,128,128]{2,1,0:T(8,128)(2,1)S(1)}, u32[]{:S(2)}, u32[]{:S(2)}) collective-permute-start(bf16[21,128,128]{2,1,0:T(8,128)(2,1)S(1)} %get-tuple-element.66), channel_id=1, source_target_pairs={{0,1},{1,0},{2,3},{3,2},{4,5},{5,4},{6,7},{7,6},{8,9},{9,8},{10,11... | collective-permute-start | bytes 2064392 | tf_op jit(solution)/shard_map/ppermute | solution.py:293
  82.1 17.1 %collective-permute-start.12 = (bf16[12,128,128]{2,1,0:T(8,128)(2,1)S(1)}, bf16[12,128,128]{2,1,0:T(8,128)(2,1)S(1)}, u32[]{:S(2)}, u32[]{:S(2)}) collective-permute-start(bf16[12,128,128]{2,1,0:T(8,128)(2,1)S(1)} %get-tuple-element.71), channel_id=1, source_target_pairs={{0,2},{1,3},{2,0},{3,1},{4,6},{5,7},{6,4},{7,5},{8,10},{9,11},{10,... | collective-permute-start | bytes 1179656 | tf_op jit(solution)/shard_map/ppermute | solution.py:293
  83.4 11.2 %collective-permute-start.14 = (bf16[8,128,128]{2,1,0:T(8,128)(2,1)S(1)}, bf16[8,128,128]{2,1,0:T(8,128)(2,1)S(1)}, u32[]{:S(2)}, u32[]{:S(2)}) collective-permute-start(bf16[8,128,128]{2,1,0:T(8,128)(2,1)S(1)} %get-tuple-element.73), channel_id=1, source_target_pairs={{2,4},{3,5},{4,2},{5,3},{6,8},{7,9},{8,6},{9,7},{10,12},{11,13},{1... | collective-permute-start | bytes 786440 | tf_op jit(solution)/shard_map/ppermute | solution.py:293
  86.0 8.5 %collective-permute-start.13 = (bf16[6,128,128]{2,1,0:T(8,128)(2,1)S(1)}, bf16[6,128,128]{2,1,0:T(8,128)(2,1)S(1)}, u32[]{:S(2)}, u32[]{:S(2)}) collective-permute-start(bf16[6,128,128]{2,1,0:T(8,128)(2,1)S(1)} %get-tuple-element.72), channel_id=1, source_target_pairs={{0,4},{1,5},{4,8},{5,9},{6,2},{7,3},{8,12},{9,13},{10,6},{11,7},{1... | collective-permute-start | bytes 589832 | tf_op jit(solution)/shard_map/ppermute | solution.py:293
  89.5 1.7 %collective-permute-start.15 = (bf16[2,128,128]{2,1,0:T(8,128)(2,1)S(1)}, bf16[2,128,128]{2,1,0:T(8,128)(2,1)S(1)}, u32[]{:S(2)}, u32[]{:S(2)}) collective-permute-start(bf16[2,128,128]{2,1,0:T(8,128)(2,1)S(1)} %get-tuple-element.74), channel_id=1, source_target_pairs={{2,6},{5,1},{6,10},{9,5},{10,14},{13,9},{18,22},{21,17},{22,26},{2... | collective-permute-start | bytes 196616 | tf_op jit(solution)/shard_map/ppermute | solution.py:293

commit v4 on v3

--- a/solution.py
+++ b/solution.py
@@ -35,6 +35,7 @@
     return ahead + back
 
 
+MERGED = (2, 3, 4)
 SIZES = [max(len(items(spot)) for spot in spots) for spots in DESTS]
 STARTS = [sum(SIZES[:d]) for d in range(len(SIZES))]
 PLACE = {spot: (d, i) for d, spots in enumerate(DESTS) for i, spot in enumerate(spots)}
@@ -79,8 +80,10 @@
 
     def copies(i):
         span = pl.ds(i * step, step)
-        targets = (outs[0].at[span], outs[0].at[pl.ds(windows + i * step, step)]) if len(outs) == 1 else [out.at[span] for out in outs]
-        return [pltpu.make_async_copy(white.at[k, span], target, sems.at[k, i]) for k, target in enumerate(targets)]
+        targets = [(n, out.at[span]) for n, out in enumerate(outs)]
+        if outs[0].shape[0] > windows:
+            targets.append((1, outs[0].at[pl.ds(windows + i * step, step)]))
+        return [pltpu.make_async_copy(white.at[k, span], target, sems.at[n, i]) for n, (k, target) in enumerate(targets)]
 
     for one in copies(at):
         one.start()
@@ -96,7 +99,7 @@
     _, windows, lags, width = traces.shape
     bins = lags // 2
     part = width // PLANE
-    other = len(lengths) - 1
+    other = lengths[0] == windows
 
     def half(i):
         far = whereabouts()[0]
@@ -114,7 +117,7 @@
         out_shape=[jax.ShapeDtypeStruct((n, 2, bins, part), jnp.bfloat16) for n in lengths],
         scratch_shapes=[
             pltpu.VMEM((2, windows, 2, bins, part), jnp.bfloat16),
-            pltpu.SemaphoreType.DMA((2, windows // STEP)),
+            pltpu.SemaphoreType.DMA((3, windows // STEP)),
         ],
         compiler_params=pltpu.CompilerParams(vmem_limit_bytes=57 * MIB),
         cost_estimate=pl.CostEstimate(flops=windows * lags * lags * width, bytes_accessed=2 * windows * lags * width, transcendentals=0),
@@ -193,7 +196,7 @@
     most = max(len(flat(groups)) for groups in work)
     anywhere = pl.BlockSpec(memory_space=pl.ANY)
     scalars = pl.BlockSpec(memory_space=pltpu.SMEM)
-    lengths = [SIZES[0]] + [2 * size for size in SIZES[1:]] + [sum(SIZES)]
+    lengths = [size * (2 if d in MERGED else 1) for d, size in enumerate(SIZES)] + [sum(SIZES)]
     return pl.pallas_call(
         functools.partial(correlate_body, work=work, sources=sources, filled=len(filled)),
         in_specs=[scalars] + [pl.BlockSpec(memory_space=pltpu.VMEM)] * (1 + len(whites)) + [anywhere] * len(filled),
@@ -211,11 +214,11 @@
 
 
 def merge_body(sib, *refs):
-    outs, sems = refs[len(DESTS) - 1:-1], refs[-1]
+    outs, sems = refs[len(MERGED):-1], refs[-1]
     copies = []
-    for d in range(1, len(DESTS)):
+    for n, d in enumerate(MERGED):
         copies.append(pltpu.make_async_copy(
-            sib.at[pl.ds(STARTS[d], SIZES[d])], outs[d - 1].at[pl.ds(SIZES[d], SIZES[d])], sems.at[d - 1]))
+            sib.at[pl.ds(STARTS[d], SIZES[d])], outs[n].at[pl.ds(SIZES[d], SIZES[d])], sems.at[n]))
     for one in copies:
         one.start()
     for one in copies:
@@ -259,7 +262,7 @@
                 copy.wait()
 
 
-def assemble(parts, shape, plan, filled=()):
+def assemble(parts, shape, plan, filled=(), weight=1):
     steps = max(sum(len(items(spot)) for _, _, spot, _ in one) for one in plan)
     anywhere = pl.BlockSpec(memory_space=pl.ANY)
     bins, part = parts[0].shape[1:]
@@ -271,7 +274,7 @@
         scratch_shapes=[pltpu.VMEM((steps, bins, part), jnp.float32), pltpu.SemaphoreType.DMA((steps,))],
         input_output_aliases={len(parts) + i: i for i in range(len(filled))},
         compiler_params=pltpu.CompilerParams(vmem_limit_bytes=12 * MIB),
-        cost_estimate=pl.CostEstimate(flops=steps * bins * part, bytes_accessed=6 * steps * bins * part, transcendentals=0),
+        cost_estimate=pl.CostEstimate(flops=weight * steps * bins * part, bytes_accessed=6 * steps * bins * part, transcendentals=0),
     )(*parts, *filled)
 
 
@@ -303,11 +306,11 @@
     tables = jnp.asarray(tables)
     rows = jnp.asarray(np.ascontiguousarray(causal.T))
     t2, t3 = whiten(mask, rows, traces, (windows, windows))
-    t01, = whiten(after(mask, t2), rows, traces, (2 * windows,))
+    t01, t1 = whiten(after(mask, t2), rows, traces, (2 * windows, windows))
 
     y2, y3 = send(t2, 2, HERE), send(t3, 3, HERE)
     z, e = send(t01, 0, OUTWARD), send(t01, 0, INNER_INWARD)
-    u1 = send(t01[windows:], 1, HERE)
+    u1 = send(t1, 1, HERE)
     r2 = send(after(y2, u1), 0, INWARD)
     r3b = send(after(t3, y2)[relayed(windows):], 3, OUTWARD)
 
@@ -336,15 +339,18 @@
             whole((0, 0), (1, 1), (2, 2), (3, 3), (4, 4)) | {-1: last},
             whole((0, 1), (1, 0), (2, 3), (3, 2)) | {-2: last}), filled=parts)
 
+    near = send(f, 2, HERE)
     sib = send(sib, 1, HERE)
-    f, x, v, w = merge(sib, (f, x, v, w))
-    f, x, v = send(f, 2, HERE), send(x, 0, INWARD), send(v, 2, OUTWARD)
+    x, v, w = merge(sib, (x, v, w))
+    rest = send(sib[STARTS[1]:STARTS[2]], 2, HERE)
+    v, x = send(v, 2, OUTWARD), send(x, 0, INWARD)
     w = send(w, 0, INNER_OUTWARD)
 
     shape = (MAXP, lags // 2, width)
     filled = assemble((keep, sib), shape, [[(0, 0, mine, 0), (1, 1, mine, 0)] for mine in range(2)])
-    return tuple(assemble((f, x, v, w), shape, [
-        [(0, 2, 3 - mine, 0), (0, 3, 3 - mine, SIZES[1]), (1, 0, 4 + mine, 0), (1, 1, 4 + mine, SIZES[2]),
+    filled = assemble((near,), shape, [[(0, 2, 3 - mine, 0)] for mine in range(2)], filled, weight=50000)
+    return tuple(assemble((rest, x, v, w), shape, [
+        [(0, 3, 3 - mine, 0), (1, 0, 4 + mine, 0), (1, 1, 4 + mine, SIZES[2]),
          (2, 2, -1 - mine, 0), (2, 3, -1 - mine, SIZES[3])] + inner
         for mine, inner in enumerate(([], [(3, 0, -3, 0), (3, 1, -3, 1)]))], filled))
 

time: 101 us -> 99 us (0.980)
  waiting for transfers between devices: 45.8 us -> 41.6 us
  starting transfers between devices: 27.7 us -> 29.2 us
    ppermute x16 -> x17, waiting for transfers between devices: 45.8 us -> 41.6 us  [send(): return lax.ppermute(value, 'chan', pairs)]
    unnamed x8 -> x10, local copies, waits for them, and re-layouts: 0.02 us -> 1.61 us
    ppermute x16 -> x17, starting transfers between devices: 27.7 us -> 29.2 us  [send(): return lax.ppermute(value, 'chan', pairs)]
    slice x1, local copies, waits for them, and re-layouts: 1.44 us -> 0.01 us  [local(): rest = send(sib[STARTS[1]:STARTS[2]], 2, HERE)]
    pallas_call x2 -> x3, Pallas kernels: 2.46 us -> 3.1 us  [assemble(): pl.pallas_call(functools.partial(assemble_body, plan=plan, count=len(part...]
  transfers between devices with their start and end apart: 16 -> 17, of which waited for: 8 -> 8; matrix products, arithmetic and copies ran while one was open for 2% -> 0% of each run, Pallas kernels for 16% -> 17%
where the time goes in v4:
time: 99 us; the launch traced here: 98.5 us
  waiting for transfers between devices  41.6 us (42%)
  starting transfers between devices  29.2 us (29%)
  Pallas kernels  25 us (25%)
  local copies, waits for them, and re-layouts  1.9 us (2%)
    ppermute x17, waiting for transfers between devices, send(): return lax.ppermute(value, 'chan', pairs)  41.6 us
    ppermute x17, starting transfers between devices, send(): return lax.ppermute(value, 'chan', pairs)  29.2 us
    pallas_call x4, Pallas kernels, correlate(): pl.pallas_call(functools.partial(correlate_body, work=work, sources=sourc...  14.6 us
    pallas_call x2, Pallas kernels, whiten(): pl.pallas_call(whiten_body, grid=(windows // STEP,), in_specs=[pl.BlockSp...  6.89 us
    pallas_call x3, Pallas kernels, assemble(): pl.pallas_call(functools.partial(assemble_body, plan=plan, count=len(part...  3.1 us
  transfers between devices with their start and end apart: 17, of which 8 were waited for; matrix products, arithmetic and copies ran while one was open for 0% of the time, Pallas kernels for 17%

profile of v4, /device:TPU:16, one launch (start us, length us, event | category | flops | bytes accessed | tf_op | source)
XLA Modules:
  0.0 98.5 jit_solution(8381333032437531192)
XLA Ops:
  0.6 3.4 %shard_map.68 = (bf16[16,2,128,128]{3,2,1,0:T(8,128)(2,1)}, bf16[16,2,128,128]{3,2,1,0:T(8,128)(2,1)}) custom-call(s32[16,16]{1,0:T(8,128)} %mask_ref.2, bf16[256,256]{1,0:T(8,128)(2,1)} %constant.5.clone.table_ref, bf16[1,16,256,512]{3,2,1,0:T(8,128)(2,1)} %traces_ref.3), custom_call_target="tpu_custom_call" | custom-call | flops 536870912 | bytes 4194304 | tf_op jit(solution)/shard_map/pallas_call | solution.py:108
  4.0 0.0 copy-start.4
  4.0 0.0 copy-start.2
  4.0 0.0 copy-start.3
  4.0 1.6 %collective-permute-start.1 = (bf16[16,2,128,128]{3,2,1,0:T(8,128)(2,1)}, bf16[16,2,128,128]{3,2,1,0:T(8,128)(2,1)S(1)}, u32[]{:S(2)}, u32[]{:S(2)}) collective-permute-start(bf16[16,2,128,128]{3,2,1,0:T(8,128)(2,1)} %get-tuple-element.43), channel_id=1, source_target_pairs={{0,2},{1,3},{2,0},{3,1},{4,6},{5,7},{6,4},{7,5},{8,10},{9,11},{10,... | collective-permute-start | bytes 3145736 | tf_op jit(solution)/shard_map/ppermute | solution.py:296
  5.6 3.5 %shard_map.69 = (bf16[32,2,128,128]{3,2,1,0:T(8,128)(2,1)}, bf16[16,2,128,128]{3,2,1,0:T(8,128)(2,1)}) custom-call(s32[16,16]{1,0:T(8,128)} %mask_ref.2, bf16[256,256]{1,0:T(8,128)(2,1)} %constant.5.clone.table_ref, bf16[1,16,256,512]{3,2,1,0:T(8,128)(2,1)} %traces_ref.3), custom_call_target="tpu_custom_call" | custom-call | flops 536870912 | bytes 4194304 | tf_op jit(solution)/shard_map/pallas_call | solution.py:108
  9.2 0.1 collective-permute-start
  9.2 0.8 collective-permute-start.9
  10.0 2.4 %collective-permute-start.3 = (bf16[32,2,128,128]{3,2,1,0:T(8,128)(2,1)}, bf16[32,2,128,128]{3,2,1,0:T(8,128)(2,1)S(1)}, u32[]{:S(2)}, u32[]{:S(2)}) collective-permute-start(bf16[32,2,128,128]{3,2,1,0:T(8,128)(2,1)} %get-tuple-element.45.refs_0_), channel_id=1, source_target_pairs={{2,6},{3,7},{4,0},{5,1},{6,10},{7,11},{8,4},{9,5},{10,14},{11,15},... | collective-permute-start | bytes 6291464 | tf_op jit(solution)/shard_map/ppermute | solution.py:296
  12.4 0.0 copy-done.4
  12.4 1.5 %collective-permute-start.2 = (bf16[16,2,128,128]{3,2,1,0:T(8,128)(2,1)S(1)}, bf16[16,2,128,128]{3,2,1,0:T(8,128)(2,1)S(1)}, u32[]{:S(2)}, u32[]{:S(2)}) collective-permute-start(bf16[16,2,128,128]{3,2,1,0:T(8,128)(2,1)S(1)} %copy-done.4), channel_id=1, source_target_pairs={{0,3},{1,2},{2,1},{3,0},{4,7},{5,6},{6,5},{7,4},{8,11},{9,10},{10,... | collective-permute-start | bytes 3145736 | tf_op jit(solution)/shard_map/ppermute | solution.py:296
  13.9 16.4 %collective-permute-done.1.refs_2_ = bf16[16,2,128,128]{3,2,1,0:T(8,128)(2,1)S(1)} collective-permute-done((bf16[16,2,128,128]{3,2,1,0:T(8,128)(2,1)}, bf16[16,2,128,128]{3,2,1,0:T(8,128)(2,1)S(1)}, u32[]{:S(2)}, u32[]{:S(2)}) %collective-permute-start.1) | collective-permute-done | bytes 1048608 | tf_op jit(solution)/shard_map/ppermute | solution.py:296
  30.4 0.0 collective-permute-done.refs_1_
  30.4 3.5 %collective-permute-start.8 = (bf16[16,2,128,128]{3,2,1,0:T(8,128)(2,1)S(1)}, bf16[16,2,128,128]{3,2,1,0:T(8,128)(2,1)S(1)}, u32[]{:S(2)}, u32[]{:S(2)}) collective-permute-start(bf16[16,2,128,128]{3,2,1,0:T(8,128)(2,1)S(1)} %collective-permute-done.1.refs_2_), channel_id=1, source_target_pairs={{0,4},{1,5},{4,8},{5,9},{6,2},{7,3},{8,12},{9,13},{10,6},{11,7},{1... | collective-permute-start | bytes 3145736 | tf_op jit(solution)/shard_map/ppermute | solution.py:296
  33.8 0.0 copy-done.2
  33.9 0.0 copy-done.3
  33.9 0.0 copy-start
  33.9 1.6 %copy-done = bf16[32,2,128,128]{3,2,1,0:T(8,128)(2,1)S(1)} copy-done((bf16[32,2,128,128]{3,2,1,0:T(8,128)(2,1)S(1)}, bf16[32,2,128,128]{3,2,1,0:T(8,128)(2,1)}, u32[]{:S(2)}) %copy-start) | copy-done | bytes 2097176
  35.5 2.3 %shard_map.70 = (bf16[7,128,128]{2,1,0:T(8,128)(2,1)S(1)}, bf16[6,128,128]{2,1,0:T(8,128)(2,1)S(1)}, bf16[6,128,128]{2,1,0:T(8,128)(2,1)S(1)}, bf16[8,128,128]{2...) custom-call(s32[16]{0:T(128)S(1)} %copy-done.3, ...), custom_call_target="tpu_custom_call" | custom-call | flops 15728640000 | bytes 3145728 | tf_op jit(solution)/shard_map/pallas_call | solution.py:200
  37.7 13.0 %collective-permute-done.2.refs_3_ = bf16[16,2,128,128]{3,2,1,0:T(8,128)(2,1)S(1)} collective-permute-done((bf16[16,2,128,128]{3,2,1,0:T(8,128)(2,1)S(1)}, bf16[16,2,128,128]{3,2,1,0:T(8,128)(2,1)S(1)}, u32[]{:S(2)}, u32[]{:S(2)}) %collective-permute-start.2) | collective-permute-done | bytes 1048608 | tf_op jit(solution)/shard_map/ppermute | solution.py:296
  50.7 0.1 slice.18
  50.8 0.0 copy-start.1
  50.8 3.6 %collective-permute-start.4 = (bf16[10,2,128,128]{3,2,1,0:T(8,128)(2,1)S(1)}, bf16[10,2,128,128]{3,2,1,0:T(8,128)(2,1)S(1)}, u32[]{:S(2)}, u32[]{:S(2)}) collective-permute-start(bf16[10,2,128,128]{3,2,1,0:T(8,128)(2,1)S(1)} %slice.18), channel_id=1, source_target_pairs={{0,4},{1,5},{4,8},{5,9},{6,2},{7,3},{8,12},{9,13},{10,6},{11,7},{1... | collective-permute-start | bytes 1966088 | tf_op jit(solution)/shard_map/ppermute | solution.py:296
  54.4 0.0 collective-permute-done.9.refs_9_
  54.4 0.1 slice.22
  54.5 1.3 %collective-permute-start.10 = (bf16[16,2,128,128]{3,2,1,0:T(8,128)(2,1)S(1)}, bf16[16,2,128,128]{3,2,1,0:T(8,128)(2,1)S(1)}, u32[]{:S(2)}, u32[]{:S(2)}) collective-permute-start(bf16[16,2,128,128]{3,2,1,0:T(8,128)(2,1)S(1)} %slice.22), channel_id=1, source_target_pairs={{1,0},{2,3},{5,4},{6,7},{9,8},{10,11},{13,12},{14,15},{17,16},{18,... | collective-permute-start | bytes 3145736 | tf_op jit(solution)/shard_map/ppermute | solution.py:296
  55.8 0.0 copy-done.1
  55.9 2.4 %shard_map.71 = (bf16[7,128,128]{2,1,0:T(8,128)(2,1)S(1)}, bf16[6,128,128]{2,1,0:T(8,128)(2,1)S(1)}, bf16[6,128,128]{2,1,0:T(8,128)(2,1)S(1)}, bf16[8,128,128]{2...) custom-call(s32[16]{0:T(128)S(1)} %copy-done.3, ...), custom_call_target="tpu_custom_call", output_to_operand_aliasing={{0}: (6, {}), {1}: (7, {}), {2}: (8, {}), {3}: (9, {}), {4}... | custom-call | flops 15728640000 | bytes 4194304 | tf_op jit(solution)/shard_map/pallas_call | solution.py:200
  58.2 0.4 collective-permute-done.3.refs_4_
  58.7 0.1 fusion
  58.8 2.2 %collective-permute-start.7 = (bf16[8,2,128,128]{3,2,1,0:T(8,128)(2,1)S(1)}, bf16[8,2,128,128]{3,2,1,0:T(8,128)(2,1)S(1)}, u32[]{:S(2)}, u32[]{:S(2)}) collective-permute-start(bf16[8,2,128,128]{3,2,1,0:T(8,128)(2,1)S(1)} %get-tuple-element.84), channel_id=1, source_target_pairs={{0,1},{1,0},{2,3},{3,2},{4,5},{5,4},{6,7},{7,6},{8,9},{9,8},{10,11... | collective-permute-start | bytes 1572872 | tf_op jit(solution)/shard_map/ppermute | solution.py:296
  60.9 0.1 collective-permute-start.6
  61.0 0.0 collective-permute-done.8.refs_7_
  61.1 1.9 %collective-permute-start.5 = (bf16[6,2,128,128]{3,2,1,0:T(8,128)(2,1)S(1)}, bf16[6,2,128,128]{3,2,1,0:T(8,128)(2,1)S(1)}, u32[]{:S(2)}, u32[]{:S(2)}) collective-permute-start(bf16[6,2,128,128]{3,2,1,0:T(8,128)(2,1)S(1)} %slice.19), channel_id=1, source_target_pairs={{2,5},{3,4},{4,3},{5,2},{6,9},{7,8},{8,7},{9,6},{10,13},{11,12},{1... | collective-permute-start | bytes 1179656 | tf_op jit(solution)/shard_map/ppermute | solution.py:296
  63.0 0.0 collective-permute-done.7.refs_6_
  63.0 0.2 collective-permute-done.6.refs_5_
  63.2 0.0 collective-permute-done.10.refs_8_
  63.2 6.7 %shard_map.72 = (bf16[7,128,128]{2,1,0:T(8,128)(2,1)S(1)}, bf16[6,128,128]{2,1,0:T(8,128)(2,1)S(1)}, bf16[6,128,128]{2,1,0:T(8,128)(2,1)S(1)}, bf16[8,128,128]{2...) custom-call(s32[16]{0:T(128)S(1)} %copy-done.3, ...), custom_call_target="tpu_custom_call", output_to_operand_aliasing={{0}: (12, {}), {1}: (13, {}), {2}: (14, {}), {3}: (15, {}),... | custom-call | tf_op jit(solution)/shard_map/pallas_call | solution.py:200
  70.0 4.7 %collective-permute-done.5.refs_6_ = bf16[6,2,128,128]{3,2,1,0:T(8,128)(2,1)S(1)} collective-permute-done((bf16[6,2,128,128]{3,2,1,0:T(8,128)(2,1)S(1)}, bf16[6,2,128,128]{3,2,1,0:T(8,128)(2,1)S(1)}, u32[]{:S(2)}, u32[]{:S(2)}) %collective-permute-start.5) | collective-permute-done | bytes 393248 | tf_op jit(solution)/shard_map/ppermute | solution.py:296
  74.7 0.0 collective-permute-done.4.refs_5_
  74.7 3.2 %shard_map.73 = (bf16[7,128,128]{2,1,0:T(8,128)(2,1)S(1)}, bf16[6,128,128]{2,1,0:T(8,128)(2,1)S(1)}, bf16[6,128,128]{2,1,0:T(8,128)(2,1)S(1)}, bf16[8,128,128]{2...) custom-call(s32[16]{0:T(128)S(1)} %copy-done.3, ...), custom_call_target="tpu_custom_call", output_to_operand_aliasing={{0}: (9, {}), {1}: (10, {}), {2}: (11, {}), {3}: (12, {}), ... | custom-call | flops 104857600 | bytes 7340032 | tf_op jit(solution)/shard_map/pallas_call | solution.py:200
  77.9 0.5 collective-permute-start.11
  78.4 0.9 collective-permute-start.16
  79.3 0.9 collective-permute-done.11.sib.refs_1_
  80.2 0.3 shard_map.74
  80.5 0.7 collective-permute-start.15
  81.2 2.5 %collective-permute-start.12 = (bf16[6,128,128]{2,1,0:T(8,128)(2,1)S(1)}, bf16[6,128,128]{2,1,0:T(8,128)(2,1)S(1)}, u32[]{:S(2)}, u32[]{:S(2)}) collective-permute-start(bf16[6,128,128]{2,1,0:T(8,128)(2,1)S(1)} %slice.24), channel_id=1, source_target_pairs={{0,2},{1,3},{2,0},{3,1},{4,6},{5,7},{6,4},{7,5},{8,10},{9,11},{10,... | collective-permute-start | bytes 589832 | tf_op jit(solution)/shard_map/ppermute | solution.py:296
  83.7 1.9 %collective-permute-start.13 = (bf16[6,128,128]{2,1,0:T(8,128)(2,1)S(1)}, bf16[6,128,128]{2,1,0:T(8,128)(2,1)S(1)}, u32[]{:S(2)}, u32[]{:S(2)}) collective-permute-start(bf16[6,128,128]{2,1,0:T(8,128)(2,1)S(1)} %get-tuple-element.75), channel_id=1, source_target_pairs={{0,4},{1,5},{4,8},{5,9},{6,2},{7,3},{8,12},{9,13},{10,6},{11,7},{1... | collective-permute-start | bytes 589832 | tf_op jit(solution)/shard_map/ppermute | solution.py:296
  85.6 3.9 %collective-permute-start.14 = (bf16[8,128,128]{2,1,0:T(8,128)(2,1)S(1)}, bf16[8,128,128]{2,1,0:T(8,128)(2,1)S(1)}, u32[]{:S(2)}, u32[]{:S(2)}) collective-permute-start(bf16[8,128,128]{2,1,0:T(8,128)(2,1)S(1)} %get-tuple-element.76), channel_id=1, source_target_pairs={{2,4},{3,5},{4,2},{5,3},{6,8},{7,9},{8,6},{9,7},{10,12},{11,13},{1... | collective-permute-start | bytes 786440 | tf_op jit(solution)/shard_map/ppermute | solution.py:296
  89.5 1.1 %shard_map.75 = (f32[1,5,128,512]{3,2,1,0:T(8,128)}, f32[1,5,128,512]{3,2,1,0:T(8,128)}) custom-call(bf16[7,128,128]{2,1,0:T(8,128)(2,1)S(1)} %get-tuple-element.79.refs_0_, bf16[21,128,128]{2,1,0:T(8,128)(2,1)S(1)} %collective-permute-done.11.sib.refs_1_), custom_call_target="tpu_custom_call" | custom-call | flops 229376 | bytes 1376256 | tf_op jit(solution)/shard_map/pallas_call | solution.py:269
  90.6 0.0 collective-permute-done.16.refs_0_
  90.6 0.8 shard_map.76
  91.4 0.0 collective-permute-done.15.refs_3_
  91.4 0.0 collective-permute-done.12.refs_0_
  91.4 0.3 collective-permute-done.13.refs_1_
  91.8 5.5 %collective-permute-done.14.refs_2_ = bf16[8,128,128]{2,1,0:T(8,128)(2,1)S(1)} collective-permute-done((bf16[8,128,128]{2,1,0:T(8,128)(2,1)S(1)}, bf16[8,128,128]{2,1,0:T(8,128)(2,1)S(1)}, u32[]{:S(2)}, u32[]{:S(2)}) %collective-permute-start.14) | collective-permute-done | bytes 262176 | tf_op jit(solution)/shard_map/ppermute | solution.py:296
  97.3 1.2 %shard_map.77 = (f32[1,5,128,512]{3,2,1,0:T(8,128)}, f32[1,5,128,512]{3,2,1,0:T(8,128)}) custom-call(bf16[6,128,128]{2,1,0:T(8,128)(2,1)S(1)} %collective-permute-done.12.refs_0_, bf16[6,128,128]{2,1,0:T(8,128)(2,1)S(1)} %collective-permute-done.13.refs_1_, ...), custom_call_target="tpu_custom_call", output_to_operand_aliasing={{0}: (4, {}), {1}: (5, {})} | custom-call | flops 360448 | bytes 2162688 | tf_op jit(solution)/shard_map/pallas_call | solution.py:269
  (2 shorter events, 0.0 us)
Async XLA Ops:
  4.0 8.4 %copy-start.4 = (bf16[16,2,128,128]{3,2,1,0:T(8,128)(2,1)S(1)}, bf16[16,2,128,128]{3,2,1,0:T(8,128)(2,1)}, u32[]{:S(2)}) copy-start(bf16[16,2,128,128]{3,2,1,0:T(8,128)(2,1)} %get-tuple-element.57) | copy-start | bytes 3145732
  4.0 29.8 %copy-start.2 = (bf16[2,256,256]{2,1,0:T(8,128)(2,1)S(1)}, bf16[2,256,256]{2,1,0:T(8,128)(2,1)}, u32[]{:S(2)}) copy-start(bf16[2,256,256]{2,1,0:T(8,128)(2,1)} %constant.4.clone.table_ref) | copy-start | bytes 786436
  4.0 29.8 %copy-start.3 = (s32[16]{0:T(128)S(1)}, s32[16]{0:T(128)}, u32[]{:S(2)}) copy-start(s32[16]{0:T(128)} %counts_ref.7) | copy-start | bytes 196
  4.0 26.3 %collective-permute-start.1 = (bf16[16,2,128,128]{3,2,1,0:T(8,128)(2,1)}, bf16[16,2,128,128]{3,2,1,0:T(8,128)(2,1)S(1)}, u32[]{:S(2)}, u32[]{:S(2)}) collective-permute-start(bf16[16,2,128,128]{3,2,1,0:T(8,128)(2,1)} %get-tuple-element.43), channel_id=1, source_target_pairs={{0,2},{1,3},{2,0},{3,1},{4,6},{5,7},{6,4},{7,5},{8,10},{9,11},{10,... | collective-permute-start | bytes 3145736 | tf_op jit(solution)/shard_map/ppermute | solution.py:296
  9.2 21.2 %collective-permute-start = (bf16[16,2,128,128]{3,2,1,0:T(8,128)(2,1)}, bf16[16,2,128,128]{3,2,1,0:T(8,128)(2,1)S(1)}, u32[]{:S(2)}, u32[]{:S(2)}) collective-permute-start(bf16[16,2,128,128]{3,2,1,0:T(8,128)(2,1)} %get-tuple-element.46), channel_id=1, source_target_pairs={{0,1},{1,0},{2,3},{3,2},{4,5},{5,4},{6,7},{7,6},{8,9},{9,8},{10,11... | collective-permute-start | bytes 3145736 | tf_op jit(solution)/shard_map/ppermute | solution.py:296
  9.2 45.2 %collective-permute-start.9 = (bf16[32,2,128,128]{3,2,1,0:T(8,128)(2,1)}, bf16[32,2,128,128]{3,2,1,0:T(8,128)(2,1)S(1)}, u32[]{:S(2)}, u32[]{:S(2)}) collective-permute-start(bf16[32,2,128,128]{3,2,1,0:T(8,128)(2,1)} %get-tuple-element.45.refs_0_), channel_id=1, source_target_pairs={{1,5},{5,9},{6,2},{9,13},{10,6},{14,10},{17,21},{21,25},{22,18},{2... | collective-permute-start | bytes 6291464 | tf_op jit(solution)/shard_map/ppermute | solution.py:296
  10.0 48.6 %collective-permute-start.3 = (bf16[32,2,128,128]{3,2,1,0:T(8,128)(2,1)}, bf16[32,2,128,128]{3,2,1,0:T(8,128)(2,1)S(1)}, u32[]{:S(2)}, u32[]{:S(2)}) collective-permute-start(bf16[32,2,128,128]{3,2,1,0:T(8,128)(2,1)} %get-tuple-element.45.refs_0_), channel_id=1, source_target_pairs={{2,6},{3,7},{4,0},{5,1},{6,10},{7,11},{8,4},{9,5},{10,14},{11,15},... | collective-permute-start | bytes 6291464 | tf_op jit(solution)/shard_map/ppermute | solution.py:296
  12.4 38.3 %collective-permute-start.2 = (bf16[16,2,128,128]{3,2,1,0:T(8,128)(2,1)S(1)}, bf16[16,2,128,128]{3,2,1,0:T(8,128)(2,1)S(1)}, u32[]{:S(2)}, u32[]{:S(2)}) collective-permute-start(bf16[16,2,128,128]{3,2,1,0:T(8,128)(2,1)S(1)} %copy-done.4), channel_id=1, source_target_pairs={{0,3},{1,2},{2,1},{3,0},{4,7},{5,6},{6,5},{7,4},{8,11},{9,10},{10,... | collective-permute-start | bytes 3145736 | tf_op jit(solution)/shard_map/ppermute | solution.py:296
  30.4 30.7 %collective-permute-start.8 = (bf16[16,2,128,128]{3,2,1,0:T(8,128)(2,1)S(1)}, bf16[16,2,128,128]{3,2,1,0:T(8,128)(2,1)S(1)}, u32[]{:S(2)}, u32[]{:S(2)}) collective-permute-start(bf16[16,2,128,128]{3,2,1,0:T(8,128)(2,1)S(1)} %collective-permute-done.1.refs_2_), channel_id=1, source_target_pairs={{0,4},{1,5},{4,8},{5,9},{6,2},{7,3},{8,12},{9,13},{10,6},{11,7},{1... | collective-permute-start | bytes 3145736 | tf_op jit(solution)/shard_map/ppermute | solution.py:296
  33.9 1.6 %copy-start = (bf16[32,2,128,128]{3,2,1,0:T(8,128)(2,1)S(1)}, bf16[32,2,128,128]{3,2,1,0:T(8,128)(2,1)}, u32[]{:S(2)}) copy-start(bf16[32,2,128,128]{3,2,1,0:T(8,128)(2,1)} %get-tuple-element.45.refs_0_) | copy-start | bytes 6291460
  50.8 5.1 %copy-start.1 = (bf16[32,2,128,128]{3,2,1,0:T(8,128)(2,1)S(1)}, bf16[32,2,128,128]{3,2,1,0:T(8,128)(2,1)}, u32[]{:S(2)}) copy-start(bf16[32,2,128,128]{3,2,1,0:T(8,128)(2,1)} %get-tuple-element.45.refs_0_) | copy-start | bytes 6291460
  50.8 23.9 %collective-permute-start.4 = (bf16[10,2,128,128]{3,2,1,0:T(8,128)(2,1)S(1)}, bf16[10,2,128,128]{3,2,1,0:T(8,128)(2,1)S(1)}, u32[]{:S(2)}, u32[]{:S(2)}) collective-permute-start(bf16[10,2,128,128]{3,2,1,0:T(8,128)(2,1)S(1)} %slice.18), channel_id=1, source_target_pairs={{0,4},{1,5},{4,8},{5,9},{6,2},{7,3},{8,12},{9,13},{10,6},{11,7},{1... | collective-permute-start | bytes 1966088 | tf_op jit(solution)/shard_map/ppermute | solution.py:296
  54.5 8.7 %collective-permute-start.10 = (bf16[16,2,128,128]{3,2,1,0:T(8,128)(2,1)S(1)}, bf16[16,2,128,128]{3,2,1,0:T(8,128)(2,1)S(1)}, u32[]{:S(2)}, u32[]{:S(2)}) collective-permute-start(bf16[16,2,128,128]{3,2,1,0:T(8,128)(2,1)S(1)} %slice.22), channel_id=1, source_target_pairs={{1,0},{2,3},{5,4},{6,7},{9,8},{10,11},{13,12},{14,15},{17,16},{18,... | collective-permute-start | bytes 3145736 | tf_op jit(solution)/shard_map/ppermute | solution.py:296
  58.8 4.2 %collective-permute-start.7 = (bf16[8,2,128,128]{3,2,1,0:T(8,128)(2,1)S(1)}, bf16[8,2,128,128]{3,2,1,0:T(8,128)(2,1)S(1)}, u32[]{:S(2)}, u32[]{:S(2)}) collective-permute-start(bf16[8,2,128,128]{3,2,1,0:T(8,128)(2,1)S(1)} %get-tuple-element.84), channel_id=1, source_target_pairs={{0,1},{1,0},{2,3},{3,2},{4,5},{5,4},{6,7},{7,6},{8,9},{9,8},{10,11... | collective-permute-start | bytes 1572872 | tf_op jit(solution)/shard_map/ppermute | solution.py:296
  60.9 2.3 %collective-permute-start.6 = (bf16[8,2,128,128]{3,2,1,0:T(8,128)(2,1)S(1)}, bf16[8,2,128,128]{3,2,1,0:T(8,128)(2,1)S(1)}, u32[]{:S(2)}, u32[]{:S(2)}) collective-permute-start(bf16[8,2,128,128]{3,2,1,0:T(8,128)(2,1)S(1)} %get-tuple-element.85), channel_id=1, source_target_pairs={{0,1},{1,0},{2,3},{3,2},{4,5},{5,4},{6,7},{7,6},{8,9},{9,8},{10,11... | collective-permute-start | bytes 1572872 | tf_op jit(solution)/shard_map/ppermute | solution.py:296
  61.1 13.6 %collective-permute-start.5 = (bf16[6,2,128,128]{3,2,1,0:T(8,128)(2,1)S(1)}, bf16[6,2,128,128]{3,2,1,0:T(8,128)(2,1)S(1)}, u32[]{:S(2)}, u32[]{:S(2)}) collective-permute-start(bf16[6,2,128,128]{3,2,1,0:T(8,128)(2,1)S(1)} %slice.19), channel_id=1, source_target_pairs={{2,5},{3,4},{4,3},{5,2},{6,9},{7,8},{8,7},{9,6},{10,13},{11,12},{1... | collective-permute-start | bytes 1179656 | tf_op jit(solution)/shard_map/ppermute | solution.py:296
  77.9 2.2 %collective-permute-start.11 = (bf16[21,128,128]{2,1,0:T(8,128)(2,1)S(1)}, bf16[21,128,128]{2,1,0:T(8,128)(2,1)S(1)}, u32[]{:S(2)}, u32[]{:S(2)}) collective-permute-start(bf16[21,128,128]{2,1,0:T(8,128)(2,1)S(1)} %get-tuple-element.71), channel_id=1, source_target_pairs={{0,1},{1,0},{2,3},{3,2},{4,5},{5,4},{6,7},{7,6},{8,9},{9,8},{10,11... | collective-permute-start | bytes 2064392 | tf_op jit(solution)/shard_map/ppermute | solution.py:296
  78.4 12.2 %collective-permute-start.16 = (bf16[6,128,128]{2,1,0:T(8,128)(2,1)S(1)}, bf16[6,128,128]{2,1,0:T(8,128)(2,1)S(1)}, u32[]{:S(2)}, u32[]{:S(2)}) collective-permute-start(bf16[6,128,128]{2,1,0:T(8,128)(2,1)S(1)} %get-tuple-element.78), channel_id=1, source_target_pairs={{0,2},{1,3},{2,0},{3,1},{4,6},{5,7},{6,4},{7,5},{8,10},{9,11},{10,... | collective-permute-start | bytes 589832 | tf_op jit(solution)/shard_map/ppermute | solution.py:296
  80.5 10.9 %collective-permute-start.15 = (bf16[2,128,128]{2,1,0:T(8,128)(2,1)S(1)}, bf16[2,128,128]{2,1,0:T(8,128)(2,1)S(1)}, u32[]{:S(2)}, u32[]{:S(2)}) collective-permute-start(bf16[2,128,128]{2,1,0:T(8,128)(2,1)S(1)} %get-tuple-element.77), channel_id=1, source_target_pairs={{2,6},{5,1},{6,10},{9,5},{10,14},{13,9},{18,22},{21,17},{22,26},{2... | collective-permute-start | bytes 196616 | tf_op jit(solution)/shard_map/ppermute | solution.py:296
  81.2 10.2 %collective-permute-start.12 = (bf16[6,128,128]{2,1,0:T(8,128)(2,1)S(1)}, bf16[6,128,128]{2,1,0:T(8,128)(2,1)S(1)}, u32[]{:S(2)}, u32[]{:S(2)}) collective-permute-start(bf16[6,128,128]{2,1,0:T(8,128)(2,1)S(1)} %slice.24), channel_id=1, source_target_pairs={{0,2},{1,3},{2,0},{3,1},{4,6},{5,7},{6,4},{7,5},{8,10},{9,11},{10,... | collective-permute-start | bytes 589832 | tf_op jit(solution)/shard_map/ppermute | solution.py:296
  83.7 8.1 %collective-permute-start.13 = (bf16[6,128,128]{2,1,0:T(8,128)(2,1)S(1)}, bf16[6,128,128]{2,1,0:T(8,128)(2,1)S(1)}, u32[]{:S(2)}, u32[]{:S(2)}) collective-permute-start(bf16[6,128,128]{2,1,0:T(8,128)(2,1)S(1)} %get-tuple-element.75), channel_id=1, source_target_pairs={{0,4},{1,5},{4,8},{5,9},{6,2},{7,3},{8,12},{9,13},{10,6},{11,7},{1... | collective-permute-start | bytes 589832 | tf_op jit(solution)/shard_map/ppermute | solution.py:296
  85.6 11.7 %collective-permute-start.14 = (bf16[8,128,128]{2,1,0:T(8,128)(2,1)S(1)}, bf16[8,128,128]{2,1,0:T(8,128)(2,1)S(1)}, u32[]{:S(2)}, u32[]{:S(2)}) collective-permute-start(bf16[8,128,128]{2,1,0:T(8,128)(2,1)S(1)} %get-tuple-element.76), channel_id=1, source_target_pairs={{2,4},{3,5},{4,2},{5,3},{6,8},{7,9},{8,6},{9,7},{10,12},{11,13},{1... | collective-permute-start | bytes 786440 | tf_op jit(solution)/shard_map/ppermute | solution.py:296

commit v5 on v4

--- a/solution.py
+++ b/solution.py
@@ -125,12 +125,13 @@
 
 
 def relayed(windows):
-    return windows * 5 // 8
+    return windows * 11 // 16
 
 
 def correlate_body(counts_ref, table_ref, *refs, work, sources, filled):
-    ins, refs = refs[:len(refs) - 2 * len(DESTS) - 3 - filled], refs[len(refs) - 2 * len(DESTS) - 3:]
-    outs, stack, kept, out_sems = refs[:len(DESTS) + 1], refs[len(DESTS) + 1], refs[len(DESTS) + 2:-1], refs[-1]
+    count = len(DESTS) + 1
+    outs, stack = refs[-count - 1:-1], refs[-1]
+    held, ins = refs[len(refs) - count - 1 - filled:-count - 1], refs[:len(refs) - count - 1 - filled]
     windows, _, bins, part = ins[1].shape
     far, m, base, _ = whereabouts()
     blocks = counts_ref.shape[0]
@@ -158,7 +159,7 @@
                         out.append(sums[2 * n + 1] + (imag[a] * real[b] - real[a] * imag[b]))
                     return tuple(out)
 
-                sums = lax.fori_loop(0, stop - start, window, sums, unroll=math.gcd(stop - start, 8))
+                sums = lax.fori_loop(0, stop - start, window, sums, unroll=stop - start if stop - start <= 12 else 8)
             for n in range(len(group)):
                 lanes = pl.ds((at + n) * part, part)
                 stack[rows, lanes] = (sums[2 * n] * scale).astype(jnp.bfloat16)
@@ -170,7 +171,8 @@
     for mine in range(2):
         @pl.when(m == mine)
         def _(mine=mine):
-            copies = []
+            for out, old in zip(outs, held):
+                out[...] = old[...]
             for g, group in enumerate(work[mine]):
                 at = len(flat(work[mine][:g]))
                 sum_up(group, at, sources[mine])
@@ -182,32 +184,21 @@
                     for spot, kind, rows in ((a, "ahead", corr[:bins]), (b, "back", corr[bins:])):
                         d, i = PLACE[spot]
                         row = items(spot).index((kind, b - a - 1))
-                        kept[d][i, row] = rows.astype(jnp.bfloat16)
-                        target = outs[d].at[row] if i == mine else outs[-1].at[STARTS[d] + row]
-                        one = pltpu.make_async_copy(kept[d].at[i, row], target, out_sems.at[len(copies)])
-                        one.start()
-                        copies.append(one)
-            for one in copies:
-                one.wait()
+                        out, row = (outs[d], row) if i == mine else (outs[-1], STARTS[d] + row)
+                        out[row] = rows.astype(jnp.bfloat16)
 
 
 def correlate(counts, tables, whites, work, sources, filled=(), weight=1):
     windows, _, bins, part = whites[1].shape
     most = max(len(flat(groups)) for groups in work)
-    anywhere = pl.BlockSpec(memory_space=pl.ANY)
     scalars = pl.BlockSpec(memory_space=pltpu.SMEM)
     lengths = [size * (2 if d in MERGED else 1) for d, size in enumerate(SIZES)] + [sum(SIZES)]
     return pl.pallas_call(
         functools.partial(correlate_body, work=work, sources=sources, filled=len(filled)),
-        in_specs=[scalars] + [pl.BlockSpec(memory_space=pltpu.VMEM)] * (1 + len(whites)) + [anywhere] * len(filled),
-        out_specs=[anywhere] * len(lengths),
+        in_specs=[scalars] + [pl.BlockSpec(memory_space=pltpu.VMEM)] * (1 + len(whites) + len(filled)),
+        out_specs=[pl.BlockSpec(memory_space=pltpu.VMEM)] * len(lengths),
         out_shape=[jax.ShapeDtypeStruct((n, bins, part), jnp.bfloat16) for n in lengths],
-        scratch_shapes=[
-            pltpu.VMEM((2 * bins, most * part), jnp.bfloat16),
-            *[pltpu.VMEM((2, size, bins, part), jnp.bfloat16) for size in SIZES],
-            pltpu.SemaphoreType.DMA((2 * most,)),
-        ],
-        input_output_aliases={2 + len(whites) + i: i for i in range(len(filled))},
+        scratch_shapes=[pltpu.VMEM((2 * bins, most * part), jnp.bfloat16)],
         compiler_params=pltpu.CompilerParams(vmem_limit_bytes=12 * MIB),
         cost_estimate=pl.CostEstimate(flops=weight * 100 * most * windows * bins * part, bytes_accessed=min(weight, 1) * 4 * len(whites) * windows * bins * part, transcendentals=0),
     )(counts, tables, *whites, *filled)
@@ -348,7 +339,7 @@
 
     shape = (MAXP, lags // 2, width)
     filled = assemble((keep, sib), shape, [[(0, 0, mine, 0), (1, 1, mine, 0)] for mine in range(2)])
-    filled = assemble((near,), shape, [[(0, 2, 3 - mine, 0)] for mine in range(2)], filled, weight=50000)
+    filled = assemble((near,), shape, [[(0, 2, 3 - mine, 0)] for mine in range(2)], filled, weight=12000)
     return tuple(assemble((rest, x, v, w), shape, [
         [(0, 3, 3 - mine, 0), (1, 0, 4 + mine, 0), (1, 1, 4 + mine, SIZES[2]),
          (2, 2, -1 - mine, 0), (2, 3, -1 - mine, SIZES[3])] + inner

time: 99 us -> 96.9 us (0.979)
  Pallas kernels: 25 us -> 22.7 us
    pallas_call x4, Pallas kernels: 14.6 us -> 12.4 us  [correlate(): pl.pallas_call(functools.partial(correlate_body, work=work, sources=sourc...]
  transfers between devices with their start and end apart: 17 -> 17, of which waited for: 8 -> 8; matrix products, arithmetic and copies ran while one was open for 0% -> 0% of each run, Pallas kernels for 17% -> 16%
where the time goes in v5:
time: 96.9 us; the launch traced here: 96.2 us
  waiting for transfers between devices  42.1 us (43%)
  starting transfers between devices  28.6 us (30%)
  Pallas kernels  22.7 us (23%)
  local copies, waits for them, and re-layouts  1.91 us (2%)
    ppermute x17, waiting for transfers between devices, send(): return lax.ppermute(value, 'chan', pairs)  42.1 us
    ppermute x17, starting transfers between devices, send(): return lax.ppermute(value, 'chan', pairs)  28.6 us
    pallas_call x4, Pallas kernels, correlate(): pl.pallas_call(functools.partial(correlate_body, work=work, sources=sourc...  12.4 us
    pallas_call x2, Pallas kernels, whiten(): pl.pallas_call(whiten_body, grid=(windows // STEP,), in_specs=[pl.BlockSp...  6.89 us
    pallas_call x3, Pallas kernels, assemble(): pl.pallas_call(functools.partial(assemble_body, plan=plan, count=len(part...  3.1 us
  transfers between devices with their start and end apart: 17, of which 8 were waited for; matrix products, arithmetic and copies ran while one was open for 0% of the time, Pallas kernels for 16%

profile of v5, /device:TPU:16, one launch (start us, length us, event | category | flops | bytes accessed | tf_op | source)
XLA Modules:
  0.0 96.2 jit_solution(14742823947906333425)
XLA Ops:
  0.6 3.4 %shard_map.68 = (bf16[16,2,128,128]{3,2,1,0:T(8,128)(2,1)}, bf16[16,2,128,128]{3,2,1,0:T(8,128)(2,1)}) custom-call(s32[16,16]{1,0:T(8,128)} %mask_ref.2, bf16[256,256]{1,0:T(8,128)(2,1)} %constant.5.clone.table_ref, bf16[1,16,256,512]{3,2,1,0:T(8,128)(2,1)} %traces_ref.3), custom_call_target="tpu_custom_call" | custom-call | flops 536870912 | bytes 4194304 | tf_op jit(solution)/shard_map/pallas_call | solution.py:108
  4.0 0.0 copy-start.4
  4.0 0.0 copy-start.2
  4.0 0.0 copy-start.3
  4.0 1.6 %collective-permute-start.1 = (bf16[16,2,128,128]{3,2,1,0:T(8,128)(2,1)}, bf16[16,2,128,128]{3,2,1,0:T(8,128)(2,1)S(1)}, u32[]{:S(2)}, u32[]{:S(2)}) collective-permute-start(bf16[16,2,128,128]{3,2,1,0:T(8,128)(2,1)} %get-tuple-element.43), channel_id=1, source_target_pairs={{0,2},{1,3},{2,0},{3,1},{4,6},{5,7},{6,4},{7,5},{8,10},{9,11},{10,... | collective-permute-start | bytes 3145736 | tf_op jit(solution)/shard_map/ppermute | solution.py:287
  5.6 3.5 %shard_map.69 = (bf16[32,2,128,128]{3,2,1,0:T(8,128)(2,1)}, bf16[16,2,128,128]{3,2,1,0:T(8,128)(2,1)}) custom-call(s32[16,16]{1,0:T(8,128)} %mask_ref.2, bf16[256,256]{1,0:T(8,128)(2,1)} %constant.5.clone.table_ref, bf16[1,16,256,512]{3,2,1,0:T(8,128)(2,1)} %traces_ref.3), custom_call_target="tpu_custom_call" | custom-call | flops 536870912 | bytes 4194304 | tf_op jit(solution)/shard_map/pallas_call | solution.py:108
  9.2 0.1 collective-permute-start
  9.2 0.8 collective-permute-start.9
  10.0 2.4 %collective-permute-start.3 = (bf16[32,2,128,128]{3,2,1,0:T(8,128)(2,1)}, bf16[32,2,128,128]{3,2,1,0:T(8,128)(2,1)S(1)}, u32[]{:S(2)}, u32[]{:S(2)}) collective-permute-start(bf16[32,2,128,128]{3,2,1,0:T(8,128)(2,1)} %get-tuple-element.45.refs_0_), channel_id=1, source_target_pairs={{2,6},{3,7},{4,0},{5,1},{6,10},{7,11},{8,4},{9,5},{10,14},{11,15},... | collective-permute-start | bytes 6291464 | tf_op jit(solution)/shard_map/ppermute | solution.py:287
  12.4 0.0 copy-done.4
  12.4 1.5 %collective-permute-start.2 = (bf16[16,2,128,128]{3,2,1,0:T(8,128)(2,1)S(1)}, bf16[16,2,128,128]{3,2,1,0:T(8,128)(2,1)S(1)}, u32[]{:S(2)}, u32[]{:S(2)}) collective-permute-start(bf16[16,2,128,128]{3,2,1,0:T(8,128)(2,1)S(1)} %copy-done.4), channel_id=1, source_target_pairs={{0,3},{1,2},{2,1},{3,0},{4,7},{5,6},{6,5},{7,4},{8,11},{9,10},{10,... | collective-permute-start | bytes 3145736 | tf_op jit(solution)/shard_map/ppermute | solution.py:287
  13.9 16.4 %collective-permute-done.1.refs_2_ = bf16[16,2,128,128]{3,2,1,0:T(8,128)(2,1)S(1)} collective-permute-done((bf16[16,2,128,128]{3,2,1,0:T(8,128)(2,1)}, bf16[16,2,128,128]{3,2,1,0:T(8,128)(2,1)S(1)}, u32[]{:S(2)}, u32[]{:S(2)}) %collective-permute-start.1) | collective-permute-done | bytes 1048608 | tf_op jit(solution)/shard_map/ppermute | solution.py:287
  30.4 0.0 collective-permute-done.refs_1_
  30.4 3.5 %collective-permute-start.8 = (bf16[16,2,128,128]{3,2,1,0:T(8,128)(2,1)S(1)}, bf16[16,2,128,128]{3,2,1,0:T(8,128)(2,1)S(1)}, u32[]{:S(2)}, u32[]{:S(2)}) collective-permute-start(bf16[16,2,128,128]{3,2,1,0:T(8,128)(2,1)S(1)} %collective-permute-done.1.refs_2_), channel_id=1, source_target_pairs={{0,4},{1,5},{4,8},{5,9},{6,2},{7,3},{8,12},{9,13},{10,6},{11,7},{1... | collective-permute-start | bytes 3145736 | tf_op jit(solution)/shard_map/ppermute | solution.py:287
  33.8 0.0 copy-done.2
  33.9 0.0 copy-done.3
  33.9 0.0 copy-start
  33.9 1.6 %copy-done = bf16[32,2,128,128]{3,2,1,0:T(8,128)(2,1)S(1)} copy-done((bf16[32,2,128,128]{3,2,1,0:T(8,128)(2,1)S(1)}, bf16[32,2,128,128]{3,2,1,0:T(8,128)(2,1)}, u32[]{:S(2)}) %copy-start) | copy-done | bytes 2097176
  35.5 1.9 %shard_map.70 = (bf16[7,128,128]{2,1,0:T(8,128)(2,1)S(1)}, bf16[6,128,128]{2,1,0:T(8,128)(2,1)S(1)}, bf16[6,128,128]{2,1,0:T(8,128)(2,1)S(1)}, bf16[8,128,128]{2...) custom-call(s32[16]{0:T(128)S(1)} %copy-done.3, ...), custom_call_target="tpu_custom_call" | custom-call | flops 15728640000 | bytes 3145728 | tf_op jit(solution)/shard_map/pallas_call | solution.py:196
  37.4 13.3 %collective-permute-done.2.refs_3_ = bf16[16,2,128,128]{3,2,1,0:T(8,128)(2,1)S(1)} collective-permute-done((bf16[16,2,128,128]{3,2,1,0:T(8,128)(2,1)S(1)}, bf16[16,2,128,128]{3,2,1,0:T(8,128)(2,1)S(1)}, u32[]{:S(2)}, u32[]{:S(2)}) %collective-permute-start.2) | collective-permute-done | bytes 1048608 | tf_op jit(solution)/shard_map/ppermute | solution.py:287
  50.7 0.1 slice.18
  50.8 0.0 copy-start.1
  50.8 3.6 %collective-permute-start.4 = (bf16[11,2,128,128]{3,2,1,0:T(8,128)(2,1)S(1)}, bf16[11,2,128,128]{3,2,1,0:T(8,128)(2,1)S(1)}, u32[]{:S(2)}, u32[]{:S(2)}) collective-permute-start(bf16[11,2,128,128]{3,2,1,0:T(8,128)(2,1)S(1)} %slice.18), channel_id=1, source_target_pairs={{0,4},{1,5},{4,8},{5,9},{6,2},{7,3},{8,12},{9,13},{10,6},{11,7},{1... | collective-permute-start | bytes 2162696 | tf_op jit(solution)/shard_map/ppermute | solution.py:287
  54.4 0.0 collective-permute-done.9.refs_9_
  54.4 0.1 slice.22
  54.6 1.3 %collective-permute-start.10 = (bf16[16,2,128,128]{3,2,1,0:T(8,128)(2,1)S(1)}, bf16[16,2,128,128]{3,2,1,0:T(8,128)(2,1)S(1)}, u32[]{:S(2)}, u32[]{:S(2)}) collective-permute-start(bf16[16,2,128,128]{3,2,1,0:T(8,128)(2,1)S(1)} %slice.22), channel_id=1, source_target_pairs={{1,0},{2,3},{5,4},{6,7},{9,8},{10,11},{13,12},{14,15},{17,16},{18,... | collective-permute-start | bytes 3145736 | tf_op jit(solution)/shard_map/ppermute | solution.py:287
  55.9 0.0 copy-done.1
  55.9 2.2 %shard_map.71 = (bf16[7,128,128]{2,1,0:T(8,128)(2,1)S(1)}, bf16[6,128,128]{2,1,0:T(8,128)(2,1)S(1)}, bf16[6,128,128]{2,1,0:T(8,128)(2,1)S(1)}, bf16[8,128,128]{2...) custom-call(s32[16]{0:T(128)S(1)} %copy-done.3, ...), custom_call_target="tpu_custom_call" | custom-call | flops 15728640000 | bytes 4194304 | tf_op jit(solution)/shard_map/pallas_call | solution.py:196
  58.0 0.6 collective-permute-done.3.refs_4_
  58.7 0.1 fusion
  58.8 2.2 %collective-permute-start.7 = (bf16[8,2,128,128]{3,2,1,0:T(8,128)(2,1)S(1)}, bf16[8,2,128,128]{3,2,1,0:T(8,128)(2,1)S(1)}, u32[]{:S(2)}, u32[]{:S(2)}) collective-permute-start(bf16[8,2,128,128]{3,2,1,0:T(8,128)(2,1)S(1)} %get-tuple-element.84), channel_id=1, source_target_pairs={{0,1},{1,0},{2,3},{3,2},{4,5},{5,4},{6,7},{7,6},{8,9},{9,8},{10,11... | collective-permute-start | bytes 1572872 | tf_op jit(solution)/shard_map/ppermute | solution.py:287
  60.9 0.1 collective-permute-start.6
  61.0 0.0 collective-permute-done.8.refs_7_
  61.1 1.9 %collective-permute-start.5 = (bf16[5,2,128,128]{3,2,1,0:T(8,128)(2,1)S(1)}, bf16[5,2,128,128]{3,2,1,0:T(8,128)(2,1)S(1)}, u32[]{:S(2)}, u32[]{:S(2)}) collective-permute-start(bf16[5,2,128,128]{3,2,1,0:T(8,128)(2,1)S(1)} %slice.19), channel_id=1, source_target_pairs={{2,5},{3,4},{4,3},{5,2},{6,9},{7,8},{8,7},{9,6},{10,13},{11,12},{1... | collective-permute-start | bytes 983048 | tf_op jit(solution)/shard_map/ppermute | solution.py:287
  63.0 0.0 collective-permute-done.7.refs_6_
  63.0 0.2 collective-permute-done.6.refs_5_
  63.2 0.0 collective-permute-done.10.refs_8_
  63.2 5.7 %shard_map.72 = (bf16[7,128,128]{2,1,0:T(8,128)(2,1)S(1)}, bf16[6,128,128]{2,1,0:T(8,128)(2,1)S(1)}, bf16[6,128,128]{2,1,0:T(8,128)(2,1)S(1)}, bf16[8,128,128]{2...) custom-call(s32[16]{0:T(128)S(1)} %copy-done.3, ...), custom_call_target="tpu_custom_call" | custom-call | tf_op jit(solution)/shard_map/pallas_call | solution.py:196
  68.9 4.4 %collective-permute-done.5.refs_6_ = bf16[5,2,128,128]{3,2,1,0:T(8,128)(2,1)S(1)} collective-permute-done((bf16[5,2,128,128]{3,2,1,0:T(8,128)(2,1)S(1)}, bf16[5,2,128,128]{3,2,1,0:T(8,128)(2,1)S(1)}, u32[]{:S(2)}, u32[]{:S(2)}) %collective-permute-start.5) | collective-permute-done | bytes 327712 | tf_op jit(solution)/shard_map/ppermute | solution.py:287
  73.3 0.5 collective-permute-done.4.refs_5_
  73.8 2.6 %shard_map.73 = (bf16[7,128,128]{2,1,0:T(8,128)(2,1)S(1)}, bf16[6,128,128]{2,1,0:T(8,128)(2,1)S(1)}, bf16[6,128,128]{2,1,0:T(8,128)(2,1)S(1)}, bf16[8,128,128]{2...) custom-call(s32[16]{0:T(128)S(1)} %copy-done.3, ...), custom_call_target="tpu_custom_call" | custom-call | flops 104857600 | bytes 7340032 | tf_op jit(solution)/shard_map/pallas_call | solution.py:196
  76.4 0.9 collective-permute-start.11
  77.3 1.2 %collective-permute-start.16 = (bf16[6,128,128]{2,1,0:T(8,128)(2,1)S(1)}, bf16[6,128,128]{2,1,0:T(8,128)(2,1)S(1)}, u32[]{:S(2)}, u32[]{:S(2)}) collective-permute-start(bf16[6,128,128]{2,1,0:T(8,128)(2,1)S(1)} %get-tuple-element.78), channel_id=1, source_target_pairs={{0,2},{1,3},{2,0},{3,1},{4,6},{5,7},{6,4},{7,5},{8,10},{9,11},{10,... | collective-permute-start | bytes 589832 | tf_op jit(solution)/shard_map/ppermute | solution.py:287
  78.5 0.5 collective-permute-done.11.sib.refs_1_
  79.0 0.3 shard_map.74
  79.4 3.3 %collective-permute-start.14 = (bf16[8,128,128]{2,1,0:T(8,128)(2,1)S(1)}, bf16[8,128,128]{2,1,0:T(8,128)(2,1)S(1)}, u32[]{:S(2)}, u32[]{:S(2)}) collective-permute-start(bf16[8,128,128]{2,1,0:T(8,128)(2,1)S(1)} %get-tuple-element.76), channel_id=1, source_target_pairs={{2,4},{3,5},{4,2},{5,3},{6,8},{7,9},{8,6},{9,7},{10,12},{11,13},{1... | collective-permute-start | bytes 786440 | tf_op jit(solution)/shard_map/ppermute | solution.py:287
  82.8 1.7 %collective-permute-start.12 = (bf16[6,128,128]{2,1,0:T(8,128)(2,1)S(1)}, bf16[6,128,128]{2,1,0:T(8,128)(2,1)S(1)}, u32[]{:S(2)}, u32[]{:S(2)}) collective-permute-start(bf16[6,128,128]{2,1,0:T(8,128)(2,1)S(1)} %slice.24), channel_id=1, source_target_pairs={{0,2},{1,3},{2,0},{3,1},{4,6},{5,7},{6,4},{7,5},{8,10},{9,11},{10,... | collective-permute-start | bytes 589832 | tf_op jit(solution)/shard_map/ppermute | solution.py:287
  84.5 1.9 %collective-permute-start.13 = (bf16[6,128,128]{2,1,0:T(8,128)(2,1)S(1)}, bf16[6,128,128]{2,1,0:T(8,128)(2,1)S(1)}, u32[]{:S(2)}, u32[]{:S(2)}) collective-permute-start(bf16[6,128,128]{2,1,0:T(8,128)(2,1)S(1)} %get-tuple-element.75), channel_id=1, source_target_pairs={{0,4},{1,5},{4,8},{5,9},{6,2},{7,3},{8,12},{9,13},{10,6},{11,7},{1... | collective-permute-start | bytes 589832 | tf_op jit(solution)/shard_map/ppermute | solution.py:287
  86.4 0.7 collective-permute-start.15
  87.0 1.1 %shard_map.75 = (f32[1,5,128,512]{3,2,1,0:T(8,128)}, f32[1,5,128,512]{3,2,1,0:T(8,128)}) custom-call(bf16[7,128,128]{2,1,0:T(8,128)(2,1)S(1)} %get-tuple-element.79.refs_0_, bf16[21,128,128]{2,1,0:T(8,128)(2,1)S(1)} %collective-permute-done.11.sib.refs_1_), custom_call_target="tpu_custom_call" | custom-call | flops 229376 | bytes 1376256 | tf_op jit(solution)/shard_map/pallas_call | solution.py:260
  88.1 0.0 collective-permute-done.16.refs_0_
  88.1 0.8 shard_map.76
  88.9 0.0 collective-permute-done.15.refs_3_
  89.0 6.0 %collective-permute-done.12.refs_0_ = bf16[6,128,128]{2,1,0:T(8,128)(2,1)S(1)} collective-permute-done((bf16[6,128,128]{2,1,0:T(8,128)(2,1)S(1)}, bf16[6,128,128]{2,1,0:T(8,128)(2,1)S(1)}, u32[]{:S(2)}, u32[]{:S(2)}) %collective-permute-start.12) | collective-permute-done | bytes 196640 | tf_op jit(solution)/shard_map/ppermute | solution.py:287
  95.0 0.0 collective-permute-done.13.refs_1_
  95.0 0.0 collective-permute-done.14.refs_2_
  95.0 1.2 %shard_map.77 = (f32[1,5,128,512]{3,2,1,0:T(8,128)}, f32[1,5,128,512]{3,2,1,0:T(8,128)}) custom-call(bf16[6,128,128]{2,1,0:T(8,128)(2,1)S(1)} %collective-permute-done.12.refs_0_, bf16[6,128,128]{2,1,0:T(8,128)(2,1)S(1)} %collective-permute-done.13.refs_1_, ...), custom_call_target="tpu_custom_call", output_to_operand_aliasing={{0}: (4, {}), {1}: (5, {})} | custom-call | flops 360448 | bytes 2162688 | tf_op jit(solution)/shard_map/pallas_call | solution.py:260
  (2 shorter events, 0.0 us)
Async XLA Ops:
  4.0 8.4 %copy-start.4 = (bf16[16,2,128,128]{3,2,1,0:T(8,128)(2,1)S(1)}, bf16[16,2,128,128]{3,2,1,0:T(8,128)(2,1)}, u32[]{:S(2)}) copy-start(bf16[16,2,128,128]{3,2,1,0:T(8,128)(2,1)} %get-tuple-element.57) | copy-start | bytes 3145732
  4.0 29.8 %copy-start.2 = (bf16[2,256,256]{2,1,0:T(8,128)(2,1)S(1)}, bf16[2,256,256]{2,1,0:T(8,128)(2,1)}, u32[]{:S(2)}) copy-start(bf16[2,256,256]{2,1,0:T(8,128)(2,1)} %constant.4.clone.table_ref) | copy-start | bytes 786436
  4.0 29.8 %copy-start.3 = (s32[16]{0:T(128)S(1)}, s32[16]{0:T(128)}, u32[]{:S(2)}) copy-start(s32[16]{0:T(128)} %counts_ref.7) | copy-start | bytes 196
  4.0 26.3 %collective-permute-start.1 = (bf16[16,2,128,128]{3,2,1,0:T(8,128)(2,1)}, bf16[16,2,128,128]{3,2,1,0:T(8,128)(2,1)S(1)}, u32[]{:S(2)}, u32[]{:S(2)}) collective-permute-start(bf16[16,2,128,128]{3,2,1,0:T(8,128)(2,1)} %get-tuple-element.43), channel_id=1, source_target_pairs={{0,2},{1,3},{2,0},{3,1},{4,6},{5,7},{6,4},{7,5},{8,10},{9,11},{10,... | collective-permute-start | bytes 3145736 | tf_op jit(solution)/shard_map/ppermute | solution.py:287
  9.2 21.2 %collective-permute-start = (bf16[16,2,128,128]{3,2,1,0:T(8,128)(2,1)}, bf16[16,2,128,128]{3,2,1,0:T(8,128)(2,1)S(1)}, u32[]{:S(2)}, u32[]{:S(2)}) collective-permute-start(bf16[16,2,128,128]{3,2,1,0:T(8,128)(2,1)} %get-tuple-element.46), channel_id=1, source_target_pairs={{0,1},{1,0},{2,3},{3,2},{4,5},{5,4},{6,7},{7,6},{8,9},{9,8},{10,11... | collective-permute-start | bytes 3145736 | tf_op jit(solution)/shard_map/ppermute | solution.py:287
  9.2 45.2 %collective-permute-start.9 = (bf16[32,2,128,128]{3,2,1,0:T(8,128)(2,1)}, bf16[32,2,128,128]{3,2,1,0:T(8,128)(2,1)S(1)}, u32[]{:S(2)}, u32[]{:S(2)}) collective-permute-start(bf16[32,2,128,128]{3,2,1,0:T(8,128)(2,1)} %get-tuple-element.45.refs_0_), channel_id=1, source_target_pairs={{1,5},{5,9},{6,2},{9,13},{10,6},{14,10},{17,21},{21,25},{22,18},{2... | collective-permute-start | bytes 6291464 | tf_op jit(solution)/shard_map/ppermute | solution.py:287
  10.0 48.6 %collective-permute-start.3 = (bf16[32,2,128,128]{3,2,1,0:T(8,128)(2,1)}, bf16[32,2,128,128]{3,2,1,0:T(8,128)(2,1)S(1)}, u32[]{:S(2)}, u32[]{:S(2)}) collective-permute-start(bf16[32,2,128,128]{3,2,1,0:T(8,128)(2,1)} %get-tuple-element.45.refs_0_), channel_id=1, source_target_pairs={{2,6},{3,7},{4,0},{5,1},{6,10},{7,11},{8,4},{9,5},{10,14},{11,15},... | collective-permute-start | bytes 6291464 | tf_op jit(solution)/shard_map/ppermute | solution.py:287
  12.4 38.3 %collective-permute-start.2 = (bf16[16,2,128,128]{3,2,1,0:T(8,128)(2,1)S(1)}, bf16[16,2,128,128]{3,2,1,0:T(8,128)(2,1)S(1)}, u32[]{:S(2)}, u32[]{:S(2)}) collective-permute-start(bf16[16,2,128,128]{3,2,1,0:T(8,128)(2,1)S(1)} %copy-done.4), channel_id=1, source_target_pairs={{0,3},{1,2},{2,1},{3,0},{4,7},{5,6},{6,5},{7,4},{8,11},{9,10},{10,... | collective-permute-start | bytes 3145736 | tf_op jit(solution)/shard_map/ppermute | solution.py:287
  30.4 30.7 %collective-permute-start.8 = (bf16[16,2,128,128]{3,2,1,0:T(8,128)(2,1)S(1)}, bf16[16,2,128,128]{3,2,1,0:T(8,128)(2,1)S(1)}, u32[]{:S(2)}, u32[]{:S(2)}) collective-permute-start(bf16[16,2,128,128]{3,2,1,0:T(8,128)(2,1)S(1)} %collective-permute-done.1.refs_2_), channel_id=1, source_target_pairs={{0,4},{1,5},{4,8},{5,9},{6,2},{7,3},{8,12},{9,13},{10,6},{11,7},{1... | collective-permute-start | bytes 3145736 | tf_op jit(solution)/shard_map/ppermute | solution.py:287
  33.9 1.6 %copy-start = (bf16[32,2,128,128]{3,2,1,0:T(8,128)(2,1)S(1)}, bf16[32,2,128,128]{3,2,1,0:T(8,128)(2,1)}, u32[]{:S(2)}) copy-start(bf16[32,2,128,128]{3,2,1,0:T(8,128)(2,1)} %get-tuple-element.45.refs_0_) | copy-start | bytes 6291460
  50.8 5.1 %copy-start.1 = (bf16[32,2,128,128]{3,2,1,0:T(8,128)(2,1)S(1)}, bf16[32,2,128,128]{3,2,1,0:T(8,128)(2,1)}, u32[]{:S(2)}) copy-start(bf16[32,2,128,128]{3,2,1,0:T(8,128)(2,1)} %get-tuple-element.45.refs_0_) | copy-start | bytes 6291460
  50.8 23.0 %collective-permute-start.4 = (bf16[11,2,128,128]{3,2,1,0:T(8,128)(2,1)S(1)}, bf16[11,2,128,128]{3,2,1,0:T(8,128)(2,1)S(1)}, u32[]{:S(2)}, u32[]{:S(2)}) collective-permute-start(bf16[11,2,128,128]{3,2,1,0:T(8,128)(2,1)S(1)} %slice.18), channel_id=1, source_target_pairs={{0,4},{1,5},{4,8},{5,9},{6,2},{7,3},{8,12},{9,13},{10,6},{11,7},{1... | collective-permute-start | bytes 2162696 | tf_op jit(solution)/shard_map/ppermute | solution.py:287
  54.6 8.7 %collective-permute-start.10 = (bf16[16,2,128,128]{3,2,1,0:T(8,128)(2,1)S(1)}, bf16[16,2,128,128]{3,2,1,0:T(8,128)(2,1)S(1)}, u32[]{:S(2)}, u32[]{:S(2)}) collective-permute-start(bf16[16,2,128,128]{3,2,1,0:T(8,128)(2,1)S(1)} %slice.22), channel_id=1, source_target_pairs={{1,0},{2,3},{5,4},{6,7},{9,8},{10,11},{13,12},{14,15},{17,16},{18,... | collective-permute-start | bytes 3145736 | tf_op jit(solution)/shard_map/ppermute | solution.py:287
  58.8 4.2 %collective-permute-start.7 = (bf16[8,2,128,128]{3,2,1,0:T(8,128)(2,1)S(1)}, bf16[8,2,128,128]{3,2,1,0:T(8,128)(2,1)S(1)}, u32[]{:S(2)}, u32[]{:S(2)}) collective-permute-start(bf16[8,2,128,128]{3,2,1,0:T(8,128)(2,1)S(1)} %get-tuple-element.84), channel_id=1, source_target_pairs={{0,1},{1,0},{2,3},{3,2},{4,5},{5,4},{6,7},{7,6},{8,9},{9,8},{10,11... | collective-permute-start | bytes 1572872 | tf_op jit(solution)/shard_map/ppermute | solution.py:287
  60.9 2.3 %collective-permute-start.6 = (bf16[8,2,128,128]{3,2,1,0:T(8,128)(2,1)S(1)}, bf16[8,2,128,128]{3,2,1,0:T(8,128)(2,1)S(1)}, u32[]{:S(2)}, u32[]{:S(2)}) collective-permute-start(bf16[8,2,128,128]{3,2,1,0:T(8,128)(2,1)S(1)} %get-tuple-element.85), channel_id=1, source_target_pairs={{0,1},{1,0},{2,3},{3,2},{4,5},{5,4},{6,7},{7,6},{8,9},{9,8},{10,11... | collective-permute-start | bytes 1572872 | tf_op jit(solution)/shard_map/ppermute | solution.py:287
  61.1 12.2 %collective-permute-start.5 = (bf16[5,2,128,128]{3,2,1,0:T(8,128)(2,1)S(1)}, bf16[5,2,128,128]{3,2,1,0:T(8,128)(2,1)S(1)}, u32[]{:S(2)}, u32[]{:S(2)}) collective-permute-start(bf16[5,2,128,128]{3,2,1,0:T(8,128)(2,1)S(1)} %slice.19), channel_id=1, source_target_pairs={{2,5},{3,4},{4,3},{5,2},{6,9},{7,8},{8,7},{9,6},{10,13},{11,12},{1... | collective-permute-start | bytes 983048 | tf_op jit(solution)/shard_map/ppermute | solution.py:287
  76.4 2.7 %collective-permute-start.11 = (bf16[21,128,128]{2,1,0:T(8,128)(2,1)S(1)}, bf16[21,128,128]{2,1,0:T(8,128)(2,1)S(1)}, u32[]{:S(2)}, u32[]{:S(2)}) collective-permute-start(bf16[21,128,128]{2,1,0:T(8,128)(2,1)S(1)} %get-tuple-element.71), channel_id=1, source_target_pairs={{0,1},{1,0},{2,3},{3,2},{4,5},{5,4},{6,7},{7,6},{8,9},{9,8},{10,11... | collective-permute-start | bytes 2064392 | tf_op jit(solution)/shard_map/ppermute | solution.py:287
  77.3 10.8 %collective-permute-start.16 = (bf16[6,128,128]{2,1,0:T(8,128)(2,1)S(1)}, bf16[6,128,128]{2,1,0:T(8,128)(2,1)S(1)}, u32[]{:S(2)}, u32[]{:S(2)}) collective-permute-start(bf16[6,128,128]{2,1,0:T(8,128)(2,1)S(1)} %get-tuple-element.78), channel_id=1, source_target_pairs={{0,2},{1,3},{2,0},{3,1},{4,6},{5,7},{6,4},{7,5},{8,10},{9,11},{10,... | collective-permute-start | bytes 589832 | tf_op jit(solution)/shard_map/ppermute | solution.py:287
  79.4 15.6 %collective-permute-start.14 = (bf16[8,128,128]{2,1,0:T(8,128)(2,1)S(1)}, bf16[8,128,128]{2,1,0:T(8,128)(2,1)S(1)}, u32[]{:S(2)}, u32[]{:S(2)}) collective-permute-start(bf16[8,128,128]{2,1,0:T(8,128)(2,1)S(1)} %get-tuple-element.76), channel_id=1, source_target_pairs={{2,4},{3,5},{4,2},{5,3},{6,8},{7,9},{8,6},{9,7},{10,12},{11,13},{1... | collective-permute-start | bytes 786440 | tf_op jit(solution)/shard_map/ppermute | solution.py:287
  82.8 12.2 %collective-permute-start.12 = (bf16[6,128,128]{2,1,0:T(8,128)(2,1)S(1)}, bf16[6,128,128]{2,1,0:T(8,128)(2,1)S(1)}, u32[]{:S(2)}, u32[]{:S(2)}) collective-permute-start(bf16[6,128,128]{2,1,0:T(8,128)(2,1)S(1)} %slice.24), channel_id=1, source_target_pairs={{0,2},{1,3},{2,0},{3,1},{4,6},{5,7},{6,4},{7,5},{8,10},{9,11},{10,... | collective-permute-start | bytes 589832 | tf_op jit(solution)/shard_map/ppermute | solution.py:287
  84.5 10.5 %collective-permute-start.13 = (bf16[6,128,128]{2,1,0:T(8,128)(2,1)S(1)}, bf16[6,128,128]{2,1,0:T(8,128)(2,1)S(1)}, u32[]{:S(2)}, u32[]{:S(2)}) collective-permute-start(bf16[6,128,128]{2,1,0:T(8,128)(2,1)S(1)} %get-tuple-element.75), channel_id=1, source_target_pairs={{0,4},{1,5},{4,8},{5,9},{6,2},{7,3},{8,12},{9,13},{10,6},{11,7},{1... | collective-permute-start | bytes 589832 | tf_op jit(solution)/shard_map/ppermute | solution.py:287
  86.4 2.6 %collective-permute-start.15 = (bf16[2,128,128]{2,1,0:T(8,128)(2,1)S(1)}, bf16[2,128,128]{2,1,0:T(8,128)(2,1)S(1)}, u32[]{:S(2)}, u32[]{:S(2)}) collective-permute-start(bf16[2,128,128]{2,1,0:T(8,128)(2,1)S(1)} %get-tuple-element.77), channel_id=1, source_target_pairs={{2,6},{5,1},{6,10},{9,5},{10,14},{13,9},{18,22},{21,17},{22,26},{2... | collective-permute-start | bytes 196616 | tf_op jit(solution)/shard_map/ppermute | solution.py:287

commit v6 on v5

--- a/solution.py
+++ b/solution.py
@@ -340,10 +340,10 @@
     shape = (MAXP, lags // 2, width)
     filled = assemble((keep, sib), shape, [[(0, 0, mine, 0), (1, 1, mine, 0)] for mine in range(2)])
     filled = assemble((near,), shape, [[(0, 2, 3 - mine, 0)] for mine in range(2)], filled, weight=12000)
-    return tuple(assemble((rest, x, v, w), shape, [
-        [(0, 3, 3 - mine, 0), (1, 0, 4 + mine, 0), (1, 1, 4 + mine, SIZES[2]),
-         (2, 2, -1 - mine, 0), (2, 3, -1 - mine, SIZES[3])] + inner
-        for mine, inner in enumerate(([], [(3, 0, -3, 0), (3, 1, -3, 1)]))], filled))
+    filled = assemble((x, v, w), shape, [
+        [(0, 0, 4 + mine, 0), (0, 1, 4 + mine, SIZES[2]), (1, 2, -1 - mine, 0), (1, 3, -1 - mine, SIZES[3])] + inner
+        for mine, inner in enumerate(([], [(2, 0, -3, 0), (2, 1, -3, 1)]))], filled)
+    return tuple(assemble((rest,), shape, [[(0, 3, 3 - mine, 0)] for mine in range(2)], filled))
 
 
 def solution(mesh):

time: 96.9 us -> 96.4 us (level)
  waiting for transfers between devices: 42.1 us -> 40.6 us
    ppermute x17, waiting for transfers between devices: 42.1 us -> 40.6 us  [send(): return lax.ppermute(value, 'chan', pairs)]
    pallas_call x3 -> x4, Pallas kernels: 3.1 us -> 3.71 us  [assemble(): pl.pallas_call(functools.partial(assemble_body, plan=plan, count=len(part...]
  transfers between devices with their start and end apart: 17 -> 17, of which waited for: 8 -> 9; matrix products, arithmetic and copies ran while one was open for 0% -> 0% of each run, Pallas kernels for 16% -> 17%
where the time goes in v6:
time: 96.4 us; the launch traced here: 95.8 us
  waiting for transfers between devices  40.6 us (42%)
  starting transfers between devices  29 us (30%)
  Pallas kernels  23.3 us (24%)
  local copies, waits for them, and re-layouts  1.91 us (2%)
    ppermute x17, waiting for transfers between devices, send(): return lax.ppermute(value, 'chan', pairs)  40.6 us
    ppermute x17, starting transfers between devices, send(): return lax.ppermute(value, 'chan', pairs)  29 us
    pallas_call x4, Pallas kernels, correlate(): pl.pallas_call(functools.partial(correlate_body, work=work, sources=sourc...  12.4 us
    pallas_call x2, Pallas kernels, whiten(): pl.pallas_call(whiten_body, grid=(windows // STEP,), in_specs=[pl.BlockSp...  6.89 us
    pallas_call x4, Pallas kernels, assemble(): pl.pallas_call(functools.partial(assemble_body, plan=plan, count=len(part...  3.71 us
  transfers between devices with their start and end apart: 17, of which 9 were waited for; matrix products, arithmetic and copies ran while one was open for 0% of the time, Pallas kernels for 17%

profile of v6, /device:TPU:16, one launch (start us, length us, event | category | flops | bytes accessed | tf_op | source)
XLA Modules:
  0.0 95.8 jit_solution(10794339717791175806)
XLA Ops:
  0.6 3.4 %shard_map.68 = (bf16[16,2,128,128]{3,2,1,0:T(8,128)(2,1)}, bf16[16,2,128,128]{3,2,1,0:T(8,128)(2,1)}) custom-call(s32[16,16]{1,0:T(8,128)} %mask_ref.2, bf16[256,256]{1,0:T(8,128)(2,1)} %constant.5.clone.table_ref, bf16[1,16,256,512]{3,2,1,0:T(8,128)(2,1)} %traces_ref.3), custom_call_target="tpu_custom_call" | custom-call | flops 536870912 | bytes 4194304 | tf_op jit(solution)/shard_map/pallas_call | solution.py:108
  4.0 0.0 copy-start.4
  4.0 0.0 copy-start.2
  4.0 0.0 copy-start.3
  4.0 1.6 %collective-permute-start.1 = (bf16[16,2,128,128]{3,2,1,0:T(8,128)(2,1)}, bf16[16,2,128,128]{3,2,1,0:T(8,128)(2,1)S(1)}, u32[]{:S(2)}, u32[]{:S(2)}) collective-permute-start(bf16[16,2,128,128]{3,2,1,0:T(8,128)(2,1)} %get-tuple-element.45), channel_id=1, source_target_pairs={{0,2},{1,3},{2,0},{3,1},{4,6},{5,7},{6,4},{7,5},{8,10},{9,11},{10,... | collective-permute-start | bytes 3145736 | tf_op jit(solution)/shard_map/ppermute | solution.py:287
  5.6 3.5 %shard_map.69 = (bf16[32,2,128,128]{3,2,1,0:T(8,128)(2,1)}, bf16[16,2,128,128]{3,2,1,0:T(8,128)(2,1)}) custom-call(s32[16,16]{1,0:T(8,128)} %mask_ref.2, bf16[256,256]{1,0:T(8,128)(2,1)} %constant.5.clone.table_ref, bf16[1,16,256,512]{3,2,1,0:T(8,128)(2,1)} %traces_ref.3), custom_call_target="tpu_custom_call" | custom-call | flops 536870912 | bytes 4194304 | tf_op jit(solution)/shard_map/pallas_call | solution.py:108
  9.2 0.1 collective-permute-start
  9.2 0.8 collective-permute-start.9
  10.0 2.4 %collective-permute-start.3 = (bf16[32,2,128,128]{3,2,1,0:T(8,128)(2,1)}, bf16[32,2,128,128]{3,2,1,0:T(8,128)(2,1)S(1)}, u32[]{:S(2)}, u32[]{:S(2)}) collective-permute-start(bf16[32,2,128,128]{3,2,1,0:T(8,128)(2,1)} %get-tuple-element.47.refs_0_), channel_id=1, source_target_pairs={{2,6},{3,7},{4,0},{5,1},{6,10},{7,11},{8,4},{9,5},{10,14},{11,15},... | collective-permute-start | bytes 6291464 | tf_op jit(solution)/shard_map/ppermute | solution.py:287
  12.4 0.0 copy-done.4
  12.4 1.5 %collective-permute-start.2 = (bf16[16,2,128,128]{3,2,1,0:T(8,128)(2,1)S(1)}, bf16[16,2,128,128]{3,2,1,0:T(8,128)(2,1)S(1)}, u32[]{:S(2)}, u32[]{:S(2)}) collective-permute-start(bf16[16,2,128,128]{3,2,1,0:T(8,128)(2,1)S(1)} %copy-done.4), channel_id=1, source_target_pairs={{0,3},{1,2},{2,1},{3,0},{4,7},{5,6},{6,5},{7,4},{8,11},{9,10},{10,... | collective-permute-start | bytes 3145736 | tf_op jit(solution)/shard_map/ppermute | solution.py:287
  13.9 16.4 %collective-permute-done.1.refs_2_ = bf16[16,2,128,128]{3,2,1,0:T(8,128)(2,1)S(1)} collective-permute-done((bf16[16,2,128,128]{3,2,1,0:T(8,128)(2,1)}, bf16[16,2,128,128]{3,2,1,0:T(8,128)(2,1)S(1)}, u32[]{:S(2)}, u32[]{:S(2)}) %collective-permute-start.1) | collective-permute-done | bytes 1048608 | tf_op jit(solution)/shard_map/ppermute | solution.py:287
  30.4 0.0 collective-permute-done.refs_1_
  30.4 3.5 %collective-permute-start.8 = (bf16[16,2,128,128]{3,2,1,0:T(8,128)(2,1)S(1)}, bf16[16,2,128,128]{3,2,1,0:T(8,128)(2,1)S(1)}, u32[]{:S(2)}, u32[]{:S(2)}) collective-permute-start(bf16[16,2,128,128]{3,2,1,0:T(8,128)(2,1)S(1)} %collective-permute-done.1.refs_2_), channel_id=1, source_target_pairs={{0,4},{1,5},{4,8},{5,9},{6,2},{7,3},{8,12},{9,13},{10,6},{11,7},{1... | collective-permute-start | bytes 3145736 | tf_op jit(solution)/shard_map/ppermute | solution.py:287
  33.8 0.0 copy-done.2
  33.9 0.0 copy-done.3
  33.9 0.0 copy-start
  33.9 1.6 %copy-done = bf16[32,2,128,128]{3,2,1,0:T(8,128)(2,1)S(1)} copy-done((bf16[32,2,128,128]{3,2,1,0:T(8,128)(2,1)S(1)}, bf16[32,2,128,128]{3,2,1,0:T(8,128)(2,1)}, u32[]{:S(2)}) %copy-start) | copy-done | bytes 2097176
  35.5 1.9 %shard_map.70 = (bf16[7,128,128]{2,1,0:T(8,128)(2,1)S(1)}, bf16[6,128,128]{2,1,0:T(8,128)(2,1)S(1)}, bf16[6,128,128]{2,1,0:T(8,128)(2,1)S(1)}, bf16[8,128,128]{2...) custom-call(s32[16]{0:T(128)S(1)} %copy-done.3, ...), custom_call_target="tpu_custom_call" | custom-call | flops 15728640000 | bytes 3145728 | tf_op jit(solution)/shard_map/pallas_call | solution.py:196
  37.4 13.3 %collective-permute-done.2.refs_3_ = bf16[16,2,128,128]{3,2,1,0:T(8,128)(2,1)S(1)} collective-permute-done((bf16[16,2,128,128]{3,2,1,0:T(8,128)(2,1)S(1)}, bf16[16,2,128,128]{3,2,1,0:T(8,128)(2,1)S(1)}, u32[]{:S(2)}, u32[]{:S(2)}) %collective-permute-start.2) | collective-permute-done | bytes 1048608 | tf_op jit(solution)/shard_map/ppermute | solution.py:287
  50.7 0.1 slice.18
  50.8 0.0 copy-start.1
  50.8 3.6 %collective-permute-start.4 = (bf16[11,2,128,128]{3,2,1,0:T(8,128)(2,1)S(1)}, bf16[11,2,128,128]{3,2,1,0:T(8,128)(2,1)S(1)}, u32[]{:S(2)}, u32[]{:S(2)}) collective-permute-start(bf16[11,2,128,128]{3,2,1,0:T(8,128)(2,1)S(1)} %slice.18), channel_id=1, source_target_pairs={{0,4},{1,5},{4,8},{5,9},{6,2},{7,3},{8,12},{9,13},{10,6},{11,7},{1... | collective-permute-start | bytes 2162696 | tf_op jit(solution)/shard_map/ppermute | solution.py:287
  54.4 0.0 collective-permute-done.9.refs_9_
  54.4 0.1 slice.22
  54.6 1.3 %collective-permute-start.10 = (bf16[16,2,128,128]{3,2,1,0:T(8,128)(2,1)S(1)}, bf16[16,2,128,128]{3,2,1,0:T(8,128)(2,1)S(1)}, u32[]{:S(2)}, u32[]{:S(2)}) collective-permute-start(bf16[16,2,128,128]{3,2,1,0:T(8,128)(2,1)S(1)} %slice.22), channel_id=1, source_target_pairs={{1,0},{2,3},{5,4},{6,7},{9,8},{10,11},{13,12},{14,15},{17,16},{18,... | collective-permute-start | bytes 3145736 | tf_op jit(solution)/shard_map/ppermute | solution.py:287
  55.9 0.0 copy-done.1
  55.9 2.2 %shard_map.71 = (bf16[7,128,128]{2,1,0:T(8,128)(2,1)S(1)}, bf16[6,128,128]{2,1,0:T(8,128)(2,1)S(1)}, bf16[6,128,128]{2,1,0:T(8,128)(2,1)S(1)}, bf16[8,128,128]{2...) custom-call(s32[16]{0:T(128)S(1)} %copy-done.3, ...), custom_call_target="tpu_custom_call" | custom-call | flops 15728640000 | bytes 4194304 | tf_op jit(solution)/shard_map/pallas_call | solution.py:196
  58.0 0.6 collective-permute-done.3.refs_4_
  58.7 0.1 fusion
  58.8 2.2 %collective-permute-start.7 = (bf16[8,2,128,128]{3,2,1,0:T(8,128)(2,1)S(1)}, bf16[8,2,128,128]{3,2,1,0:T(8,128)(2,1)S(1)}, u32[]{:S(2)}, u32[]{:S(2)}) collective-permute-start(bf16[8,2,128,128]{3,2,1,0:T(8,128)(2,1)S(1)} %get-tuple-element.88), channel_id=1, source_target_pairs={{0,1},{1,0},{2,3},{3,2},{4,5},{5,4},{6,7},{7,6},{8,9},{9,8},{10,11... | collective-permute-start | bytes 1572872 | tf_op jit(solution)/shard_map/ppermute | solution.py:287
  60.9 0.1 collective-permute-start.6
  61.0 0.0 collective-permute-done.8.refs_7_
  61.1 1.9 %collective-permute-start.5 = (bf16[5,2,128,128]{3,2,1,0:T(8,128)(2,1)S(1)}, bf16[5,2,128,128]{3,2,1,0:T(8,128)(2,1)S(1)}, u32[]{:S(2)}, u32[]{:S(2)}) collective-permute-start(bf16[5,2,128,128]{3,2,1,0:T(8,128)(2,1)S(1)} %slice.19), channel_id=1, source_target_pairs={{2,5},{3,4},{4,3},{5,2},{6,9},{7,8},{8,7},{9,6},{10,13},{11,12},{1... | collective-permute-start | bytes 983048 | tf_op jit(solution)/shard_map/ppermute | solution.py:287
  63.0 0.0 collective-permute-done.7.refs_6_
  63.0 0.2 collective-permute-done.6.refs_5_
  63.2 0.0 collective-permute-done.10.refs_8_
  63.2 5.7 %shard_map.72 = (bf16[7,128,128]{2,1,0:T(8,128)(2,1)S(1)}, bf16[6,128,128]{2,1,0:T(8,128)(2,1)S(1)}, bf16[6,128,128]{2,1,0:T(8,128)(2,1)S(1)}, bf16[8,128,128]{2...) custom-call(s32[16]{0:T(128)S(1)} %copy-done.3, ...), custom_call_target="tpu_custom_call" | custom-call | tf_op jit(solution)/shard_map/pallas_call | solution.py:196
  68.9 4.4 %collective-permute-done.5.refs_6_ = bf16[5,2,128,128]{3,2,1,0:T(8,128)(2,1)S(1)} collective-permute-done((bf16[5,2,128,128]{3,2,1,0:T(8,128)(2,1)S(1)}, bf16[5,2,128,128]{3,2,1,0:T(8,128)(2,1)S(1)}, u32[]{:S(2)}, u32[]{:S(2)}) %collective-permute-start.5) | collective-permute-done | bytes 327712 | tf_op jit(solution)/shard_map/ppermute | solution.py:287
  73.3 0.5 collective-permute-done.4.refs_5_
  73.8 2.6 %shard_map.73 = (bf16[7,128,128]{2,1,0:T(8,128)(2,1)S(1)}, bf16[6,128,128]{2,1,0:T(8,128)(2,1)S(1)}, bf16[6,128,128]{2,1,0:T(8,128)(2,1)S(1)}, bf16[8,128,128]{2...) custom-call(s32[16]{0:T(128)S(1)} %copy-done.3, ...), custom_call_target="tpu_custom_call" | custom-call | flops 104857600 | bytes 7340032 | tf_op jit(solution)/shard_map/pallas_call | solution.py:196
  76.4 0.9 collective-permute-start.11
  77.3 1.2 %collective-permute-start.16 = (bf16[6,128,128]{2,1,0:T(8,128)(2,1)S(1)}, bf16[6,128,128]{2,1,0:T(8,128)(2,1)S(1)}, u32[]{:S(2)}, u32[]{:S(2)}) collective-permute-start(bf16[6,128,128]{2,1,0:T(8,128)(2,1)S(1)} %get-tuple-element.80), channel_id=1, source_target_pairs={{0,2},{1,3},{2,0},{3,1},{4,6},{5,7},{6,4},{7,5},{8,10},{9,11},{10,... | collective-permute-start | bytes 589832 | tf_op jit(solution)/shard_map/ppermute | solution.py:287
  78.5 0.5 collective-permute-done.11.sib.refs_1_
  79.1 0.3 shard_map.74
  79.4 3.3 %collective-permute-start.14 = (bf16[8,128,128]{2,1,0:T(8,128)(2,1)S(1)}, bf16[8,128,128]{2,1,0:T(8,128)(2,1)S(1)}, u32[]{:S(2)}, u32[]{:S(2)}) collective-permute-start(bf16[8,128,128]{2,1,0:T(8,128)(2,1)S(1)} %get-tuple-element.78), channel_id=1, source_target_pairs={{2,4},{3,5},{4,2},{5,3},{6,8},{7,9},{8,6},{9,7},{10,12},{11,13},{1... | collective-permute-start | bytes 786440 | tf_op jit(solution)/shard_map/ppermute | solution.py:287
  82.7 3.5 %collective-permute-start.13 = (bf16[6,128,128]{2,1,0:T(8,128)(2,1)S(1)}, bf16[6,128,128]{2,1,0:T(8,128)(2,1)S(1)}, u32[]{:S(2)}, u32[]{:S(2)}) collective-permute-start(bf16[6,128,128]{2,1,0:T(8,128)(2,1)S(1)} %get-tuple-element.77), channel_id=1, source_target_pairs={{0,4},{1,5},{4,8},{5,9},{6,2},{7,3},{8,12},{9,13},{10,6},{11,7},{1... | collective-permute-start | bytes 589832 | tf_op jit(solution)/shard_map/ppermute | solution.py:287
  86.3 0.6 collective-permute-start.12
  86.8 0.7 collective-permute-start.15
  87.5 1.1 %shard_map.75 = (f32[1,5,128,512]{3,2,1,0:T(8,128)}, f32[1,5,128,512]{3,2,1,0:T(8,128)}) custom-call(bf16[7,128,128]{2,1,0:T(8,128)(2,1)S(1)} %get-tuple-element.81.refs_0_, bf16[21,128,128]{2,1,0:T(8,128)(2,1)S(1)} %collective-permute-done.11.sib.refs_1_), custom_call_target="tpu_custom_call" | custom-call | flops 229376 | bytes 1376256 | tf_op jit(solution)/shard_map/pallas_call | solution.py:260
  88.5 0.0 collective-permute-done.16.refs_0_
  88.6 0.8 shard_map.76
  89.4 0.0 collective-permute-done.15.refs_2_
  89.4 1.9 %collective-permute-done.13.refs_0_ = bf16[6,128,128]{2,1,0:T(8,128)(2,1)S(1)} collective-permute-done((bf16[6,128,128]{2,1,0:T(8,128)(2,1)S(1)}, bf16[6,128,128]{2,1,0:T(8,128)(2,1)S(1)}, u32[]{:S(2)}, u32[]{:S(2)}) %collective-permute-start.13) | collective-permute-done | bytes 196640 | tf_op jit(solution)/shard_map/ppermute | solution.py:287
  91.3 0.0 collective-permute-done.14.refs_1_
  91.3 1.1 %shard_map.77 = (f32[1,5,128,512]{3,2,1,0:T(8,128)}, f32[1,5,128,512]{3,2,1,0:T(8,128)}) custom-call(bf16[6,128,128]{2,1,0:T(8,128)(2,1)S(1)} %collective-permute-done.13.refs_0_, bf16[8,128,128]{2,1,0:T(8,128)(2,1)S(1)} %collective-permute-done.14.refs_1_, ...), custom_call_target="tpu_custom_call", output_to_operand_aliasing={{0}: (3, {}), {1}: (4, {})} | custom-call | flops 262144 | bytes 1572864 | tf_op jit(solution)/shard_map/pallas_call | solution.py:260
  92.4 2.6 %collective-permute-done.12.refs_0_ = bf16[6,128,128]{2,1,0:T(8,128)(2,1)S(1)} collective-permute-done((bf16[6,128,128]{2,1,0:T(8,128)(2,1)S(1)}, bf16[6,128,128]{2,1,0:T(8,128)(2,1)S(1)}, u32[]{:S(2)}, u32[]{:S(2)}) %collective-permute-start.12) | collective-permute-done | bytes 196640 | tf_op jit(solution)/shard_map/ppermute | solution.py:287
  95.0 0.8 shard_map.78
  (2 shorter events, 0.0 us)
Async XLA Ops:
  4.0 8.4 %copy-start.4 = (bf16[16,2,128,128]{3,2,1,0:T(8,128)(2,1)S(1)}, bf16[16,2,128,128]{3,2,1,0:T(8,128)(2,1)}, u32[]{:S(2)}) copy-start(bf16[16,2,128,128]{3,2,1,0:T(8,128)(2,1)} %get-tuple-element.59) | copy-start | bytes 3145732
  4.0 29.8 %copy-start.2 = (bf16[2,256,256]{2,1,0:T(8,128)(2,1)S(1)}, bf16[2,256,256]{2,1,0:T(8,128)(2,1)}, u32[]{:S(2)}) copy-start(bf16[2,256,256]{2,1,0:T(8,128)(2,1)} %constant.4.clone.table_ref) | copy-start | bytes 786436
  4.0 29.8 %copy-start.3 = (s32[16]{0:T(128)S(1)}, s32[16]{0:T(128)}, u32[]{:S(2)}) copy-start(s32[16]{0:T(128)} %counts_ref.7) | copy-start | bytes 196
  4.0 26.3 %collective-permute-start.1 = (bf16[16,2,128,128]{3,2,1,0:T(8,128)(2,1)}, bf16[16,2,128,128]{3,2,1,0:T(8,128)(2,1)S(1)}, u32[]{:S(2)}, u32[]{:S(2)}) collective-permute-start(bf16[16,2,128,128]{3,2,1,0:T(8,128)(2,1)} %get-tuple-element.45), channel_id=1, source_target_pairs={{0,2},{1,3},{2,0},{3,1},{4,6},{5,7},{6,4},{7,5},{8,10},{9,11},{10,... | collective-permute-start | bytes 3145736 | tf_op jit(solution)/shard_map/ppermute | solution.py:287
  9.2 21.2 %collective-permute-start = (bf16[16,2,128,128]{3,2,1,0:T(8,128)(2,1)}, bf16[16,2,128,128]{3,2,1,0:T(8,128)(2,1)S(1)}, u32[]{:S(2)}, u32[]{:S(2)}) collective-permute-start(bf16[16,2,128,128]{3,2,1,0:T(8,128)(2,1)} %get-tuple-element.48), channel_id=1, source_target_pairs={{0,1},{1,0},{2,3},{3,2},{4,5},{5,4},{6,7},{7,6},{8,9},{9,8},{10,11... | collective-permute-start | bytes 3145736 | tf_op jit(solution)/shard_map/ppermute | solution.py:287
  9.2 45.2 %collective-permute-start.9 = (bf16[32,2,128,128]{3,2,1,0:T(8,128)(2,1)}, bf16[32,2,128,128]{3,2,1,0:T(8,128)(2,1)S(1)}, u32[]{:S(2)}, u32[]{:S(2)}) collective-permute-start(bf16[32,2,128,128]{3,2,1,0:T(8,128)(2,1)} %get-tuple-element.47.refs_0_), channel_id=1, source_target_pairs={{1,5},{5,9},{6,2},{9,13},{10,6},{14,10},{17,21},{21,25},{22,18},{2... | collective-permute-start | bytes 6291464 | tf_op jit(solution)/shard_map/ppermute | solution.py:287
  10.0 48.6 %collective-permute-start.3 = (bf16[32,2,128,128]{3,2,1,0:T(8,128)(2,1)}, bf16[32,2,128,128]{3,2,1,0:T(8,128)(2,1)S(1)}, u32[]{:S(2)}, u32[]{:S(2)}) collective-permute-start(bf16[32,2,128,128]{3,2,1,0:T(8,128)(2,1)} %get-tuple-element.47.refs_0_), channel_id=1, source_target_pairs={{2,6},{3,7},{4,0},{5,1},{6,10},{7,11},{8,4},{9,5},{10,14},{11,15},... | collective-permute-start | bytes 6291464 | tf_op jit(solution)/shard_map/ppermute | solution.py:287
  12.4 38.3 %collective-permute-start.2 = (bf16[16,2,128,128]{3,2,1,0:T(8,128)(2,1)S(1)}, bf16[16,2,128,128]{3,2,1,0:T(8,128)(2,1)S(1)}, u32[]{:S(2)}, u32[]{:S(2)}) collective-permute-start(bf16[16,2,128,128]{3,2,1,0:T(8,128)(2,1)S(1)} %copy-done.4), channel_id=1, source_target_pairs={{0,3},{1,2},{2,1},{3,0},{4,7},{5,6},{6,5},{7,4},{8,11},{9,10},{10,... | collective-permute-start | bytes 3145736 | tf_op jit(solution)/shard_map/ppermute | solution.py:287
  30.4 30.7 %collective-permute-start.8 = (bf16[16,2,128,128]{3,2,1,0:T(8,128)(2,1)S(1)}, bf16[16,2,128,128]{3,2,1,0:T(8,128)(2,1)S(1)}, u32[]{:S(2)}, u32[]{:S(2)}) collective-permute-start(bf16[16,2,128,128]{3,2,1,0:T(8,128)(2,1)S(1)} %collective-permute-done.1.refs_2_), channel_id=1, source_target_pairs={{0,4},{1,5},{4,8},{5,9},{6,2},{7,3},{8,12},{9,13},{10,6},{11,7},{1... | collective-permute-start | bytes 3145736 | tf_op jit(solution)/shard_map/ppermute | solution.py:287
  33.9 1.6 %copy-start = (bf16[32,2,128,128]{3,2,1,0:T(8,128)(2,1)S(1)}, bf16[32,2,128,128]{3,2,1,0:T(8,128)(2,1)}, u32[]{:S(2)}) copy-start(bf16[32,2,128,128]{3,2,1,0:T(8,128)(2,1)} %get-tuple-element.47.refs_0_) | copy-start | bytes 6291460
  50.8 5.1 %copy-start.1 = (bf16[32,2,128,128]{3,2,1,0:T(8,128)(2,1)S(1)}, bf16[32,2,128,128]{3,2,1,0:T(8,128)(2,1)}, u32[]{:S(2)}) copy-start(bf16[32,2,128,128]{3,2,1,0:T(8,128)(2,1)} %get-tuple-element.47.refs_0_) | copy-start | bytes 6291460
  50.8 23.0 %collective-permute-start.4 = (bf16[11,2,128,128]{3,2,1,0:T(8,128)(2,1)S(1)}, bf16[11,2,128,128]{3,2,1,0:T(8,128)(2,1)S(1)}, u32[]{:S(2)}, u32[]{:S(2)}) collective-permute-start(bf16[11,2,128,128]{3,2,1,0:T(8,128)(2,1)S(1)} %slice.18), channel_id=1, source_target_pairs={{0,4},{1,5},{4,8},{5,9},{6,2},{7,3},{8,12},{9,13},{10,6},{11,7},{1... | collective-permute-start | bytes 2162696 | tf_op jit(solution)/shard_map/ppermute | solution.py:287
  54.6 8.7 %collective-permute-start.10 = (bf16[16,2,128,128]{3,2,1,0:T(8,128)(2,1)S(1)}, bf16[16,2,128,128]{3,2,1,0:T(8,128)(2,1)S(1)}, u32[]{:S(2)}, u32[]{:S(2)}) collective-permute-start(bf16[16,2,128,128]{3,2,1,0:T(8,128)(2,1)S(1)} %slice.22), channel_id=1, source_target_pairs={{1,0},{2,3},{5,4},{6,7},{9,8},{10,11},{13,12},{14,15},{17,16},{18,... | collective-permute-start | bytes 3145736 | tf_op jit(solution)/shard_map/ppermute | solution.py:287
  58.8 4.2 %collective-permute-start.7 = (bf16[8,2,128,128]{3,2,1,0:T(8,128)(2,1)S(1)}, bf16[8,2,128,128]{3,2,1,0:T(8,128)(2,1)S(1)}, u32[]{:S(2)}, u32[]{:S(2)}) collective-permute-start(bf16[8,2,128,128]{3,2,1,0:T(8,128)(2,1)S(1)} %get-tuple-element.88), channel_id=1, source_target_pairs={{0,1},{1,0},{2,3},{3,2},{4,5},{5,4},{6,7},{7,6},{8,9},{9,8},{10,11... | collective-permute-start | bytes 1572872 | tf_op jit(solution)/shard_map/ppermute | solution.py:287
  60.9 2.3 %collective-permute-start.6 = (bf16[8,2,128,128]{3,2,1,0:T(8,128)(2,1)S(1)}, bf16[8,2,128,128]{3,2,1,0:T(8,128)(2,1)S(1)}, u32[]{:S(2)}, u32[]{:S(2)}) collective-permute-start(bf16[8,2,128,128]{3,2,1,0:T(8,128)(2,1)S(1)} %get-tuple-element.89), channel_id=1, source_target_pairs={{0,1},{1,0},{2,3},{3,2},{4,5},{5,4},{6,7},{7,6},{8,9},{9,8},{10,11... | collective-permute-start | bytes 1572872 | tf_op jit(solution)/shard_map/ppermute | solution.py:287
  61.1 12.2 %collective-permute-start.5 = (bf16[5,2,128,128]{3,2,1,0:T(8,128)(2,1)S(1)}, bf16[5,2,128,128]{3,2,1,0:T(8,128)(2,1)S(1)}, u32[]{:S(2)}, u32[]{:S(2)}) collective-permute-start(bf16[5,2,128,128]{3,2,1,0:T(8,128)(2,1)S(1)} %slice.19), channel_id=1, source_target_pairs={{2,5},{3,4},{4,3},{5,2},{6,9},{7,8},{8,7},{9,6},{10,13},{11,12},{1... | collective-permute-start | bytes 983048 | tf_op jit(solution)/shard_map/ppermute | solution.py:287
  76.4 2.7 %collective-permute-start.11 = (bf16[21,128,128]{2,1,0:T(8,128)(2,1)S(1)}, bf16[21,128,128]{2,1,0:T(8,128)(2,1)S(1)}, u32[]{:S(2)}, u32[]{:S(2)}) collective-permute-start(bf16[21,128,128]{2,1,0:T(8,128)(2,1)S(1)} %get-tuple-element.73), channel_id=1, source_target_pairs={{0,1},{1,0},{2,3},{3,2},{4,5},{5,4},{6,7},{7,6},{8,9},{9,8},{10,11... | collective-permute-start | bytes 2064392 | tf_op jit(solution)/shard_map/ppermute | solution.py:287
  77.3 11.3 %collective-permute-start.16 = (bf16[6,128,128]{2,1,0:T(8,128)(2,1)S(1)}, bf16[6,128,128]{2,1,0:T(8,128)(2,1)S(1)}, u32[]{:S(2)}, u32[]{:S(2)}) collective-permute-start(bf16[6,128,128]{2,1,0:T(8,128)(2,1)S(1)} %get-tuple-element.80), channel_id=1, source_target_pairs={{0,2},{1,3},{2,0},{3,1},{4,6},{5,7},{6,4},{7,5},{8,10},{9,11},{10,... | collective-permute-start | bytes 589832 | tf_op jit(solution)/shard_map/ppermute | solution.py:287
  79.4 11.9 %collective-permute-start.14 = (bf16[8,128,128]{2,1,0:T(8,128)(2,1)S(1)}, bf16[8,128,128]{2,1,0:T(8,128)(2,1)S(1)}, u32[]{:S(2)}, u32[]{:S(2)}) collective-permute-start(bf16[8,128,128]{2,1,0:T(8,128)(2,1)S(1)} %get-tuple-element.78), channel_id=1, source_target_pairs={{2,4},{3,5},{4,2},{5,3},{6,8},{7,9},{8,6},{9,7},{10,12},{11,13},{1... | collective-permute-start | bytes 786440 | tf_op jit(solution)/shard_map/ppermute | solution.py:287
  82.7 8.6 %collective-permute-start.13 = (bf16[6,128,128]{2,1,0:T(8,128)(2,1)S(1)}, bf16[6,128,128]{2,1,0:T(8,128)(2,1)S(1)}, u32[]{:S(2)}, u32[]{:S(2)}) collective-permute-start(bf16[6,128,128]{2,1,0:T(8,128)(2,1)S(1)} %get-tuple-element.77), channel_id=1, source_target_pairs={{0,4},{1,5},{4,8},{5,9},{6,2},{7,3},{8,12},{9,13},{10,6},{11,7},{1... | collective-permute-start | bytes 589832 | tf_op jit(solution)/shard_map/ppermute | solution.py:287
  86.3 8.7 %collective-permute-start.12 = (bf16[6,128,128]{2,1,0:T(8,128)(2,1)S(1)}, bf16[6,128,128]{2,1,0:T(8,128)(2,1)S(1)}, u32[]{:S(2)}, u32[]{:S(2)}) collective-permute-start(bf16[6,128,128]{2,1,0:T(8,128)(2,1)S(1)} %slice.24), channel_id=1, source_target_pairs={{0,2},{1,3},{2,0},{3,1},{4,6},{5,7},{6,4},{7,5},{8,10},{9,11},{10,... | collective-permute-start | bytes 589832 | tf_op jit(solution)/shard_map/ppermute | solution.py:287
  86.8 2.6 %collective-permute-start.15 = (bf16[2,128,128]{2,1,0:T(8,128)(2,1)S(1)}, bf16[2,128,128]{2,1,0:T(8,128)(2,1)S(1)}, u32[]{:S(2)}, u32[]{:S(2)}) collective-permute-start(bf16[2,128,128]{2,1,0:T(8,128)(2,1)S(1)} %get-tuple-element.79), channel_id=1, source_target_pairs={{2,6},{5,1},{6,10},{9,5},{10,14},{13,9},{18,22},{21,17},{22,26},{2... | collective-permute-start | bytes 196616 | tf_op jit(solution)/shard_map/ppermute | solution.py:287

commit v7 on v6

--- a/solution.py
+++ b/solution.py
@@ -209,7 +209,7 @@
     copies = []
     for n, d in enumerate(MERGED):
         copies.append(pltpu.make_async_copy(
-            sib.at[pl.ds(STARTS[d], SIZES[d])], outs[n].at[pl.ds(SIZES[d], SIZES[d])], sems.at[n]))
+            sib.at[pl.ds(STARTS[d] - SIZES[0], SIZES[d])], outs[n].at[pl.ds(SIZES[d], SIZES[d])], sems.at[n]))
     for one in copies:
         one.start()
     for one in copies:
@@ -331,14 +331,15 @@
             whole((0, 1), (1, 0), (2, 3), (3, 2)) | {-2: last}), filled=parts)
 
     near = send(f, 2, HERE)
-    sib = send(sib, 1, HERE)
-    x, v, w = merge(sib, (x, v, w))
-    rest = send(sib[STARTS[1]:STARTS[2]], 2, HERE)
+    others = send(sib[SIZES[0]:], 1, HERE)
+    x, v, w = merge(others, (x, v, w))
+    rest = send(others[:SIZES[1]], 2, HERE)
+    twin = send(sib[:SIZES[0]], 1, HERE)
     v, x = send(v, 2, OUTWARD), send(x, 0, INWARD)
     w = send(w, 0, INNER_OUTWARD)
 
     shape = (MAXP, lags // 2, width)
-    filled = assemble((keep, sib), shape, [[(0, 0, mine, 0), (1, 1, mine, 0)] for mine in range(2)])
+    filled = assemble((keep, twin), shape, [[(0, 0, mine, 0), (1, 1, mine, 0)] for mine in range(2)])
     filled = assemble((near,), shape, [[(0, 2, 3 - mine, 0)] for mine in range(2)], filled, weight=12000)
     filled = assemble((x, v, w), shape, [
         [(0, 0, 4 + mine, 0), (0, 1, 4 + mine, SIZES[2]), (1, 2, -1 - mine, 0), (1, 3, -1 - mine, SIZES[3])] + inner

time: 96.4 us -> 96.1 us (level)
    ppermute x17 -> x18, waiting for transfers between devices: 40.6 us -> 39.8 us  [send(): return lax.ppermute(value, 'chan', pairs)]
    ppermute x17 -> x18, starting transfers between devices: 29 us -> 29.5 us  [send(): return lax.ppermute(value, 'chan', pairs)]
  transfers between devices with their start and end apart: 17 -> 18, of which waited for: 9 -> 8; matrix products, arithmetic and copies ran while one was open for 0% -> 0% of each run, Pallas kernels for 17% -> 17%
where the time goes in v7:
time: 96.1 us; the launch traced here: 95.5 us
  waiting for transfers between devices  39.8 us (41%)
  starting transfers between devices  29.5 us (31%)
  Pallas kernels  23.3 us (24%)
  local copies, waits for them, and re-layouts  1.95 us (2%)
    ppermute x18, waiting for transfers between devices, send(): return lax.ppermute(value, 'chan', pairs)  39.8 us
    ppermute x18, starting transfers between devices, send(): return lax.ppermute(value, 'chan', pairs)  29.5 us
    pallas_call x4, Pallas kernels, correlate(): pl.pallas_call(functools.partial(correlate_body, work=work, sources=sourc...  12.4 us
    pallas_call x2, Pallas kernels, whiten(): pl.pallas_call(whiten_body, grid=(windows // STEP,), in_specs=[pl.BlockSp...  6.89 us
    pallas_call x4, Pallas kernels, assemble(): pl.pallas_call(functools.partial(assemble_body, plan=plan, count=len(part...  3.7 us
  transfers between devices with their start and end apart: 18, of which 8 were waited for; matrix products, arithmetic and copies ran while one was open for 0% of the time, Pallas kernels for 17%

profile of v7, /device:TPU:16, one launch (start us, length us, event | category | flops | bytes accessed | tf_op | source)
XLA Modules:
  0.0 95.5 jit_solution(441189308811808028)
XLA Ops:
  0.6 3.4 %shard_map.68 = (bf16[16,2,128,128]{3,2,1,0:T(8,128)(2,1)}, bf16[16,2,128,128]{3,2,1,0:T(8,128)(2,1)}) custom-call(s32[16,16]{1,0:T(8,128)} %mask_ref.2, bf16[256,256]{1,0:T(8,128)(2,1)} %constant.5.clone.table_ref, bf16[1,16,256,512]{3,2,1,0:T(8,128)(2,1)} %traces_ref.3), custom_call_target="tpu_custom_call" | custom-call | flops 536870912 | bytes 4194304 | tf_op jit(solution)/shard_map/pallas_call | solution.py:108
  4.0 0.0 copy-start.4
  4.0 0.0 copy-start.2
  4.0 0.0 copy-start.3
  4.0 1.6 %collective-permute-start.1 = (bf16[16,2,128,128]{3,2,1,0:T(8,128)(2,1)}, bf16[16,2,128,128]{3,2,1,0:T(8,128)(2,1)S(1)}, u32[]{:S(2)}, u32[]{:S(2)}) collective-permute-start(bf16[16,2,128,128]{3,2,1,0:T(8,128)(2,1)} %get-tuple-element.45), channel_id=1, source_target_pairs={{0,2},{1,3},{2,0},{3,1},{4,6},{5,7},{6,4},{7,5},{8,10},{9,11},{10,... | collective-permute-start | bytes 3145736 | tf_op jit(solution)/shard_map/ppermute | solution.py:287
  5.6 3.5 %shard_map.69 = (bf16[32,2,128,128]{3,2,1,0:T(8,128)(2,1)}, bf16[16,2,128,128]{3,2,1,0:T(8,128)(2,1)}) custom-call(s32[16,16]{1,0:T(8,128)} %mask_ref.2, bf16[256,256]{1,0:T(8,128)(2,1)} %constant.5.clone.table_ref, bf16[1,16,256,512]{3,2,1,0:T(8,128)(2,1)} %traces_ref.3), custom_call_target="tpu_custom_call" | custom-call | flops 536870912 | bytes 4194304 | tf_op jit(solution)/shard_map/pallas_call | solution.py:108
  9.2 0.1 collective-permute-start
  9.2 0.8 collective-permute-start.9
  10.0 2.4 %collective-permute-start.3 = (bf16[32,2,128,128]{3,2,1,0:T(8,128)(2,1)}, bf16[32,2,128,128]{3,2,1,0:T(8,128)(2,1)S(1)}, u32[]{:S(2)}, u32[]{:S(2)}) collective-permute-start(bf16[32,2,128,128]{3,2,1,0:T(8,128)(2,1)} %get-tuple-element.47.refs_0_), channel_id=1, source_target_pairs={{2,6},{3,7},{4,0},{5,1},{6,10},{7,11},{8,4},{9,5},{10,14},{11,15},... | collective-permute-start | bytes 6291464 | tf_op jit(solution)/shard_map/ppermute | solution.py:287
  12.4 0.0 copy-done.4
  12.4 1.5 %collective-permute-start.2 = (bf16[16,2,128,128]{3,2,1,0:T(8,128)(2,1)S(1)}, bf16[16,2,128,128]{3,2,1,0:T(8,128)(2,1)S(1)}, u32[]{:S(2)}, u32[]{:S(2)}) collective-permute-start(bf16[16,2,128,128]{3,2,1,0:T(8,128)(2,1)S(1)} %copy-done.4), channel_id=1, source_target_pairs={{0,3},{1,2},{2,1},{3,0},{4,7},{5,6},{6,5},{7,4},{8,11},{9,10},{10,... | collective-permute-start | bytes 3145736 | tf_op jit(solution)/shard_map/ppermute | solution.py:287
  13.9 16.5 %collective-permute-done.1.refs_2_ = bf16[16,2,128,128]{3,2,1,0:T(8,128)(2,1)S(1)} collective-permute-done((bf16[16,2,128,128]{3,2,1,0:T(8,128)(2,1)}, bf16[16,2,128,128]{3,2,1,0:T(8,128)(2,1)S(1)}, u32[]{:S(2)}, u32[]{:S(2)}) %collective-permute-start.1) | collective-permute-done | bytes 1048608 | tf_op jit(solution)/shard_map/ppermute | solution.py:287
  30.4 0.0 collective-permute-done.refs_1_
  30.4 3.5 %collective-permute-start.8 = (bf16[16,2,128,128]{3,2,1,0:T(8,128)(2,1)S(1)}, bf16[16,2,128,128]{3,2,1,0:T(8,128)(2,1)S(1)}, u32[]{:S(2)}, u32[]{:S(2)}) collective-permute-start(bf16[16,2,128,128]{3,2,1,0:T(8,128)(2,1)S(1)} %collective-permute-done.1.refs_2_), channel_id=1, source_target_pairs={{0,4},{1,5},{4,8},{5,9},{6,2},{7,3},{8,12},{9,13},{10,6},{11,7},{1... | collective-permute-start | bytes 3145736 | tf_op jit(solution)/shard_map/ppermute | solution.py:287
  33.8 0.0 copy-done.2
  33.9 0.0 copy-done.3
  33.9 0.0 copy-start
  33.9 1.6 %copy-done = bf16[32,2,128,128]{3,2,1,0:T(8,128)(2,1)S(1)} copy-done((bf16[32,2,128,128]{3,2,1,0:T(8,128)(2,1)S(1)}, bf16[32,2,128,128]{3,2,1,0:T(8,128)(2,1)}, u32[]{:S(2)}) %copy-start) | copy-done | bytes 2097176
  35.5 1.9 %shard_map.70 = (bf16[7,128,128]{2,1,0:T(8,128)(2,1)S(1)}, bf16[6,128,128]{2,1,0:T(8,128)(2,1)S(1)}, bf16[6,128,128]{2,1,0:T(8,128)(2,1)S(1)}, bf16[8,128,128]{2...) custom-call(s32[16]{0:T(128)S(1)} %copy-done.3, ...), custom_call_target="tpu_custom_call" | custom-call | flops 15728640000 | bytes 3145728 | tf_op jit(solution)/shard_map/pallas_call | solution.py:196
  37.4 13.3 %collective-permute-done.2.refs_3_ = bf16[16,2,128,128]{3,2,1,0:T(8,128)(2,1)S(1)} collective-permute-done((bf16[16,2,128,128]{3,2,1,0:T(8,128)(2,1)S(1)}, bf16[16,2,128,128]{3,2,1,0:T(8,128)(2,1)S(1)}, u32[]{:S(2)}, u32[]{:S(2)}) %collective-permute-start.2) | collective-permute-done | bytes 1048608 | tf_op jit(solution)/shard_map/ppermute | solution.py:287
  50.7 0.1 slice.24
  50.8 0.0 copy-start.1
  50.8 3.6 %collective-permute-start.4 = (bf16[11,2,128,128]{3,2,1,0:T(8,128)(2,1)S(1)}, bf16[11,2,128,128]{3,2,1,0:T(8,128)(2,1)S(1)}, u32[]{:S(2)}, u32[]{:S(2)}) collective-permute-start(bf16[11,2,128,128]{3,2,1,0:T(8,128)(2,1)S(1)} %slice.24), channel_id=1, source_target_pairs={{0,4},{1,5},{4,8},{5,9},{6,2},{7,3},{8,12},{9,13},{10,6},{11,7},{1... | collective-permute-start | bytes 2162696 | tf_op jit(solution)/shard_map/ppermute | solution.py:287
  54.4 0.0 collective-permute-done.9.refs_9_
  54.4 0.1 slice.28
  54.5 1.3 %collective-permute-start.10 = (bf16[16,2,128,128]{3,2,1,0:T(8,128)(2,1)S(1)}, bf16[16,2,128,128]{3,2,1,0:T(8,128)(2,1)S(1)}, u32[]{:S(2)}, u32[]{:S(2)}) collective-permute-start(bf16[16,2,128,128]{3,2,1,0:T(8,128)(2,1)S(1)} %slice.28), channel_id=1, source_target_pairs={{1,0},{2,3},{5,4},{6,7},{9,8},{10,11},{13,12},{14,15},{17,16},{18,... | collective-permute-start | bytes 3145736 | tf_op jit(solution)/shard_map/ppermute | solution.py:287
  55.9 0.0 copy-done.1
  55.9 2.2 %shard_map.71 = (bf16[7,128,128]{2,1,0:T(8,128)(2,1)S(1)}, bf16[6,128,128]{2,1,0:T(8,128)(2,1)S(1)}, bf16[6,128,128]{2,1,0:T(8,128)(2,1)S(1)}, bf16[8,128,128]{2...) custom-call(s32[16]{0:T(128)S(1)} %copy-done.3, ...), custom_call_target="tpu_custom_call" | custom-call | flops 15728640000 | bytes 4194304 | tf_op jit(solution)/shard_map/pallas_call | solution.py:196
  58.0 0.6 collective-permute-done.3.refs_4_
  58.6 0.1 fusion
  58.8 2.2 %collective-permute-start.7 = (bf16[8,2,128,128]{3,2,1,0:T(8,128)(2,1)S(1)}, bf16[8,2,128,128]{3,2,1,0:T(8,128)(2,1)S(1)}, u32[]{:S(2)}, u32[]{:S(2)}) collective-permute-start(bf16[8,2,128,128]{3,2,1,0:T(8,128)(2,1)S(1)} %get-tuple-element.88), channel_id=1, source_target_pairs={{0,1},{1,0},{2,3},{3,2},{4,5},{5,4},{6,7},{7,6},{8,9},{9,8},{10,11... | collective-permute-start | bytes 1572872 | tf_op jit(solution)/shard_map/ppermute | solution.py:287
  60.9 0.1 collective-permute-start.6
  61.0 0.0 collective-permute-done.8.refs_7_
  61.0 1.9 %collective-permute-start.5 = (bf16[5,2,128,128]{3,2,1,0:T(8,128)(2,1)S(1)}, bf16[5,2,128,128]{3,2,1,0:T(8,128)(2,1)S(1)}, u32[]{:S(2)}, u32[]{:S(2)}) collective-permute-start(bf16[5,2,128,128]{3,2,1,0:T(8,128)(2,1)S(1)} %slice.25), channel_id=1, source_target_pairs={{2,5},{3,4},{4,3},{5,2},{6,9},{7,8},{8,7},{9,6},{10,13},{11,12},{1... | collective-permute-start | bytes 983048 | tf_op jit(solution)/shard_map/ppermute | solution.py:287
  63.0 0.0 collective-permute-done.7.refs_6_
  63.0 0.2 collective-permute-done.6.refs_5_
  63.2 0.0 collective-permute-done.10.refs_8_
  63.2 5.7 %shard_map.72 = (bf16[7,128,128]{2,1,0:T(8,128)(2,1)S(1)}, bf16[6,128,128]{2,1,0:T(8,128)(2,1)S(1)}, bf16[6,128,128]{2,1,0:T(8,128)(2,1)S(1)}, bf16[8,128,128]{2...) custom-call(s32[16]{0:T(128)S(1)} %copy-done.3, ...), custom_call_target="tpu_custom_call" | custom-call | tf_op jit(solution)/shard_map/pallas_call | solution.py:196
  68.9 4.4 %collective-permute-done.5.refs_6_ = bf16[5,2,128,128]{3,2,1,0:T(8,128)(2,1)S(1)} collective-permute-done((bf16[5,2,128,128]{3,2,1,0:T(8,128)(2,1)S(1)}, bf16[5,2,128,128]{3,2,1,0:T(8,128)(2,1)S(1)}, u32[]{:S(2)}, u32[]{:S(2)}) %collective-permute-start.5) | collective-permute-done | bytes 327712 | tf_op jit(solution)/shard_map/ppermute | solution.py:287
  73.3 0.5 collective-permute-done.4.refs_5_
  73.8 2.6 %shard_map.73 = (bf16[7,128,128]{2,1,0:T(8,128)(2,1)S(1)}, bf16[6,128,128]{2,1,0:T(8,128)(2,1)S(1)}, bf16[6,128,128]{2,1,0:T(8,128)(2,1)S(1)}, bf16[8,128,128]{2...) custom-call(s32[16]{0:T(128)S(1)} %copy-done.3, ...), custom_call_target="tpu_custom_call" | custom-call | flops 104857600 | bytes 7340032 | tf_op jit(solution)/shard_map/pallas_call | solution.py:196
  76.4 0.9 collective-permute-start.11
  77.3 0.1 collective-permute-start.17
  77.4 1.7 %collective-permute-start.16 = (bf16[6,128,128]{2,1,0:T(8,128)(2,1)S(1)}, bf16[6,128,128]{2,1,0:T(8,128)(2,1)S(1)}, u32[]{:S(2)}, u32[]{:S(2)}) collective-permute-start(bf16[6,128,128]{2,1,0:T(8,128)(2,1)S(1)} %get-tuple-element.80), channel_id=1, source_target_pairs={{0,2},{1,3},{2,0},{3,1},{4,6},{5,7},{6,4},{7,5},{8,10},{9,11},{10,... | collective-permute-start | bytes 589832 | tf_op jit(solution)/shard_map/ppermute | solution.py:287
  79.1 0.0 collective-permute-done.11.sib
  79.1 0.3 shard_map.74
  79.4 3.0 %collective-permute-start.14 = (bf16[8,128,128]{2,1,0:T(8,128)(2,1)S(1)}, bf16[8,128,128]{2,1,0:T(8,128)(2,1)S(1)}, u32[]{:S(2)}, u32[]{:S(2)}) collective-permute-start(bf16[8,128,128]{2,1,0:T(8,128)(2,1)S(1)} %get-tuple-element.78), channel_id=1, source_target_pairs={{2,4},{3,5},{4,2},{5,3},{6,8},{7,9},{8,6},{9,7},{10,12},{11,13},{1... | collective-permute-start | bytes 786440 | tf_op jit(solution)/shard_map/ppermute | solution.py:287
  82.4 3.5 %collective-permute-start.13 = (bf16[6,128,128]{2,1,0:T(8,128)(2,1)S(1)}, bf16[6,128,128]{2,1,0:T(8,128)(2,1)S(1)}, u32[]{:S(2)}, u32[]{:S(2)}) collective-permute-start(bf16[6,128,128]{2,1,0:T(8,128)(2,1)S(1)} %get-tuple-element.77), channel_id=1, source_target_pairs={{0,4},{1,5},{4,8},{5,9},{6,2},{7,3},{8,12},{9,13},{10,6},{11,7},{1... | collective-permute-start | bytes 589832 | tf_op jit(solution)/shard_map/ppermute | solution.py:287
  86.0 0.9 collective-permute-start.12
  86.8 0.0 collective-permute-done.17.refs_1_
  86.8 1.0 %shard_map.75 = (f32[1,5,128,512]{3,2,1,0:T(8,128)}, f32[1,5,128,512]{3,2,1,0:T(8,128)}) custom-call(bf16[7,128,128]{2,1,0:T(8,128)(2,1)S(1)} %get-tuple-element.81.refs_0_, bf16[7,128,128]{2,1,0:T(8,128)(2,1)S(1)} %collective-permute-done.17.refs_1_), custom_call_target="tpu_custom_call" | custom-call | flops 229376 | bytes 1376256 | tf_op jit(solution)/shard_map/pallas_call | solution.py:260
  87.9 0.7 collective-permute-start.15
  88.6 0.0 collective-permute-done.16.refs_0_
  88.6 0.8 shard_map.76
  89.4 0.0 collective-permute-done.15.refs_2_
  89.4 1.6 %collective-permute-done.13.refs_0_ = bf16[6,128,128]{2,1,0:T(8,128)(2,1)S(1)} collective-permute-done((bf16[6,128,128]{2,1,0:T(8,128)(2,1)S(1)}, bf16[6,128,128]{2,1,0:T(8,128)(2,1)S(1)}, u32[]{:S(2)}, u32[]{:S(2)}) %collective-permute-start.13) | collective-permute-done | bytes 196640 | tf_op jit(solution)/shard_map/ppermute | solution.py:287
  91.0 0.0 collective-permute-done.14.refs_1_
  91.0 1.1 %shard_map.77 = (f32[1,5,128,512]{3,2,1,0:T(8,128)}, f32[1,5,128,512]{3,2,1,0:T(8,128)}) custom-call(bf16[6,128,128]{2,1,0:T(8,128)(2,1)S(1)} %collective-permute-done.13.refs_0_, bf16[8,128,128]{2,1,0:T(8,128)(2,1)S(1)} %collective-permute-done.14.refs_1_, ...), custom_call_target="tpu_custom_call", output_to_operand_aliasing={{0}: (3, {}), {1}: (4, {})} | custom-call | flops 262144 | bytes 1572864 | tf_op jit(solution)/shard_map/pallas_call | solution.py:260
  92.1 2.6 %collective-permute-done.12.refs_0_ = bf16[6,128,128]{2,1,0:T(8,128)(2,1)S(1)} collective-permute-done((bf16[6,128,128]{2,1,0:T(8,128)(2,1)S(1)}, bf16[6,128,128]{2,1,0:T(8,128)(2,1)S(1)}, u32[]{:S(2)}, u32[]{:S(2)}) %collective-permute-start.12) | collective-permute-done | bytes 196640 | tf_op jit(solution)/shard_map/ppermute | solution.py:287
  94.7 0.8 shard_map.78
  (4 shorter events, 0.1 us)
Async XLA Ops:
  4.0 8.4 %copy-start.4 = (bf16[16,2,128,128]{3,2,1,0:T(8,128)(2,1)S(1)}, bf16[16,2,128,128]{3,2,1,0:T(8,128)(2,1)}, u32[]{:S(2)}) copy-start(bf16[16,2,128,128]{3,2,1,0:T(8,128)(2,1)} %get-tuple-element.59) | copy-start | bytes 3145732
  4.0 29.8 %copy-start.2 = (bf16[2,256,256]{2,1,0:T(8,128)(2,1)S(1)}, bf16[2,256,256]{2,1,0:T(8,128)(2,1)}, u32[]{:S(2)}) copy-start(bf16[2,256,256]{2,1,0:T(8,128)(2,1)} %constant.4.clone.table_ref) | copy-start | bytes 786436
  4.0 29.8 %copy-start.3 = (s32[16]{0:T(128)S(1)}, s32[16]{0:T(128)}, u32[]{:S(2)}) copy-start(s32[16]{0:T(128)} %counts_ref.7) | copy-start | bytes 196
  4.0 26.3 %collective-permute-start.1 = (bf16[16,2,128,128]{3,2,1,0:T(8,128)(2,1)}, bf16[16,2,128,128]{3,2,1,0:T(8,128)(2,1)S(1)}, u32[]{:S(2)}, u32[]{:S(2)}) collective-permute-start(bf16[16,2,128,128]{3,2,1,0:T(8,128)(2,1)} %get-tuple-element.45), channel_id=1, source_target_pairs={{0,2},{1,3},{2,0},{3,1},{4,6},{5,7},{6,4},{7,5},{8,10},{9,11},{10,... | collective-permute-start | bytes 3145736 | tf_op jit(solution)/shard_map/ppermute | solution.py:287
  9.2 21.2 %collective-permute-start = (bf16[16,2,128,128]{3,2,1,0:T(8,128)(2,1)}, bf16[16,2,128,128]{3,2,1,0:T(8,128)(2,1)S(1)}, u32[]{:S(2)}, u32[]{:S(2)}) collective-permute-start(bf16[16,2,128,128]{3,2,1,0:T(8,128)(2,1)} %get-tuple-element.48), channel_id=1, source_target_pairs={{0,1},{1,0},{2,3},{3,2},{4,5},{5,4},{6,7},{7,6},{8,9},{9,8},{10,11... | collective-permute-start | bytes 3145736 | tf_op jit(solution)/shard_map/ppermute | solution.py:287
  9.2 45.2 %collective-permute-start.9 = (bf16[32,2,128,128]{3,2,1,0:T(8,128)(2,1)}, bf16[32,2,128,128]{3,2,1,0:T(8,128)(2,1)S(1)}, u32[]{:S(2)}, u32[]{:S(2)}) collective-permute-start(bf16[32,2,128,128]{3,2,1,0:T(8,128)(2,1)} %get-tuple-element.47.refs_0_), channel_id=1, source_target_pairs={{1,5},{5,9},{6,2},{9,13},{10,6},{14,10},{17,21},{21,25},{22,18},{2... | collective-permute-start | bytes 6291464 | tf_op jit(solution)/shard_map/ppermute | solution.py:287
  10.0 48.6 %collective-permute-start.3 = (bf16[32,2,128,128]{3,2,1,0:T(8,128)(2,1)}, bf16[32,2,128,128]{3,2,1,0:T(8,128)(2,1)S(1)}, u32[]{:S(2)}, u32[]{:S(2)}) collective-permute-start(bf16[32,2,128,128]{3,2,1,0:T(8,128)(2,1)} %get-tuple-element.47.refs_0_), channel_id=1, source_target_pairs={{2,6},{3,7},{4,0},{5,1},{6,10},{7,11},{8,4},{9,5},{10,14},{11,15},... | collective-permute-start | bytes 6291464 | tf_op jit(solution)/shard_map/ppermute | solution.py:287
  12.4 38.3 %collective-permute-start.2 = (bf16[16,2,128,128]{3,2,1,0:T(8,128)(2,1)S(1)}, bf16[16,2,128,128]{3,2,1,0:T(8,128)(2,1)S(1)}, u32[]{:S(2)}, u32[]{:S(2)}) collective-permute-start(bf16[16,2,128,128]{3,2,1,0:T(8,128)(2,1)S(1)} %copy-done.4), channel_id=1, source_target_pairs={{0,3},{1,2},{2,1},{3,0},{4,7},{5,6},{6,5},{7,4},{8,11},{9,10},{10,... | collective-permute-start | bytes 3145736 | tf_op jit(solution)/shard_map/ppermute | solution.py:287
  30.4 30.7 %collective-permute-start.8 = (bf16[16,2,128,128]{3,2,1,0:T(8,128)(2,1)S(1)}, bf16[16,2,128,128]{3,2,1,0:T(8,128)(2,1)S(1)}, u32[]{:S(2)}, u32[]{:S(2)}) collective-permute-start(bf16[16,2,128,128]{3,2,1,0:T(8,128)(2,1)S(1)} %collective-permute-done.1.refs_2_), channel_id=1, source_target_pairs={{0,4},{1,5},{4,8},{5,9},{6,2},{7,3},{8,12},{9,13},{10,6},{11,7},{1... | collective-permute-start | bytes 3145736 | tf_op jit(solution)/shard_map/ppermute | solution.py:287
  33.9 1.6 %copy-start = (bf16[32,2,128,128]{3,2,1,0:T(8,128)(2,1)S(1)}, bf16[32,2,128,128]{3,2,1,0:T(8,128)(2,1)}, u32[]{:S(2)}) copy-start(bf16[32,2,128,128]{3,2,1,0:T(8,128)(2,1)} %get-tuple-element.47.refs_0_) | copy-start | bytes 6291460
  50.8 5.1 %copy-start.1 = (bf16[32,2,128,128]{3,2,1,0:T(8,128)(2,1)S(1)}, bf16[32,2,128,128]{3,2,1,0:T(8,128)(2,1)}, u32[]{:S(2)}) copy-start(bf16[32,2,128,128]{3,2,1,0:T(8,128)(2,1)} %get-tuple-element.47.refs_0_) | copy-start | bytes 6291460
  50.8 23.0 %collective-permute-start.4 = (bf16[11,2,128,128]{3,2,1,0:T(8,128)(2,1)S(1)}, bf16[11,2,128,128]{3,2,1,0:T(8,128)(2,1)S(1)}, u32[]{:S(2)}, u32[]{:S(2)}) collective-permute-start(bf16[11,2,128,128]{3,2,1,0:T(8,128)(2,1)S(1)} %slice.24), channel_id=1, source_target_pairs={{0,4},{1,5},{4,8},{5,9},{6,2},{7,3},{8,12},{9,13},{10,6},{11,7},{1... | collective-permute-start | bytes 2162696 | tf_op jit(solution)/shard_map/ppermute | solution.py:287
  54.5 8.7 %collective-permute-start.10 = (bf16[16,2,128,128]{3,2,1,0:T(8,128)(2,1)S(1)}, bf16[16,2,128,128]{3,2,1,0:T(8,128)(2,1)S(1)}, u32[]{:S(2)}, u32[]{:S(2)}) collective-permute-start(bf16[16,2,128,128]{3,2,1,0:T(8,128)(2,1)S(1)} %slice.28), channel_id=1, source_target_pairs={{1,0},{2,3},{5,4},{6,7},{9,8},{10,11},{13,12},{14,15},{17,16},{18,... | collective-permute-start | bytes 3145736 | tf_op jit(solution)/shard_map/ppermute | solution.py:287
  58.8 4.2 %collective-permute-start.7 = (bf16[8,2,128,128]{3,2,1,0:T(8,128)(2,1)S(1)}, bf16[8,2,128,128]{3,2,1,0:T(8,128)(2,1)S(1)}, u32[]{:S(2)}, u32[]{:S(2)}) collective-permute-start(bf16[8,2,128,128]{3,2,1,0:T(8,128)(2,1)S(1)} %get-tuple-element.88), channel_id=1, source_target_pairs={{0,1},{1,0},{2,3},{3,2},{4,5},{5,4},{6,7},{7,6},{8,9},{9,8},{10,11... | collective-permute-start | bytes 1572872 | tf_op jit(solution)/shard_map/ppermute | solution.py:287
  60.9 2.3 %collective-permute-start.6 = (bf16[8,2,128,128]{3,2,1,0:T(8,128)(2,1)S(1)}, bf16[8,2,128,128]{3,2,1,0:T(8,128)(2,1)S(1)}, u32[]{:S(2)}, u32[]{:S(2)}) collective-permute-start(bf16[8,2,128,128]{3,2,1,0:T(8,128)(2,1)S(1)} %get-tuple-element.89), channel_id=1, source_target_pairs={{0,1},{1,0},{2,3},{3,2},{4,5},{5,4},{6,7},{7,6},{8,9},{9,8},{10,11... | collective-permute-start | bytes 1572872 | tf_op jit(solution)/shard_map/ppermute | solution.py:287
  61.0 12.2 %collective-permute-start.5 = (bf16[5,2,128,128]{3,2,1,0:T(8,128)(2,1)S(1)}, bf16[5,2,128,128]{3,2,1,0:T(8,128)(2,1)S(1)}, u32[]{:S(2)}, u32[]{:S(2)}) collective-permute-start(bf16[5,2,128,128]{3,2,1,0:T(8,128)(2,1)S(1)} %slice.25), channel_id=1, source_target_pairs={{2,5},{3,4},{4,3},{5,2},{6,9},{7,8},{8,7},{9,6},{10,13},{11,12},{1... | collective-permute-start | bytes 983048 | tf_op jit(solution)/shard_map/ppermute | solution.py:287
  76.4 2.6 %collective-permute-start.11 = (bf16[14,128,128]{2,1,0:T(8,128)(2,1)S(1)}, bf16[14,128,128]{2,1,0:T(8,128)(2,1)S(1)}, u32[]{:S(2)}, u32[]{:S(2)}) collective-permute-start(bf16[14,128,128]{2,1,0:T(8,128)(2,1)S(1)} %slice.29), channel_id=1, source_target_pairs={{0,1},{1,0},{2,3},{3,2},{4,5},{5,4},{6,7},{7,6},{8,9},{9,8},{10,11... | collective-permute-start | bytes 1376264 | tf_op jit(solution)/shard_map/ppermute | solution.py:287
  77.3 9.5 %collective-permute-start.17 = (bf16[7,128,128]{2,1,0:T(8,128)(2,1)S(1)}, bf16[7,128,128]{2,1,0:T(8,128)(2,1)S(1)}, u32[]{:S(2)}, u32[]{:S(2)}) collective-permute-start(bf16[7,128,128]{2,1,0:T(8,128)(2,1)S(1)} %slice.31), channel_id=1, source_target_pairs={{0,1},{1,0},{2,3},{3,2},{4,5},{5,4},{6,7},{7,6},{8,9},{9,8},{10,11... | collective-permute-start | bytes 688136 | tf_op jit(solution)/shard_map/ppermute | solution.py:287
  77.4 11.1 %collective-permute-start.16 = (bf16[6,128,128]{2,1,0:T(8,128)(2,1)S(1)}, bf16[6,128,128]{2,1,0:T(8,128)(2,1)S(1)}, u32[]{:S(2)}, u32[]{:S(2)}) collective-permute-start(bf16[6,128,128]{2,1,0:T(8,128)(2,1)S(1)} %get-tuple-element.80), channel_id=1, source_target_pairs={{0,2},{1,3},{2,0},{3,1},{4,6},{5,7},{6,4},{7,5},{8,10},{9,11},{10,... | collective-permute-start | bytes 589832 | tf_op jit(solution)/shard_map/ppermute | solution.py:287
  79.4 11.6 %collective-permute-start.14 = (bf16[8,128,128]{2,1,0:T(8,128)(2,1)S(1)}, bf16[8,128,128]{2,1,0:T(8,128)(2,1)S(1)}, u32[]{:S(2)}, u32[]{:S(2)}) collective-permute-start(bf16[8,128,128]{2,1,0:T(8,128)(2,1)S(1)} %get-tuple-element.78), channel_id=1, source_target_pairs={{2,4},{3,5},{4,2},{5,3},{6,8},{7,9},{8,6},{9,7},{10,12},{11,13},{1... | collective-permute-start | bytes 786440 | tf_op jit(solution)/shard_map/ppermute | solution.py:287
  82.4 8.6 %collective-permute-start.13 = (bf16[6,128,128]{2,1,0:T(8,128)(2,1)S(1)}, bf16[6,128,128]{2,1,0:T(8,128)(2,1)S(1)}, u32[]{:S(2)}, u32[]{:S(2)}) collective-permute-start(bf16[6,128,128]{2,1,0:T(8,128)(2,1)S(1)} %get-tuple-element.77), channel_id=1, source_target_pairs={{0,4},{1,5},{4,8},{5,9},{6,2},{7,3},{8,12},{9,13},{10,6},{11,7},{1... | collective-permute-start | bytes 589832 | tf_op jit(solution)/shard_map/ppermute | solution.py:287
  86.0 8.7 %collective-permute-start.12 = (bf16[6,128,128]{2,1,0:T(8,128)(2,1)S(1)}, bf16[6,128,128]{2,1,0:T(8,128)(2,1)S(1)}, u32[]{:S(2)}, u32[]{:S(2)}) collective-permute-start(bf16[6,128,128]{2,1,0:T(8,128)(2,1)S(1)} %slice.32), channel_id=1, source_target_pairs={{0,2},{1,3},{2,0},{3,1},{4,6},{5,7},{6,4},{7,5},{8,10},{9,11},{10,... | collective-permute-start | bytes 589832 | tf_op jit(solution)/shard_map/ppermute | solution.py:287
  87.9 1.5 %collective-permute-start.15 = (bf16[2,128,128]{2,1,0:T(8,128)(2,1)S(1)}, bf16[2,128,128]{2,1,0:T(8,128)(2,1)S(1)}, u32[]{:S(2)}, u32[]{:S(2)}) collective-permute-start(bf16[2,128,128]{2,1,0:T(8,128)(2,1)S(1)} %get-tuple-element.79), channel_id=1, source_target_pairs={{2,6},{5,1},{6,10},{9,5},{10,14},{13,9},{18,22},{21,17},{22,26},{2... | collective-permute-start | bytes 196616 | tf_op jit(solution)/shard_map/ppermute | solution.py:287

commit v8 on v7

--- a/solution.py
+++ b/solution.py
@@ -321,7 +321,7 @@
     z1a, z1b = send(z[windows:windows + half], 1, HERE), send(z[windows + half:], 1, HERE)
     other = ((5, 0, half), (6, half, windows))
     parts = correlate(
-        counts, tables, (t01, u1, y2, y3, z, z1a, z1b, r2, e1, e), ((BEYOND, INNER, FIRST), (BEYOND, OUTER, FIRST)), sources=(
+        counts, tables, (t01, u1, y2, y3, z, z1a, z1b, r2, e1, e), ((BEYOND, INNER + FIRST), (BEYOND, OUTER + FIRST)), sources=(
             whole((0, 0), (1, 1), (2, 2), (3, 3), (4, 4), (-2, 7), (-3, 8)) | {5: other},
             whole((0, 1), (1, 0), (2, 3), (3, 2), (5, 4), (-1, 7), (-3, 9)) | {4: other}), filled=parts, weight=0)
     last = ((5, 0, relayed(windows)), (6, relayed(windows), windows))

time: 96.1 us -> 96.1 us (level)
  no operation moved by 1% of the time
where the time goes in v8:
time: 96.1 us; the launch traced here: 95.5 us
  waiting for transfers between devices  40.1 us (42%)
  starting transfers between devices  29.5 us (31%)
  Pallas kernels  23 us (24%)
  local copies, waits for them, and re-layouts  1.95 us (2%)
    ppermute x18, waiting for transfers between devices, send(): return lax.ppermute(value, 'chan', pairs)  40.1 us
    ppermute x18, starting transfers between devices, send(): return lax.ppermute(value, 'chan', pairs)  29.5 us
    pallas_call x4, Pallas kernels, correlate(): pl.pallas_call(functools.partial(correlate_body, work=work, sources=sourc...  12.1 us
    pallas_call x2, Pallas kernels, whiten(): pl.pallas_call(whiten_body, grid=(windows // STEP,), in_specs=[pl.BlockSp...  6.89 us
    pallas_call x4, Pallas kernels, assemble(): pl.pallas_call(functools.partial(assemble_body, plan=plan, count=len(part...  3.7 us
  transfers between devices with their start and end apart: 18, of which 8 were waited for; matrix products, arithmetic and copies ran while one was open for 0% of the time, Pallas kernels for 17%

profile of v8, /device:TPU:16, one launch (start us, length us, event | category | flops | bytes accessed | tf_op | source)
XLA Modules:
  0.0 95.5 jit_solution(10340315382143261009)
XLA Ops:
  0.6 3.4 %shard_map.68 = (bf16[16,2,128,128]{3,2,1,0:T(8,128)(2,1)}, bf16[16,2,128,128]{3,2,1,0:T(8,128)(2,1)}) custom-call(s32[16,16]{1,0:T(8,128)} %mask_ref.2, bf16[256,256]{1,0:T(8,128)(2,1)} %constant.5.clone.table_ref, bf16[1,16,256,512]{3,2,1,0:T(8,128)(2,1)} %traces_ref.3), custom_call_target="tpu_custom_call" | custom-call | flops 536870912 | bytes 4194304 | tf_op jit(solution)/shard_map/pallas_call | solution.py:108
  4.0 0.0 copy-start.4
  4.0 0.0 copy-start.2
  4.0 0.0 copy-start.3
  4.0 1.6 %collective-permute-start.1 = (bf16[16,2,128,128]{3,2,1,0:T(8,128)(2,1)}, bf16[16,2,128,128]{3,2,1,0:T(8,128)(2,1)S(1)}, u32[]{:S(2)}, u32[]{:S(2)}) collective-permute-start(bf16[16,2,128,128]{3,2,1,0:T(8,128)(2,1)} %get-tuple-element.45), channel_id=1, source_target_pairs={{0,2},{1,3},{2,0},{3,1},{4,6},{5,7},{6,4},{7,5},{8,10},{9,11},{10,... | collective-permute-start | bytes 3145736 | tf_op jit(solution)/shard_map/ppermute | solution.py:287
  5.6 3.5 %shard_map.69 = (bf16[32,2,128,128]{3,2,1,0:T(8,128)(2,1)}, bf16[16,2,128,128]{3,2,1,0:T(8,128)(2,1)}) custom-call(s32[16,16]{1,0:T(8,128)} %mask_ref.2, bf16[256,256]{1,0:T(8,128)(2,1)} %constant.5.clone.table_ref, bf16[1,16,256,512]{3,2,1,0:T(8,128)(2,1)} %traces_ref.3), custom_call_target="tpu_custom_call" | custom-call | flops 536870912 | bytes 4194304 | tf_op jit(solution)/shard_map/pallas_call | solution.py:108
  9.2 0.1 collective-permute-start
  9.2 0.8 collective-permute-start.9
  10.0 2.4 %collective-permute-start.3 = (bf16[32,2,128,128]{3,2,1,0:T(8,128)(2,1)}, bf16[32,2,128,128]{3,2,1,0:T(8,128)(2,1)S(1)}, u32[]{:S(2)}, u32[]{:S(2)}) collective-permute-start(bf16[32,2,128,128]{3,2,1,0:T(8,128)(2,1)} %get-tuple-element.47.refs_0_), channel_id=1, source_target_pairs={{2,6},{3,7},{4,0},{5,1},{6,10},{7,11},{8,4},{9,5},{10,14},{11,15},... | collective-permute-start | bytes 6291464 | tf_op jit(solution)/shard_map/ppermute | solution.py:287
  12.4 0.0 copy-done.4
  12.4 1.5 %collective-permute-start.2 = (bf16[16,2,128,128]{3,2,1,0:T(8,128)(2,1)S(1)}, bf16[16,2,128,128]{3,2,1,0:T(8,128)(2,1)S(1)}, u32[]{:S(2)}, u32[]{:S(2)}) collective-permute-start(bf16[16,2,128,128]{3,2,1,0:T(8,128)(2,1)S(1)} %copy-done.4), channel_id=1, source_target_pairs={{0,3},{1,2},{2,1},{3,0},{4,7},{5,6},{6,5},{7,4},{8,11},{9,10},{10,... | collective-permute-start | bytes 3145736 | tf_op jit(solution)/shard_map/ppermute | solution.py:287
  13.9 16.5 %collective-permute-done.1.refs_2_ = bf16[16,2,128,128]{3,2,1,0:T(8,128)(2,1)S(1)} collective-permute-done((bf16[16,2,128,128]{3,2,1,0:T(8,128)(2,1)}, bf16[16,2,128,128]{3,2,1,0:T(8,128)(2,1)S(1)}, u32[]{:S(2)}, u32[]{:S(2)}) %collective-permute-start.1) | collective-permute-done | bytes 1048608 | tf_op jit(solution)/shard_map/ppermute | solution.py:287
  30.4 0.0 collective-permute-done.refs_1_
  30.4 3.5 %collective-permute-start.8 = (bf16[16,2,128,128]{3,2,1,0:T(8,128)(2,1)S(1)}, bf16[16,2,128,128]{3,2,1,0:T(8,128)(2,1)S(1)}, u32[]{:S(2)}, u32[]{:S(2)}) collective-permute-start(bf16[16,2,128,128]{3,2,1,0:T(8,128)(2,1)S(1)} %collective-permute-done.1.refs_2_), channel_id=1, source_target_pairs={{0,4},{1,5},{4,8},{5,9},{6,2},{7,3},{8,12},{9,13},{10,6},{11,7},{1... | collective-permute-start | bytes 3145736 | tf_op jit(solution)/shard_map/ppermute | solution.py:287
  33.8 0.0 copy-done.2
  33.9 0.0 copy-done.3
  33.9 0.0 copy-start
  33.9 1.6 %copy-done = bf16[32,2,128,128]{3,2,1,0:T(8,128)(2,1)S(1)} copy-done((bf16[32,2,128,128]{3,2,1,0:T(8,128)(2,1)S(1)}, bf16[32,2,128,128]{3,2,1,0:T(8,128)(2,1)}, u32[]{:S(2)}) %copy-start) | copy-done | bytes 2097176
  35.5 1.9 %shard_map.70 = (bf16[7,128,128]{2,1,0:T(8,128)(2,1)S(1)}, bf16[6,128,128]{2,1,0:T(8,128)(2,1)S(1)}, bf16[6,128,128]{2,1,0:T(8,128)(2,1)S(1)}, bf16[8,128,128]{2...) custom-call(s32[16]{0:T(128)S(1)} %copy-done.3, ...), custom_call_target="tpu_custom_call" | custom-call | flops 15728640000 | bytes 3145728 | tf_op jit(solution)/shard_map/pallas_call | solution.py:196
  37.4 13.3 %collective-permute-done.2.refs_3_ = bf16[16,2,128,128]{3,2,1,0:T(8,128)(2,1)S(1)} collective-permute-done((bf16[16,2,128,128]{3,2,1,0:T(8,128)(2,1)S(1)}, bf16[16,2,128,128]{3,2,1,0:T(8,128)(2,1)S(1)}, u32[]{:S(2)}, u32[]{:S(2)}) %collective-permute-start.2) | collective-permute-done | bytes 1048608 | tf_op jit(solution)/shard_map/ppermute | solution.py:287
  50.7 0.1 slice.24
  50.8 0.0 copy-start.1
  50.8 3.6 %collective-permute-start.4 = (bf16[11,2,128,128]{3,2,1,0:T(8,128)(2,1)S(1)}, bf16[11,2,128,128]{3,2,1,0:T(8,128)(2,1)S(1)}, u32[]{:S(2)}, u32[]{:S(2)}) collective-permute-start(bf16[11,2,128,128]{3,2,1,0:T(8,128)(2,1)S(1)} %slice.24), channel_id=1, source_target_pairs={{0,4},{1,5},{4,8},{5,9},{6,2},{7,3},{8,12},{9,13},{10,6},{11,7},{1... | collective-permute-start | bytes 2162696 | tf_op jit(solution)/shard_map/ppermute | solution.py:287
  54.4 0.0 collective-permute-done.9.refs_9_
  54.4 0.1 slice.28
  54.5 1.3 %collective-permute-start.10 = (bf16[16,2,128,128]{3,2,1,0:T(8,128)(2,1)S(1)}, bf16[16,2,128,128]{3,2,1,0:T(8,128)(2,1)S(1)}, u32[]{:S(2)}, u32[]{:S(2)}) collective-permute-start(bf16[16,2,128,128]{3,2,1,0:T(8,128)(2,1)S(1)} %slice.28), channel_id=1, source_target_pairs={{1,0},{2,3},{5,4},{6,7},{9,8},{10,11},{13,12},{14,15},{17,16},{18,... | collective-permute-start | bytes 3145736 | tf_op jit(solution)/shard_map/ppermute | solution.py:287
  55.9 0.0 copy-done.1
  55.9 2.2 %shard_map.71 = (bf16[7,128,128]{2,1,0:T(8,128)(2,1)S(1)}, bf16[6,128,128]{2,1,0:T(8,128)(2,1)S(1)}, bf16[6,128,128]{2,1,0:T(8,128)(2,1)S(1)}, bf16[8,128,128]{2...) custom-call(s32[16]{0:T(128)S(1)} %copy-done.3, ...), custom_call_target="tpu_custom_call" | custom-call | flops 15728640000 | bytes 4194304 | tf_op jit(solution)/shard_map/pallas_call | solution.py:196
  58.0 0.6 collective-permute-done.3.refs_4_
  58.6 0.1 fusion
  58.8 2.2 %collective-permute-start.7 = (bf16[8,2,128,128]{3,2,1,0:T(8,128)(2,1)S(1)}, bf16[8,2,128,128]{3,2,1,0:T(8,128)(2,1)S(1)}, u32[]{:S(2)}, u32[]{:S(2)}) collective-permute-start(bf16[8,2,128,128]{3,2,1,0:T(8,128)(2,1)S(1)} %get-tuple-element.88), channel_id=1, source_target_pairs={{0,1},{1,0},{2,3},{3,2},{4,5},{5,4},{6,7},{7,6},{8,9},{9,8},{10,11... | collective-permute-start | bytes 1572872 | tf_op jit(solution)/shard_map/ppermute | solution.py:287
  60.9 0.1 collective-permute-start.6
  61.0 0.0 collective-permute-done.8.refs_7_
  61.0 1.9 %collective-permute-start.5 = (bf16[5,2,128,128]{3,2,1,0:T(8,128)(2,1)S(1)}, bf16[5,2,128,128]{3,2,1,0:T(8,128)(2,1)S(1)}, u32[]{:S(2)}, u32[]{:S(2)}) collective-permute-start(bf16[5,2,128,128]{3,2,1,0:T(8,128)(2,1)S(1)} %slice.25), channel_id=1, source_target_pairs={{2,5},{3,4},{4,3},{5,2},{6,9},{7,8},{8,7},{9,6},{10,13},{11,12},{1... | collective-permute-start | bytes 983048 | tf_op jit(solution)/shard_map/ppermute | solution.py:287
  63.0 0.0 collective-permute-done.7.refs_6_
  63.0 0.2 collective-permute-done.6.refs_5_
  63.2 0.0 collective-permute-done.10.refs_8_
  63.2 5.4 %shard_map.72 = (bf16[7,128,128]{2,1,0:T(8,128)(2,1)S(1)}, bf16[6,128,128]{2,1,0:T(8,128)(2,1)S(1)}, bf16[6,128,128]{2,1,0:T(8,128)(2,1)S(1)}, bf16[8,128,128]{2...) custom-call(s32[16]{0:T(128)S(1)} %copy-done.3, ...), custom_call_target="tpu_custom_call" | custom-call | tf_op jit(solution)/shard_map/pallas_call | solution.py:196
  68.6 4.7 %collective-permute-done.5.refs_6_ = bf16[5,2,128,128]{3,2,1,0:T(8,128)(2,1)S(1)} collective-permute-done((bf16[5,2,128,128]{3,2,1,0:T(8,128)(2,1)S(1)}, bf16[5,2,128,128]{3,2,1,0:T(8,128)(2,1)S(1)}, u32[]{:S(2)}, u32[]{:S(2)}) %collective-permute-start.5) | collective-permute-done | bytes 327712 | tf_op jit(solution)/shard_map/ppermute | solution.py:287
  73.3 0.5 collective-permute-done.4.refs_5_
  73.8 2.6 %shard_map.73 = (bf16[7,128,128]{2,1,0:T(8,128)(2,1)S(1)}, bf16[6,128,128]{2,1,0:T(8,128)(2,1)S(1)}, bf16[6,128,128]{2,1,0:T(8,128)(2,1)S(1)}, bf16[8,128,128]{2...) custom-call(s32[16]{0:T(128)S(1)} %copy-done.3, ...), custom_call_target="tpu_custom_call" | custom-call | flops 104857600 | bytes 7340032 | tf_op jit(solution)/shard_map/pallas_call | solution.py:196
  76.4 0.9 collective-permute-start.11
  77.3 0.1 collective-permute-start.17
  77.4 1.7 %collective-permute-start.16 = (bf16[6,128,128]{2,1,0:T(8,128)(2,1)S(1)}, bf16[6,128,128]{2,1,0:T(8,128)(2,1)S(1)}, u32[]{:S(2)}, u32[]{:S(2)}) collective-permute-start(bf16[6,128,128]{2,1,0:T(8,128)(2,1)S(1)} %get-tuple-element.80), channel_id=1, source_target_pairs={{0,2},{1,3},{2,0},{3,1},{4,6},{5,7},{6,4},{7,5},{8,10},{9,11},{10,... | collective-permute-start | bytes 589832 | tf_op jit(solution)/shard_map/ppermute | solution.py:287
  79.1 0.0 collective-permute-done.11.sib
  79.1 0.3 shard_map.74
  79.4 3.0 %collective-permute-start.14 = (bf16[8,128,128]{2,1,0:T(8,128)(2,1)S(1)}, bf16[8,128,128]{2,1,0:T(8,128)(2,1)S(1)}, u32[]{:S(2)}, u32[]{:S(2)}) collective-permute-start(bf16[8,128,128]{2,1,0:T(8,128)(2,1)S(1)} %get-tuple-element.78), channel_id=1, source_target_pairs={{2,4},{3,5},{4,2},{5,3},{6,8},{7,9},{8,6},{9,7},{10,12},{11,13},{1... | collective-permute-start | bytes 786440 | tf_op jit(solution)/shard_map/ppermute | solution.py:287
  82.4 3.5 %collective-permute-start.13 = (bf16[6,128,128]{2,1,0:T(8,128)(2,1)S(1)}, bf16[6,128,128]{2,1,0:T(8,128)(2,1)S(1)}, u32[]{:S(2)}, u32[]{:S(2)}) collective-permute-start(bf16[6,128,128]{2,1,0:T(8,128)(2,1)S(1)} %get-tuple-element.77), channel_id=1, source_target_pairs={{0,4},{1,5},{4,8},{5,9},{6,2},{7,3},{8,12},{9,13},{10,6},{11,7},{1... | collective-permute-start | bytes 589832 | tf_op jit(solution)/shard_map/ppermute | solution.py:287
  86.0 0.9 collective-permute-start.12
  86.8 0.0 collective-permute-done.17.refs_1_
  86.8 1.0 %shard_map.75 = (f32[1,5,128,512]{3,2,1,0:T(8,128)}, f32[1,5,128,512]{3,2,1,0:T(8,128)}) custom-call(bf16[7,128,128]{2,1,0:T(8,128)(2,1)S(1)} %get-tuple-element.81.refs_0_, bf16[7,128,128]{2,1,0:T(8,128)(2,1)S(1)} %collective-permute-done.17.refs_1_), custom_call_target="tpu_custom_call" | custom-call | flops 229376 | bytes 1376256 | tf_op jit(solution)/shard_map/pallas_call | solution.py:260
  87.9 0.7 collective-permute-start.15
  88.6 0.0 collective-permute-done.16.refs_0_
  88.6 0.8 shard_map.76
  89.4 0.0 collective-permute-done.15.refs_2_
  89.4 1.6 %collective-permute-done.13.refs_0_ = bf16[6,128,128]{2,1,0:T(8,128)(2,1)S(1)} collective-permute-done((bf16[6,128,128]{2,1,0:T(8,128)(2,1)S(1)}, bf16[6,128,128]{2,1,0:T(8,128)(2,1)S(1)}, u32[]{:S(2)}, u32[]{:S(2)}) %collective-permute-start.13) | collective-permute-done | bytes 196640 | tf_op jit(solution)/shard_map/ppermute | solution.py:287
  91.0 0.0 collective-permute-done.14.refs_1_
  91.0 1.1 %shard_map.77 = (f32[1,5,128,512]{3,2,1,0:T(8,128)}, f32[1,5,128,512]{3,2,1,0:T(8,128)}) custom-call(bf16[6,128,128]{2,1,0:T(8,128)(2,1)S(1)} %collective-permute-done.13.refs_0_, bf16[8,128,128]{2,1,0:T(8,128)(2,1)S(1)} %collective-permute-done.14.refs_1_, ...), custom_call_target="tpu_custom_call", output_to_operand_aliasing={{0}: (3, {}), {1}: (4, {})} | custom-call | flops 262144 | bytes 1572864 | tf_op jit(solution)/shard_map/pallas_call | solution.py:260
  92.1 2.6 %collective-permute-done.12.refs_0_ = bf16[6,128,128]{2,1,0:T(8,128)(2,1)S(1)} collective-permute-done((bf16[6,128,128]{2,1,0:T(8,128)(2,1)S(1)}, bf16[6,128,128]{2,1,0:T(8,128)(2,1)S(1)}, u32[]{:S(2)}, u32[]{:S(2)}) %collective-permute-start.12) | collective-permute-done | bytes 196640 | tf_op jit(solution)/shard_map/ppermute | solution.py:287
  94.7 0.8 shard_map.78
  (4 shorter events, 0.1 us)
Async XLA Ops:
  4.0 8.4 %copy-start.4 = (bf16[16,2,128,128]{3,2,1,0:T(8,128)(2,1)S(1)}, bf16[16,2,128,128]{3,2,1,0:T(8,128)(2,1)}, u32[]{:S(2)}) copy-start(bf16[16,2,128,128]{3,2,1,0:T(8,128)(2,1)} %get-tuple-element.59) | copy-start | bytes 3145732
  4.0 29.8 %copy-start.2 = (bf16[2,256,256]{2,1,0:T(8,128)(2,1)S(1)}, bf16[2,256,256]{2,1,0:T(8,128)(2,1)}, u32[]{:S(2)}) copy-start(bf16[2,256,256]{2,1,0:T(8,128)(2,1)} %constant.4.clone.table_ref) | copy-start | bytes 786436
  4.0 29.8 %copy-start.3 = (s32[16]{0:T(128)S(1)}, s32[16]{0:T(128)}, u32[]{:S(2)}) copy-start(s32[16]{0:T(128)} %counts_ref.7) | copy-start | bytes 196
  4.0 26.3 %collective-permute-start.1 = (bf16[16,2,128,128]{3,2,1,0:T(8,128)(2,1)}, bf16[16,2,128,128]{3,2,1,0:T(8,128)(2,1)S(1)}, u32[]{:S(2)}, u32[]{:S(2)}) collective-permute-start(bf16[16,2,128,128]{3,2,1,0:T(8,128)(2,1)} %get-tuple-element.45), channel_id=1, source_target_pairs={{0,2},{1,3},{2,0},{3,1},{4,6},{5,7},{6,4},{7,5},{8,10},{9,11},{10,... | collective-permute-start | bytes 3145736 | tf_op jit(solution)/shard_map/ppermute | solution.py:287
  9.2 21.2 %collective-permute-start = (bf16[16,2,128,128]{3,2,1,0:T(8,128)(2,1)}, bf16[16,2,128,128]{3,2,1,0:T(8,128)(2,1)S(1)}, u32[]{:S(2)}, u32[]{:S(2)}) collective-permute-start(bf16[16,2,128,128]{3,2,1,0:T(8,128)(2,1)} %get-tuple-element.48), channel_id=1, source_target_pairs={{0,1},{1,0},{2,3},{3,2},{4,5},{5,4},{6,7},{7,6},{8,9},{9,8},{10,11... | collective-permute-start | bytes 3145736 | tf_op jit(solution)/shard_map/ppermute | solution.py:287
  9.2 45.2 %collective-permute-start.9 = (bf16[32,2,128,128]{3,2,1,0:T(8,128)(2,1)}, bf16[32,2,128,128]{3,2,1,0:T(8,128)(2,1)S(1)}, u32[]{:S(2)}, u32[]{:S(2)}) collective-permute-start(bf16[32,2,128,128]{3,2,1,0:T(8,128)(2,1)} %get-tuple-element.47.refs_0_), channel_id=1, source_target_pairs={{1,5},{5,9},{6,2},{9,13},{10,6},{14,10},{17,21},{21,25},{22,18},{2... | collective-permute-start | bytes 6291464 | tf_op jit(solution)/shard_map/ppermute | solution.py:287
  10.0 48.6 %collective-permute-start.3 = (bf16[32,2,128,128]{3,2,1,0:T(8,128)(2,1)}, bf16[32,2,128,128]{3,2,1,0:T(8,128)(2,1)S(1)}, u32[]{:S(2)}, u32[]{:S(2)}) collective-permute-start(bf16[32,2,128,128]{3,2,1,0:T(8,128)(2,1)} %get-tuple-element.47.refs_0_), channel_id=1, source_target_pairs={{2,6},{3,7},{4,0},{5,1},{6,10},{7,11},{8,4},{9,5},{10,14},{11,15},... | collective-permute-start | bytes 6291464 | tf_op jit(solution)/shard_map/ppermute | solution.py:287
  12.4 38.3 %collective-permute-start.2 = (bf16[16,2,128,128]{3,2,1,0:T(8,128)(2,1)S(1)}, bf16[16,2,128,128]{3,2,1,0:T(8,128)(2,1)S(1)}, u32[]{:S(2)}, u32[]{:S(2)}) collective-permute-start(bf16[16,2,128,128]{3,2,1,0:T(8,128)(2,1)S(1)} %copy-done.4), channel_id=1, source_target_pairs={{0,3},{1,2},{2,1},{3,0},{4,7},{5,6},{6,5},{7,4},{8,11},{9,10},{10,... | collective-permute-start | bytes 3145736 | tf_op jit(solution)/shard_map/ppermute | solution.py:287
  30.4 30.7 %collective-permute-start.8 = (bf16[16,2,128,128]{3,2,1,0:T(8,128)(2,1)S(1)}, bf16[16,2,128,128]{3,2,1,0:T(8,128)(2,1)S(1)}, u32[]{:S(2)}, u32[]{:S(2)}) collective-permute-start(bf16[16,2,128,128]{3,2,1,0:T(8,128)(2,1)S(1)} %collective-permute-done.1.refs_2_), channel_id=1, source_target_pairs={{0,4},{1,5},{4,8},{5,9},{6,2},{7,3},{8,12},{9,13},{10,6},{11,7},{1... | collective-permute-start | bytes 3145736 | tf_op jit(solution)/shard_map/ppermute | solution.py:287
  33.9 1.6 %copy-start = (bf16[32,2,128,128]{3,2,1,0:T(8,128)(2,1)S(1)}, bf16[32,2,128,128]{3,2,1,0:T(8,128)(2,1)}, u32[]{:S(2)}) copy-start(bf16[32,2,128,128]{3,2,1,0:T(8,128)(2,1)} %get-tuple-element.47.refs_0_) | copy-start | bytes 6291460
  50.8 5.1 %copy-start.1 = (bf16[32,2,128,128]{3,2,1,0:T(8,128)(2,1)S(1)}, bf16[32,2,128,128]{3,2,1,0:T(8,128)(2,1)}, u32[]{:S(2)}) copy-start(bf16[32,2,128,128]{3,2,1,0:T(8,128)(2,1)} %get-tuple-element.47.refs_0_) | copy-start | bytes 6291460
  50.8 23.0 %collective-permute-start.4 = (bf16[11,2,128,128]{3,2,1,0:T(8,128)(2,1)S(1)}, bf16[11,2,128,128]{3,2,1,0:T(8,128)(2,1)S(1)}, u32[]{:S(2)}, u32[]{:S(2)}) collective-permute-start(bf16[11,2,128,128]{3,2,1,0:T(8,128)(2,1)S(1)} %slice.24), channel_id=1, source_target_pairs={{0,4},{1,5},{4,8},{5,9},{6,2},{7,3},{8,12},{9,13},{10,6},{11,7},{1... | collective-permute-start | bytes 2162696 | tf_op jit(solution)/shard_map/ppermute | solution.py:287
  54.5 8.7 %collective-permute-start.10 = (bf16[16,2,128,128]{3,2,1,0:T(8,128)(2,1)S(1)}, bf16[16,2,128,128]{3,2,1,0:T(8,128)(2,1)S(1)}, u32[]{:S(2)}, u32[]{:S(2)}) collective-permute-start(bf16[16,2,128,128]{3,2,1,0:T(8,128)(2,1)S(1)} %slice.28), channel_id=1, source_target_pairs={{1,0},{2,3},{5,4},{6,7},{9,8},{10,11},{13,12},{14,15},{17,16},{18,... | collective-permute-start | bytes 3145736 | tf_op jit(solution)/shard_map/ppermute | solution.py:287
  58.8 4.2 %collective-permute-start.7 = (bf16[8,2,128,128]{3,2,1,0:T(8,128)(2,1)S(1)}, bf16[8,2,128,128]{3,2,1,0:T(8,128)(2,1)S(1)}, u32[]{:S(2)}, u32[]{:S(2)}) collective-permute-start(bf16[8,2,128,128]{3,2,1,0:T(8,128)(2,1)S(1)} %get-tuple-element.88), channel_id=1, source_target_pairs={{0,1},{1,0},{2,3},{3,2},{4,5},{5,4},{6,7},{7,6},{8,9},{9,8},{10,11... | collective-permute-start | bytes 1572872 | tf_op jit(solution)/shard_map/ppermute | solution.py:287
  60.9 2.3 %collective-permute-start.6 = (bf16[8,2,128,128]{3,2,1,0:T(8,128)(2,1)S(1)}, bf16[8,2,128,128]{3,2,1,0:T(8,128)(2,1)S(1)}, u32[]{:S(2)}, u32[]{:S(2)}) collective-permute-start(bf16[8,2,128,128]{3,2,1,0:T(8,128)(2,1)S(1)} %get-tuple-element.89), channel_id=1, source_target_pairs={{0,1},{1,0},{2,3},{3,2},{4,5},{5,4},{6,7},{7,6},{8,9},{9,8},{10,11... | collective-permute-start | bytes 1572872 | tf_op jit(solution)/shard_map/ppermute | solution.py:287
  61.0 12.2 %collective-permute-start.5 = (bf16[5,2,128,128]{3,2,1,0:T(8,128)(2,1)S(1)}, bf16[5,2,128,128]{3,2,1,0:T(8,128)(2,1)S(1)}, u32[]{:S(2)}, u32[]{:S(2)}) collective-permute-start(bf16[5,2,128,128]{3,2,1,0:T(8,128)(2,1)S(1)} %slice.25), channel_id=1, source_target_pairs={{2,5},{3,4},{4,3},{5,2},{6,9},{7,8},{8,7},{9,6},{10,13},{11,12},{1... | collective-permute-start | bytes 983048 | tf_op jit(solution)/shard_map/ppermute | solution.py:287
  76.4 2.6 %collective-permute-start.11 = (bf16[14,128,128]{2,1,0:T(8,128)(2,1)S(1)}, bf16[14,128,128]{2,1,0:T(8,128)(2,1)S(1)}, u32[]{:S(2)}, u32[]{:S(2)}) collective-permute-start(bf16[14,128,128]{2,1,0:T(8,128)(2,1)S(1)} %slice.29), channel_id=1, source_target_pairs={{0,1},{1,0},{2,3},{3,2},{4,5},{5,4},{6,7},{7,6},{8,9},{9,8},{10,11... | collective-permute-start | bytes 1376264 | tf_op jit(solution)/shard_map/ppermute | solution.py:287
  77.3 9.5 %collective-permute-start.17 = (bf16[7,128,128]{2,1,0:T(8,128)(2,1)S(1)}, bf16[7,128,128]{2,1,0:T(8,128)(2,1)S(1)}, u32[]{:S(2)}, u32[]{:S(2)}) collective-permute-start(bf16[7,128,128]{2,1,0:T(8,128)(2,1)S(1)} %slice.31), channel_id=1, source_target_pairs={{0,1},{1,0},{2,3},{3,2},{4,5},{5,4},{6,7},{7,6},{8,9},{9,8},{10,11... | collective-permute-start | bytes 688136 | tf_op jit(solution)/shard_map/ppermute | solution.py:287
  77.4 11.1 %collective-permute-start.16 = (bf16[6,128,128]{2,1,0:T(8,128)(2,1)S(1)}, bf16[6,128,128]{2,1,0:T(8,128)(2,1)S(1)}, u32[]{:S(2)}, u32[]{:S(2)}) collective-permute-start(bf16[6,128,128]{2,1,0:T(8,128)(2,1)S(1)} %get-tuple-element.80), channel_id=1, source_target_pairs={{0,2},{1,3},{2,0},{3,1},{4,6},{5,7},{6,4},{7,5},{8,10},{9,11},{10,... | collective-permute-start | bytes 589832 | tf_op jit(solution)/shard_map/ppermute | solution.py:287
  79.4 11.6 %collective-permute-start.14 = (bf16[8,128,128]{2,1,0:T(8,128)(2,1)S(1)}, bf16[8,128,128]{2,1,0:T(8,128)(2,1)S(1)}, u32[]{:S(2)}, u32[]{:S(2)}) collective-permute-start(bf16[8,128,128]{2,1,0:T(8,128)(2,1)S(1)} %get-tuple-element.78), channel_id=1, source_target_pairs={{2,4},{3,5},{4,2},{5,3},{6,8},{7,9},{8,6},{9,7},{10,12},{11,13},{1... | collective-permute-start | bytes 786440 | tf_op jit(solution)/shard_map/ppermute | solution.py:287
  82.4 8.6 %collective-permute-start.13 = (bf16[6,128,128]{2,1,0:T(8,128)(2,1)S(1)}, bf16[6,128,128]{2,1,0:T(8,128)(2,1)S(1)}, u32[]{:S(2)}, u32[]{:S(2)}) collective-permute-start(bf16[6,128,128]{2,1,0:T(8,128)(2,1)S(1)} %get-tuple-element.77), channel_id=1, source_target_pairs={{0,4},{1,5},{4,8},{5,9},{6,2},{7,3},{8,12},{9,13},{10,6},{11,7},{1... | collective-permute-start | bytes 589832 | tf_op jit(solution)/shard_map/ppermute | solution.py:287
  86.0 8.7 %collective-permute-start.12 = (bf16[6,128,128]{2,1,0:T(8,128)(2,1)S(1)}, bf16[6,128,128]{2,1,0:T(8,128)(2,1)S(1)}, u32[]{:S(2)}, u32[]{:S(2)}) collective-permute-start(bf16[6,128,128]{2,1,0:T(8,128)(2,1)S(1)} %slice.32), channel_id=1, source_target_pairs={{0,2},{1,3},{2,0},{3,1},{4,6},{5,7},{6,4},{7,5},{8,10},{9,11},{10,... | collective-permute-start | bytes 589832 | tf_op jit(solution)/shard_map/ppermute | solution.py:287
  87.9 1.5 %collective-permute-start.15 = (bf16[2,128,128]{2,1,0:T(8,128)(2,1)S(1)}, bf16[2,128,128]{2,1,0:T(8,128)(2,1)S(1)}, u32[]{:S(2)}, u32[]{:S(2)}) collective-permute-start(bf16[2,128,128]{2,1,0:T(8,128)(2,1)S(1)} %get-tuple-element.79), channel_id=1, source_target_pairs={{2,6},{5,1},{6,10},{9,5},{10,14},{13,9},{18,22},{21,17},{22,26},{2... | collective-permute-start | bytes 196616 | tf_op jit(solution)/shard_map/ppermute | solution.py:287
